TPU v7x, 32 devices: a whole 2x2x4 slice. The times are simulated.
32 devices in a mesh: comm: 16 (over z, x, core), blk: 2 (over y).
Axes of the slice: x: 2, y: 2, z: 4, core: 2. Of those that a mesh axis runs over, the one named last changes fastest.
Arguments:
- features: float32 [4096, 256], P(('comm', 'blk')), may hold values from -6 to 6
- tiles: float32 [4096, 256], P(('comm', 'blk')), may hold values from -0.375 to 0.375
- weight: float32 [256, 256], replicated, may hold values from -0.375 to 0.375
- cotangent: float32 [4096, 256], P(('comm', 'blk')), may hold values from -6 to 6
- send_count: int32 [32, 16], P(('comm', 'blk')), may hold values from 0 to 16, as said below
- send_index: int32 [32, 256], P(('comm', 'blk')), may hold values from 0 to 127
- cross_dst: int32 [32, 256], P(('comm', 'blk')), may hold values from 0 to 127
- cross_weight: float32 [32, 256], P(('comm', 'blk')), may hold values from -2.4 to 2.4
Outputs:
- output: float32 [4096, 256], P(('comm', 'blk'))
- grad_features: float32 [4096, 256], P(('comm', 'blk'))
- grad_weight: float32 [256, 256], replicated
Inputs may be any that keep to these rules, and one draw needn't show every extreme that they name: send_count[d, p] is 0 where p is d's own community and at least 1 elsewhere; every device sends exactly 16 rows to some other community.
All inputs are finite; a program needn't handle non-finite values.
Results may differ from a plain program's by a relative error of at most 0.0003.
Values sent between devices are 32-bit elements; how exact they have to be, the bound alone decides.
No kernel may reach another device: no remote copies, remote signals or barrier semaphores. Data moves between devices by JAX's collectives and lax.ppermute only.
A program may use at most 64 MiB of HBM per device.

v0:
```python
import jax
import jax.numpy as jnp
from jax import lax
from jax.sharding import PartitionSpec as P


def body(features, tiles, weight, cotangent, send_count, send_index, cross_dst, cross_weight):
    rows, width = features.shape
    groups = lax.axis_size("comm")
    blocks = lax.axis_size("blk")
    slot_total = send_index.shape[1]
    per_peer = slot_total // groups
    counts = send_count[0]
    index = send_index[0].reshape(groups, per_peer)
    valid = (jnp.arange(per_peer, dtype=jnp.int32)[None, :] < counts[:, None]).astype(jnp.float32)
    targets = cross_dst[0]
    edge_weight = cross_weight[0]
    highest = lax.Precision.HIGHEST
    outgoing = features[index] * valid[:, :, None]
    incoming = lax.all_to_all(outgoing, "comm", split_axis=0, concat_axis=0, tiled=True).reshape(
        slot_total, width
    )
    columns = tiles
    local = jnp.dot(columns, lax.all_gather(features, "blk", axis=0, tiled=True), precision=highest)
    cross = jax.ops.segment_sum(edge_weight[:, None] * incoming, targets, num_segments=rows)
    aggregated = local + cross
    pre = jnp.dot(aggregated, weight, precision=highest)
    output, pull = jax.vjp(lambda value: jax.nn.gelu(value, approximate=False), pre)
    grad_pre = pull(cotangent)[0]
    partial_weight = lax.dot_general(
        aggregated, grad_pre, (((0,), (0,)), ((), ())), precision=highest
    )
    nodes = rows * groups * blocks
    grad_weight = lax.psum(partial_weight, ("comm", "blk")) * nodes ** (-0.5)
    spread = jnp.dot(grad_pre, weight.T, precision=highest)
    columns = tiles
    inner_grad = lax.psum_scatter(
        lax.dot_general(columns, spread, (((0,), (0,)), ((), ())), precision=highest),
        "blk",
        scatter_dimension=0,
        tiled=True,
    )
    slot_grads = (edge_weight[:, None] * spread[targets]).reshape(groups, per_peer, width)
    returned = lax.all_to_all(slot_grads, "comm", split_axis=0, concat_axis=0, tiled=True)
    returned = (returned * valid[:, :, None]).reshape(slot_total, width)
    boundary_grad = jax.ops.segment_sum(returned, index.reshape(slot_total), num_segments=rows)
    return (output, inner_grad + boundary_grad, grad_weight)


def solution(mesh):
    return jax.shard_map(
        body,
        mesh=mesh,
        in_specs=(
            P(("comm", "blk"), None),
            P(("comm", "blk"), None),
            P(),
            P(("comm", "blk"), None),
            P(("comm", "blk"), None),
            P(("comm", "blk"), None),
            P(("comm", "blk"), None),
            P(("comm", "blk"), None),
        ),
        out_specs=(P(("comm", "blk"), None), P(("comm", "blk"), None), P()),
        check_vma=False,
    )
```

profile of v0, /device:TPU:0, one launch (start us, length us, event | category | flops | bytes accessed | tf_op | source)
XLA Modules:
  0.0 173.8 jit_solution(11490458766039831719)
XLA Ops:
  8.0 0.5 broadcast.83
  8.7 0.7 reduce.6
  9.6 0.6 copy-done.8
  10.3 1.9 %gather_fusion = f32[256,256]{1,0:T(8,128)S(1)} fusion(f32[128,256]{1,0:T(8,128)} %param.8, s32[1024]{0:T(1024)S(1)} %pad_clamp_fusion.1), kind=kCustom, calls=%fused_computation | custom fusion | bytes 525312 | tf_op jit(solution)/shard_map/gather | solution.py:19
  12.2 0.8 broadcast_multiply_fusion.3
  13.0 7.5 %all-to-all-start = ((f32[16,16,256]{2,1,0:T(8,128)}), f32[16,16,256]{2,1,0:T(8,128)S(1)}, u32[]{:S(2)}, u32[]{:S(2)}) async-start(f32[16,16,256]{2,1,0:T(8,128)} %broadcast_multiply_fusion.3), calls=%async_computation | async-start | bytes 524288 | tf_op jit(solution)/shard_map/all_to_all | solution.py:20
  20.6 0.5 broadcast.84
  21.2 0.7 reduce.7
  22.0 6.6 %all_gather.3 = f32[256,256]{1,0:T(8,128)S(1)} all-gather(f32[128,256]{1,0:T(8,128)S(1)} %copy-done.2), channel_id=1, replica_groups=mesh['comm'=16,'blk'=2] {'blk'}, dimensions={0}, use_global_device_ids=true | all-gather | bytes 393216 | tf_op jit(solution)/shard_map/all_gather | solution.py:24
  28.6 0.3 fusion.10
  28.9 1.6 all-to-all-done
  30.6 2.0 %scatter_fusion = f32[128,256]{1,0:T(8,128)S(1)} fusion(f32[128,256]{1,0:T(8,128)S(1)} %fusion.10, s32[256]{0:T(256)S(1)} %bitcast.28, f32[256,256]{1,0:T(8,128)S(1)} %bitcast_multiply_fusion), kind=kCustom, calls=%fused_computation.2 | custom fusion | flops 65536 | bytes 787456 | tf_op jit(solution)/shard_map/scatter-add | solution.py:25
  32.7 1.2 multiply_multiply_fusion.5
  33.9 0.4 fusion.8
  34.3 1.1 fusion.7
  35.5 1.0 gather_fusion.1
  36.4 0.8 broadcast_multiply_fusion.1
  37.2 4.1 %all-to-all-start.1 = ((f32[16,16,256]{2,1,0:T(8,128)}), f32[16,16,256]{2,1,0:T(8,128)S(1)}, u32[]{:S(2)}, u32[]{:S(2)}) async-start(f32[16,16,256]{2,1,0:T(8,128)} %broadcast_multiply_fusion.1), calls=%async_computation.2 | async-start | bytes 524288 | tf_op jit(solution)/shard_map/all_to_all | solution.py:44
  41.4 1.1 convolution_bitcast_fusion
  42.6 118.2 %all-reduce.2.cloned.1.call-done = f32[256,256]{1,0:T(8,128)} async-done(((f32[256,256]{1,0:T(8,128)}), f32[256,256]{1,0:T(8,128)}) %all-reduce.2.cloned.1.call-update) | async-done | bytes 262160 | tf_op jit(solution)/shard_map/psum | solution.py:34
  160.8 1.7 broadcast_multiply_fusion
  162.6 1.0 copy.12
  163.6 2.0 %scatter_fusion.1 = f32[128,256]{1,0:T(8,128)S(1)} fusion(f32[128,256]{1,0:T(8,128)S(1)} %copy.12, s32[256]{0:T(256)S(1)} %bitcast.29, f32[256,256]{1,0:T(8,128)S(1)} %bitcast.24), kind=kCustom, calls=%fused_computation.3 | custom fusion | flops 65536 | bytes 787456 | tf_op jit(solution)/shard_map/scatter-add | solution.py:46
  165.7 0.6 copy-done.1
  (32 shorter events, 1.1 us)
Async XLA Ops:
  8.0 24.7 %copy-start = (f32[256,256]{1,0:T(8,128)S(1)}, f32[256,256]{1,0:T(8,128)}, u32[]{:S(2)}) copy-start(f32[256,256]{1,0:T(8,128)} %param.10) | copy-start | bytes 786436
  8.0 0.7 copy-start.7
  9.6 0.7 copy-start.8
  13.0 7.6 %copy-start.6 = (s32[1,256]{1,0:T(1,128)S(1)}, s32[1,256]{1,0:T(1,128)}, u32[]{:S(2)}) copy-start(s32[1,256]{1,0:T(1,128)} %param.14) | copy-start | bytes 3076
  13.0 9.0 %copy-start.2 = (f32[128,256]{1,0:T(8,128)S(1)}, f32[128,256]{1,0:T(8,128)}, u32[]{:S(2)}) copy-start(f32[128,256]{1,0:T(8,128)} %param.8) | copy-start | bytes 393220
  13.0 17.5 %all-to-all-start = ((f32[16,16,256]{2,1,0:T(8,128)}), f32[16,16,256]{2,1,0:T(8,128)S(1)}, u32[]{:S(2)}, u32[]{:S(2)}) async-start(f32[16,16,256]{2,1,0:T(8,128)} %broadcast_multiply_fusion.3), calls=%async_computation | async-start | bytes 524288 | tf_op jit(solution)/shard_map/all_to_all | solution.py:20
  20.5 140.3 %all-reduce.2.cloned.1.call-start = ((), (), s32[]{:S(2)}) async-start(), calls=%async_computation.4 | async-start | bytes 524288 | tf_op jit(solution)/shard_map/psum | solution.py:34
  20.6 0.7 copy-start.5
  22.0 6.6 %copy-start.4 = (f32[128,256]{1,0:T(8,128)S(1)}, f32[128,256]{1,0:T(8,128)}, u32[]{:S(2)}) copy-start(f32[128,256]{1,0:T(8,128)} %param.9) | copy-start | bytes 393220
  32.7 1.2 copy-start.3
  37.2 125.2 %all-to-all-start.1 = ((f32[16,16,256]{2,1,0:T(8,128)}), f32[16,16,256]{2,1,0:T(8,128)S(1)}, u32[]{:S(2)}, u32[]{:S(2)}) async-start(f32[16,16,256]{2,1,0:T(8,128)} %broadcast_multiply_fusion.1), calls=%async_computation.2 | async-start | bytes 524288 | tf_op jit(solution)/shard_map/all_to_all | solution.py:44
  41.4 121.2 %reduce-scatter.2.cloned.1.call-start = ((), (), s32[]{:S(2)}) async-start(), calls=%async_computation.3 | async-start | bytes 393216 | tf_op jit(solution)/shard_map/reduce_scatter | solution.py:37
  165.7 0.7 copy-start.1
Sparse Core Ops, SparseCore 0:
  35.6 125.1 all-reduce.1
Sparse Core Ops, SparseCore 1:
  44.1 12.9 reduce-scatter.1
where the time goes:
time: 174 us
  waiting for transfers between devices  120 us (69%)
  between operations  15.6 us (9%)
  starting transfers between devices  11.7 us (7%)
  other arithmetic  8.95 us (5%)
  local copies, waits for them, and re-layouts  6.79 us (4%)
  blocking collectives  6.64 us (4%)
  matrix products  4.13 us (2%)
    psum x1, waiting for transfers between devices, body(): grad_weight = lax.psum(partial_weight, ('comm', 'blk')) * nodes ** (-0.5)  118 us
    all_to_all x1, starting transfers between devices, body(): lax.all_to_all(outgoing, 'comm', split_axis=0, concat_axis=0, tiled=True)  7.49 us
    all_gather x1, blocking collectives, body(): lax.all_gather(features, 'blk', axis=0, tiled=True)  6.64 us
    all_to_all x1, starting transfers between devices, body(): lax.all_to_all(slot_grads, 'comm', split_axis=0, concat_axis=0, tiled=True)  4.12 us
  transfers between devices with their start and end apart: 4, of which 2 were waited for; matrix products, arithmetic and copies ran while one was open for 4% of the time, Pallas kernels for 0%

commit v1 on v0

v1 whole, which is shorter than its diff:
```python
import functools
import math

import jax
import jax.numpy as jnp
from jax import lax
from jax.experimental import pallas as pl
from jax.experimental.pallas import tpu as pltpu
from jax.sharding import PartitionSpec as P

F32 = jnp.float32
BF16 = jnp.bfloat16
VMEM = pl.BlockSpec(memory_space=pltpu.VMEM)
HBM = pl.BlockSpec(memory_space=pltpu.HBM)


def split(value):
    high = value.astype(BF16)
    return high, (value - high.astype(F32)).astype(BF16)


def product(a, b, dims):
    return lax.dot_general(a, b, (dims, ((), ())), preferred_element_type=F32)


def dot3(a, b, dims=((1,), (0,))):
    (a_high, a_low), (b_high, b_low) = a, b
    return (product(a_low, b_high, dims) + product(a_high, b_low, dims)) + product(a_high, b_high, dims)


def dot_onehot(a, b, dims):
    return product(a, b[1], dims) + product(a, b[0], dims)


def tree(terms):
    while len(terms) > 1:
        terms = [terms[i] + terms[i + 1] for i in range(0, len(terms), 2)]
    return terms[0]


def send_matrix(counts, index, rows):
    groups, slots = counts.shape[1], index.shape[1]
    per_peer = slots // groups
    lane = lax.broadcasted_iota(jnp.int32, (groups, slots), 1)
    first = lax.broadcasted_iota(jnp.int32, (groups, slots), 0) * per_peer
    of_peer = ((lane >= first) & (lane < first + per_peer)).astype(F32)
    limit = jnp.dot(counts.astype(F32), of_peer, preferred_element_type=F32)
    place = lax.broadcasted_iota(jnp.int32, (1, slots), 1) % per_peer
    chosen = jnp.where(place.astype(F32) < limit, index, -1)
    return (lax.broadcasted_iota(jnp.int32, (rows, slots), 0) == chosen).astype(F32).astype(BF16)


def gather_kernel(
    count_hbm, index_hbm, features_hbm, own_ref, give_ref, chosen_ref, count_ref, index_ref, features_ref, rows_ref, sems
):
    pairs = ((count_hbm, count_ref), (index_hbm, index_ref), (features_hbm, features_ref))
    copies = [pltpu.make_async_copy(source, target, sems.at[i]) for i, (source, target) in enumerate(pairs)]
    for copy in copies:
        copy.start()
    copies[0].wait()
    copies[1].wait()
    chosen = send_matrix(count_ref[...], index_ref[...], features_ref.shape[0])
    chosen_ref[...] = chosen
    copies[2].wait()
    rows_ref[...] = dot_onehot(chosen, split(features_ref[...]), ((0,), (0,)))
    me = lax.axis_index("comm")
    chips, per_peer = own_ref.shape[:2]
    for mask in range(chips):
        for k, out_ref in enumerate((own_ref, give_ref)):
            start = lax.bitwise_xor(me, 2 * mask + (k ^ (mask > 0))) * per_peer
            out_ref[mask] = rows_ref[pl.ds(pl.multiple_of(start, per_peer), per_peer), :]


def prepare_kernel(
    near_ref, far_ref, tiles_ref, weight_ref, target_ref, edge_ref,
    local_ref, cross_ref, tiles_out, weight_out,
):
    rows = near_ref.shape[0]
    blocks = far_ref.shape[0] + 1
    slots = target_ref.shape[1]
    me = lax.axis_index("blk")

    total = None
    for step in range(blocks):
        start = lax.rem(me + step, blocks) * rows
        tile = split(tiles_ref[:, pl.ds(pl.multiple_of(start, rows), rows)])
        tiles_out[step, 0], tiles_out[step, 1] = tile
        term = dot3(tile, split(near_ref[...] if step == 0 else far_ref[step - 1]))
        total = term if total is None else total + term
    local_ref[...] = total
    hit = lax.broadcasted_iota(jnp.int32, (rows, slots), 0) == target_ref[...]
    cross_ref[0], cross_ref[1] = split(jnp.where(hit, edge_ref[...], 0.0))
    weight_out[0], weight_out[1] = split(weight_ref[...])


def chunk_number(chunks):
    blocks = lax.axis_size("blk")
    number = lax.axis_index("comm") * blocks + lax.axis_index("blk")
    outer = lax.div(number, chunks)
    crossed = lax.rem(outer + lax.div(outer, 2), 2) * blocks
    return lax.bitwise_xor(lax.rem(number, chunks), crossed)


def layer_kernel(
    order, parities, local_ref, cross_ref, weight_ref, cotangent_ref, own_ref, got_ref, *refs
):
    chips, per_peer = own_ref.shape[:2]
    arrived_refs, refs = refs[: chips - 1], refs[chips - 1 :]
    out_ref, spread_ref, keep_ref, give_ref, *partial_refs, slots_ref, terms_ref = refs
    peer = lax.axis_index("comm")
    for mask in range(chips):
        for k in range(2):
            start = lax.bitwise_xor(peer, 2 * mask + (k ^ (mask > 0))) * per_peer
            block = arrived_refs[mask - 1][k] if mask else (got_ref if k else own_ref)[0]
            slots_ref[pl.ds(pl.multiple_of(start, per_peer), per_peer), :] = block
    cross = cross_ref[0], cross_ref[1]
    weight = weight_ref[0], weight_ref[1]

    aggregated = split(local_ref[...] + dot3(cross, split(slots_ref[...])))
    pre = dot3(aggregated, weight)
    cdf = 0.5 * (1.0 + lax.erf(pre * math.sqrt(0.5)))
    density = jnp.exp(-0.5 * pre * pre) * (1.0 / math.sqrt(2.0 * math.pi))
    grad_pre = split(cotangent_ref[...] * (cdf + pre * density))
    out_ref[...] = pre * cdf
    terms_ref[...] = dot3(aggregated, grad_pre, ((0,), (0,)))
    spread = split(dot3(grad_pre, weight, ((1,), (1,))))
    spread_ref[0], spread_ref[1] = spread
    slots_ref[...] = dot3(cross, spread, ((0,), (0,)))

    half = 0
    if partial_refs:
        partial_refs[0][...] = terms_ref[...]
    else:
        half = terms_ref.shape[0] // 2
        share = terms_ref.shape[0] // len(order)
        me = chunk_number(len(order))
        for place, relative in enumerate(order):
            start = lax.bitwise_xor(me, relative) * share
            chunk = terms_ref[pl.ds(pl.multiple_of(start, share), share), :]
            target_ref = keep_ref if place < len(order) // 2 else give_ref
            target_ref[pl.ds(place * share % half, share), :] = chunk
    for mask in range(chips):
        for k, target_ref in enumerate((keep_ref, give_ref)):
            start = lax.bitwise_xor(peer, 2 * mask + (k ^ parities[mask])) * per_peer
            block = slots_ref[pl.ds(pl.multiple_of(start, per_peer), per_peer), :]
            target_ref[pl.ds(half + mask * per_peer, per_peer), :] = block


def place_kernel(order, mine_ref, other_ref, out_ref):
    half, share = mine_ref.shape[:2]
    me = chunk_number(len(order))
    for i, relative in enumerate(order):
        start = lax.bitwise_xor(me, relative) * share
        out_ref[pl.ds(pl.multiple_of(start, share), share), :] = mine_ref[i] if i < half else other_ref[i - half]


def inner_kernel(tiles_ref, spread_ref, value_ref, near_ref, far_ref, out_ref):
    spread = spread_ref[0], spread_ref[1]
    for step in range(far_ref.shape[0]):
        far_ref[step] = dot3((tiles_ref[step + 1, 0], tiles_ref[step + 1, 1]), spread, ((0,), (0,)))
    near_ref[...] = dot3((tiles_ref[0, 0], tiles_ref[0, 1]), spread, ((0,), (0,)))
    out_ref[...] = value_ref[...]


def value_of(piece, refs):
    if isinstance(piece, list):
        return tree([value_of(term, refs) for term in piece])
    source, first, rows = piece
    return refs[source][first : first + rows, :]


def rows_of(piece):
    return rows_of(piece[0]) if isinstance(piece, list) else piece[2]


def leaves(piece):
    return [leaf for term in piece for leaf in leaves(term)] if isinstance(piece, list) else [piece]


def renumber(piece, used):
    if isinstance(piece, list):
        return [renumber(term, used) for term in piece]
    return (used.index(piece[0]), *piece[1:])


def pack_kernel(layout, scale, count, *refs):
    for pieces, out_ref in zip(layout, refs[count:]):
        first = 0
        for piece in pieces:
            rows = rows_of(piece)
            value = value_of(piece, refs)
            out_ref[first : first + rows, :] = value if scale is None else value * scale
            first += rows


def finish_kernel(blocks, far, chosen_ref, near_ref, *refs):
    *refs, grad_ref, slots_ref = refs
    peer = lax.axis_index("comm")
    for distance, piece in blocks:
        rows = piece[2]
        start = lax.bitwise_xor(peer, distance) * rows
        slots_ref[pl.ds(pl.multiple_of(start, rows), rows), :] = value_of(piece, refs)
    total = near_ref[...]
    for piece in far:
        total += value_of(piece, refs)
    grad_ref[...] = total + dot_onehot(chosen_ref[...], split(slots_ref[...]), ((1,), (0,)))


def kernel(body, name, out, operands, spec=VMEM, scratch=(), flops=0, traffic=0, after=()):
    count = len(operands)
    if spec is HBM:
        operands = [pltpu.with_memory_space_constraint(x, pltpu.HBM) for x in operands]
    return pl.pallas_call(
        lambda *refs: body(*refs[:count], *refs[count + len(after) :]),
        out_shape=out,
        in_specs=[spec] * count + [pl.BlockSpec(memory_space=pl.ANY)] * len(after),
        out_specs=jax.tree.map(lambda _: VMEM, out),
        scratch_shapes=list(scratch),
        compiler_params=pltpu.CompilerParams(vmem_limit_bytes=16 * 1024 * 1024),
        cost_estimate=pl.CostEstimate(flops=flops, bytes_accessed=traffic, transcendentals=0),
        name=name,
    )(*operands, *after)


def body(features, tiles, weight, cotangent, send_count, send_index, cross_dst, cross_weight):
    rows, width = features.shape
    groups = lax.axis_size("comm")
    blocks = lax.axis_size("blk")
    slots = send_index.shape[1]
    per_peer = slots // groups
    nodes = rows * groups * blocks
    array = jax.ShapeDtypeStruct
    work = 2 * rows * slots * width

    def shift(value, step):
        pairs = [(i, (i + step) % blocks) for i in range(blocks)]
        return lax.ppermute(value, "blk", pairs)

    def exchange(value):
        return lax.all_to_all(value, "comm", split_axis=0, concat_axis=0, tiled=True)

    both = ("comm", "blk")
    devices = groups * blocks
    outer = min(4, groups // 2)
    chunks = devices // outer
    share = width // chunks
    low, high = blocks.bit_length() - 1, chunks.bit_length() - 1
    others = list(range(low)) + list(range(low + 1, high))
    pairs = [others[i : i + 2] for i in range(0, len(others), 2)]

    core = 1 << low
    outer_bits = list(range(high, devices.bit_length() - 1))

    def masks(bits, straight=()):
        plain = [sum((i >> j & 1) << bit for j, bit in enumerate(bits)) for i in range(1 << len(bits))]
        if bits is outer_bits:
            return [mask ^ core * (i.bit_count() % 2) for i, mask in enumerate(plain)]
        return [mask if mask in (0, core) or mask in straight else mask ^ core for mask in plain]

    def order_of(straight=()):
        order = [0]
        for bits in reversed([[low]] + pairs):
            order = [mask ^ place for mask in masks(bits, straight) for place in order]
        return order

    straight = (1,) if blocks == 2 else ()
    order, gather_order = order_of(straight), order_of()
    way_bits = [sum(1 << bit - low - 1 for bit in bits if bit > low) for bits in pairs]
    parities = [
        (sum(bool(chip & bits) for bits in way_bits) + (chip >> high - low - 1).bit_count()) % 2
        for chip in range(groups // 2)
    ]

    def swap(value, mask):
        return lax.ppermute(value, both, [(i, i ^ mask) for i in range(devices)]) if mask else value

    far = jnp.stack([shift(features, -step) for step in range(1, blocks)])
    own, give, chosen = kernel(
        gather_kernel,
        "gather",
        (
            array((groups // 2, per_peer, width), F32),
            array((groups // 2, per_peer, width), F32),
            array((rows, slots), BF16),
        ),
        (send_count, send_index, features),
        spec=HBM,
        scratch=(
            pltpu.VMEM(send_count.shape, jnp.int32),
            pltpu.VMEM(send_index.shape, jnp.int32),
            pltpu.VMEM(features.shape, F32),
            pltpu.VMEM((slots, width), F32),
            pltpu.SemaphoreType.DMA((3,)),
        ),
        flops=work,
        traffic=4 * (rows + slots) * width,
    )
    got = swap(give, 1 << low)
    packed = jnp.stack([own, got], axis=1)
    arrived = [swap(packed[mask], 2 * mask + 1 << low) for mask in range(1, groups // 2)]
    local, cross, tile_parts, weight_parts = kernel(
        prepare_kernel,
        "prepare",
        (
            array((rows, width), F32),
            array((2, rows, slots), BF16),
            array((blocks, 2, rows, rows), BF16),
            array((2, width, width), BF16),
        ),
        (features, far, tiles, weight, cross_dst, cross_weight),
        flops=3 * work,
        traffic=4 * (4 * rows + width) * width,
    )
    aligned = share % 8 == 0
    half = width // 2
    held = array((slots // 2 + (half if aligned else 0), width), F32)
    value, spread, keep, give, *partial = kernel(
        functools.partial(layer_kernel, order, parities),
        "layer",
        (array((rows, width), F32), array((2, rows, width), BF16), held, held)
        + (() if aligned else (array((width, width), F32),)),
        (local, cross, weight_parts, cotangent, own, got, *arrived),
        scratch=(pltpu.VMEM((slots, width), F32), pltpu.VMEM((width, width), F32)),
        flops=15 * work,
        traffic=4 * (4 * rows + 2 * slots) * width,
    )
    if not aligned:
        ordered = partial[0].reshape(chunks, share, width)[chunk_number(chunks) ^ jnp.array(order)]
        keep = jnp.concatenate([ordered[: chunks // 2].reshape(half, width), keep])
        give = jnp.concatenate([ordered[chunks // 2 :].reshape(half, width), give])
    inner, leaving, output = kernel(
        inner_kernel,
        "inner",
        (array((rows, width), F32), array((blocks - 1, rows, width), F32), array((rows, width), F32)),
        (tile_parts, spread, value),
        flops=3 * work,
        traffic=4 * 6 * rows * width,
    )

    arrays = [keep, give, swap(give, 1 << low)]
    terms = [[(0, i * share, share), (2, i * share, share)] for i in range(chunks // 2)]
    moving = {
        2 * m + parities[m]: [(k, (2 * k, half + m * per_peer, per_peer)) for k in range(2)]
        for m in range(groups // 2)
    }
    far_pieces = []

    def pack(name, layout, scale=None):
        used = sorted({leaf[0] for pieces in layout for leaf in leaves(pieces)})
        layout = [[renumber(piece, used) for piece in pieces] for pieces in layout]
        out = tuple(array((sum(map(rows_of, pieces)), width), F32) for pieces in layout)
        operands = [arrays[i] for i in used]
        traffic = 8 * width * sum(o.shape[0] for o in out)
        return kernel(functools.partial(pack_kernel, layout, scale, len(used)), name, out, operands, traffic=traffic)

    for bits in pairs + [outer_bits]:
        last = bits is outer_bits
        keeps = len(terms) if last else len(terms) >> len(bits)
        layout, riders = [], []
        partners = list(enumerate(masks(bits, straight)))[:0:-1]
        for i, mask in partners:
            pieces = list(terms) if last else terms[i * keeps : (i + 1) * keeps]
            way, across = mask >> low, mask & (core - 1)
            all_ways = sum(1 << bit for bit in bits) >> low
            going = [q for q in sorted(moving) if not across and q & all_ways == way & all_ways]
            riders.append([(q, come) for q in going for come, _ in moving[q]])
            pieces += [piece for q in going for _, piece in moving[q]]
            if blocks == 2 and mask == 1:
                arrays.append(leaving[0])
                pieces.append((len(arrays) - 1, 0, rows))
            layout.append(pieces)
        sent = pack("pack", layout)
        came = []
        for (_, mask), value, rides in zip(partners, sent, riders):
            arrays.append(swap(value, mask))
            number, first = len(arrays) - 1, 0
            came.append([(number, j * share, share) for j in range(keeps)])
            first = keeps * share
            for q, come in rides:
                way = mask >> low
                moving.setdefault(q ^ way, []).append((come ^ way, (number, first, per_peer)))
                first += per_peer
            if blocks == 2 and mask == 1:
                far_pieces.append((number, first, rows))
            for q in {q for q, _ in rides}:
                del moving[q]
        terms = [[terms[j]] + [pieces[j] for pieces in reversed(came)] for j in range(keeps)]
    if blocks > 2:
        for step in range(1, blocks):
            arrays.append(shift(leaving[step - 1], step))
            far_pieces.append((len(arrays) - 1, 0, rows))

    sums = pack("sum", [terms], nodes ** (-0.5))[0].reshape(1, share, width)
    for bits in reversed(pairs):
        sums = jnp.concatenate([swap(sums, mask) for mask in masks(bits)])
    other = swap(sums, 1 << low)
    if aligned:
        grad_weight = kernel(
            functools.partial(place_kernel, gather_order),
            "place",
            array((width, width), F32),
            (sums, other),
            traffic=8 * width * width,
        )
    else:
        places = jnp.array([gather_order.index(i) for i in range(chunks)])[chunk_number(chunks) ^ jnp.arange(chunks)]
        grad_weight = jnp.concatenate([sums, other])[places].reshape(width, width)

    came = moving[0]
    used = sorted({piece[0] for _, piece in came} | {piece[0] for piece in far_pieces})
    grad_features = kernel(
        functools.partial(
            finish_kernel,
            [(distance, renumber(piece, used)) for distance, piece in came],
            [renumber(piece, used) for piece in far_pieces],
        ),
        "finish",
        array((rows, width), F32),
        (chosen, inner, *(arrays[i] for i in used)),
        scratch=(pltpu.VMEM((slots, width), F32),),
        flops=2 * work,
        traffic=4 * (3 * rows + slots) * width,
    )
    return (output, grad_features, grad_weight)


def solution(mesh):
    return jax.shard_map(
        body,
        mesh=mesh,
        in_specs=(
            P(("comm", "blk"), None),
            P(("comm", "blk"), None),
            P(),
            P(("comm", "blk"), None),
            P(("comm", "blk"), None),
            P(("comm", "blk"), None),
            P(("comm", "blk"), None),
            P(("comm", "blk"), None),
        ),
        out_specs=(P(("comm", "blk"), None), P(("comm", "blk"), None), P()),
        check_vma=False,
    )
```

time: 174 us -> 48.1 us (0.28)
  waiting for transfers between devices: 120 us -> 16.4 us
  between operations: 15.6 us -> 0.72 us
  starting transfers between devices: 11.7 us -> 25.3 us
  other arithmetic: 8.95 us -> 0.03 us
  blocking collectives: 6.64 us -> 0 us
  local copies, waits for them, and re-layouts: 6.79 us -> 0.28 us
  Pallas kernels: 0 us -> 5.22 us
  matrix products: 4.13 us -> 0 us
    psum x1 -> x0, waiting for transfers between devices: 118 us -> none  [body(): grad_weight = lax.psum(partial_weight, ('comm', 'blk')) * nodes ** (-0.5)]
    ppermute x0 -> x20, starting transfers between devices: none -> 25.3 us  [the longest x19 22.7 us: swap(): lax.ppermute(value, both, [(i, i ^ mask) for i in range(devices)])]
    ppermute x0 -> x20, waiting for transfers between devices: none -> 16.4 us  [the longest x19 16.4 us: swap(): lax.ppermute(value, both, [(i, i ^ mask) for i in range(devices)])]
    all_to_all x2 -> x0, starting transfers between devices: 11.6 us -> none  [the longest x1 7.49 us: body(): lax.all_to_all(outgoing, 'comm', split_axis=0, concat_axis=0, tiled=True)]
    all_gather x1 -> x0, blocking collectives: 6.64 us -> none  [body(): lax.all_gather(features, 'blk', axis=0, tiled=True)]
    pallas_call x0 -> x9, Pallas kernels: none -> 5.22 us  [kernel(): pl.pallas_call(lambda *refs: body(*refs[:count], *refs[count + len(after)...]
    dot_general x5 -> x0, matrix products: 4.13 us -> none  [the longest x1 1.21 us: body(): pre = jnp.dot(aggregated, weight, precision=highest)]
    scatter-add x2 -> x0, other arithmetic: 4.07 us -> none  [the longest x1 2.04 us: body(): jax.ops.segment_sum(edge_weight[:, None] * incoming, targets, num_segment...]
  transfers between devices with their start and end apart: 4 -> 20, of which waited for: 2 -> 12; matrix products, arithmetic and copies ran while one was open for 4% -> 0% of each run, Pallas kernels for 0% -> 4%
where the time goes in v1:
time: 48.1 us; the launch traced here: 47.9 us
  starting transfers between devices  25.3 us (53%)
  waiting for transfers between devices  16.4 us (34%)
  Pallas kernels  5.22 us (11%)
  between operations  0.72 us (1%)
    ppermute x19, starting transfers between devices, swap(): lax.ppermute(value, both, [(i, i ^ mask) for i in range(devices)])  22.7 us
    ppermute x19, waiting for transfers between devices, swap(): lax.ppermute(value, both, [(i, i ^ mask) for i in range(devices)])  16.4 us
    pallas_call x9, Pallas kernels, kernel(): pl.pallas_call(lambda *refs: body(*refs[:count], *refs[count + len(after)...  5.22 us
    ppermute x1, starting transfers between devices, shift(): return lax.ppermute(value, 'blk', pairs)  2.6 us
  transfers between devices with their start and end apart: 20, of which 12 were waited for; matrix products, arithmetic and copies ran while one was open for 0% of the time, Pallas kernels for 4%

profile of v1, /device:TPU:0, one launch (start us, length us, event | category | flops | bytes accessed | tf_op | source)
XLA Modules:
  0.0 47.9 jit_solution(5903213376022529287)
XLA Ops:
  0.6 1.3 %gather.1 = (f32[8,16,256]{2,1,0:T(8,128)S(1)}, f32[8,16,256]{2,1,0:T(8,128)S(1)}, bf16[128,256]{1,0:T(8,128)(2,1)S(1)}) custom-call(s32[1,16]{1,0:T(1,128)} %refs_0_.3, s32[1,256]{1,0:T(1,128)} %refs_1_.1, f32[128,256]{1,0:T(8,128)} %refs_2_.3), custom_call_target="tpu_custom_call" | custom-call | flops 16777216 | bytes 393216 | tf_op jit(solution)/shard_map/gather/pallas_call | solution.py:213
  2.4 2.6 %collective-permute-start = (f32[128,256]{1,0:T(8,128)S(1)}, f32[128,256]{1,0:T(8,128)S(1)}, u32[]{:S(2)}, u32[]{:S(2)}) collective-permute-start(f32[128,256]{1,0:T(8,128)S(1)} %copy-done), channel_id=1, source_target_pairs={{0,1},{1,0},{2,3},{3,2},{4,5},{5,4},{6,7},{7,6},{8,9},{9,8},{10,11... | collective-permute-start | bytes 393224 | tf_op jit(solution)/shard_map/ppermute | solution.py:237
  5.1 4.4 %collective-permute-start.8 = (f32[2,16,256]{2,1,0:T(8,128)S(1)}, f32[2,16,256]{2,1,0:T(8,128)S(1)}, u32[]{:S(2)}, u32[]{:S(2)}) collective-permute-start(f32[2,16,256]{2,1,0:T(8,128)S(1)} %get-tuple-element.43), channel_id=1, source_target_pairs={{0,30},{1,31},{2,28},{3,29},{4,26},{5,27},{6,24},{7,25},{8,22},{9,... | collective-permute-start | bytes 98312 | tf_op jit(solution)/shard_map/ppermute | solution.py:275
  9.6 0.5 %collective-permute-start.6 = (f32[2,16,256]{2,1,0:T(8,128)S(1)}, f32[2,16,256]{2,1,0:T(8,128)S(1)}, u32[]{:S(2)}, u32[]{:S(2)}) collective-permute-start(f32[2,16,256]{2,1,0:T(8,128)S(1)} %get-tuple-element.45), channel_id=1, source_target_pairs={{0,22},{1,23},{2,20},{3,21},{4,18},{5,19},{6,16},{7,17},{8,30},{9,... | collective-permute-start | bytes 98312 | tf_op jit(solution)/shard_map/ppermute | solution.py:275
  10.1 2.1 %collective-permute-start.5 = (f32[2,16,256]{2,1,0:T(8,128)S(1)}, f32[2,16,256]{2,1,0:T(8,128)S(1)}, u32[]{:S(2)}, u32[]{:S(2)}) collective-permute-start(f32[2,16,256]{2,1,0:T(8,128)S(1)} %get-tuple-element.46), channel_id=1, source_target_pairs={{0,18},{1,19},{2,16},{3,17},{4,22},{5,23},{6,20},{7,21},{8,26},{9,... | collective-permute-start | bytes 98312 | tf_op jit(solution)/shard_map/ppermute | solution.py:275
  12.2 2.2 %collective-permute-start.4 = (f32[2,16,256]{2,1,0:T(8,128)S(1)}, f32[2,16,256]{2,1,0:T(8,128)S(1)}, u32[]{:S(2)}, u32[]{:S(2)}) collective-permute-start(f32[2,16,256]{2,1,0:T(8,128)S(1)} %get-tuple-element.47), channel_id=1, source_target_pairs={{0,14},{1,15},{2,12},{3,13},{4,10},{5,11},{6,8},{7,9},{8,6},{9,7},... | collective-permute-start | bytes 98312 | tf_op jit(solution)/shard_map/ppermute | solution.py:275
  16.3 1.4 %collective-permute-done.4.refs_8_ = f32[2,16,256]{2,1,0:T(8,128)S(1)} collective-permute-done((f32[2,16,256]{2,1,0:T(8,128)S(1)}, f32[2,16,256]{2,1,0:T(8,128)S(1)}, u32[]{:S(2)}, u32[]{:S(2)}) %collective-permute-start.4) | collective-permute-done | bytes 32800 | tf_op jit(solution)/shard_map/ppermute | solution.py:275
  18.3 1.2 %layer.1 = (f32[128,256]{1,0:T(8,128)S(1)}, bf16[2,128,256]{2,1,0:T(8,128)(2,1)S(1)}, f32[256,256]{1,0:T(8,128)S(1)}, f32[256,256]{1,0:T(8,128)S(1)}) custom-call(f32[128,256]{1,0:T(8,128)S(1)} %get-tuple-element.24.refs_0_, bf16[2,128,256]{2,1,0:T(8,128)(2,1)S(1)} %get-tuple-element.25.refs_1_, bf16[2,256,256]{2,1,0:T(8,128)(2,1)S(1)} %get-tuple-element.26.refs_2_, ...), custom_call_target="tpu_custom_call" | custom-call | flops 251658240 | bytes 1048576 | tf_op jit(solution)/shard_map/layer/pallas_call | solution.py:213
  19.5 0.6 %collective-permute-start.9 = (f32[256,256]{1,0:T(8,128)S(1)}, f32[256,256]{1,0:T(8,128)S(1)}, u32[]{:S(2)}, u32[]{:S(2)}) collective-permute-start(f32[256,256]{1,0:T(8,128)S(1)} %get-tuple-element.35), channel_id=1, source_target_pairs={{0,2},{1,3},{2,0},{3,1},{4,6},{5,7},{6,4},{7,5},{8,10},{9,11},{10,... | collective-permute-start | bytes 786440 | tf_op jit(solution)/shard_map/ppermute | solution.py:275
  20.0 0.8 %inner.1 = (f32[128,256]{1,0:T(8,128)S(1)}, f32[1,128,256]{2,1,0:T(8,128)S(1)}, f32[128,256]{1,0:T(8,128)}) custom-call(bf16[2,2,128,128]{3,2,1,0:T(8,128)(2,1)S(1)} %get-tuple-element.23.refs_0_, bf16[2,128,256]{2,1,0:T(8,128)(2,1)S(1)} %get-tuple-element.29.refs_1_, f32[128,256]{1,0:T(8,128)S(1)} %get-tuple-element.30.refs_2_), custom_call_target="tpu_custom_call" | custom-call | flops 50331648 | bytes 786432 | tf_op jit(solution)/shard_map/inner/pallas_call | solution.py:213
  21.6 1.3 %collective-permute-start.11 = (f32[160,256]{1,0:T(8,128)S(1)}, f32[160,256]{1,0:T(8,128)S(1)}, u32[]{:S(2)}, u32[]{:S(2)}) collective-permute-start(f32[160,256]{1,0:T(8,128)S(1)} %get-tuple-element.38), channel_id=1, source_target_pairs={{0,1},{1,0},{2,3},{3,2},{4,5},{5,4},{6,7},{7,6},{8,9},{9,8},{10,11... | collective-permute-start | bytes 491528 | tf_op jit(solution)/shard_map/ppermute | solution.py:275
  22.8 1.4 %collective-permute-start.12 = (f32[32,256]{1,0:T(8,128)S(1)}, f32[32,256]{1,0:T(8,128)S(1)}, u32[]{:S(2)}, u32[]{:S(2)}) collective-permute-start(f32[32,256]{1,0:T(8,128)S(1)} %get-tuple-element.39), channel_id=1, source_target_pairs={{0,7},{1,6},{2,5},{3,4},{4,3},{5,2},{6,1},{7,0},{8,15},{9,14},{10,... | collective-permute-start | bytes 98312 | tf_op jit(solution)/shard_map/ppermute | solution.py:275
  24.2 4.5 %collective-permute-done.12.refs_2_ = f32[32,256]{1,0:T(8,128)S(1)} collective-permute-done((f32[32,256]{1,0:T(8,128)S(1)}, f32[32,256]{1,0:T(8,128)S(1)}, u32[]{:S(2)}, u32[]{:S(2)}) %collective-permute-start.12) | collective-permute-done | bytes 32800 | tf_op jit(solution)/shard_map/ppermute | solution.py:275
  28.8 3.6 %collective-permute-start.13 = (f32[96,256]{1,0:T(8,128)S(1)}, f32[96,256]{1,0:T(8,128)S(1)}, u32[]{:S(2)}, u32[]{:S(2)}) collective-permute-start(f32[96,256]{1,0:T(8,128)S(1)} %get-tuple-element.40), channel_id=1, source_target_pairs={{0,24},{1,25},{2,26},{3,27},{4,28},{5,29},{6,30},{7,31},{8,16},{9,... | collective-permute-start | bytes 294920 | tf_op jit(solution)/shard_map/ppermute | solution.py:275
  32.4 0.5 %collective-permute-start.15 = (f32[96,256]{1,0:T(8,128)S(1)}, f32[96,256]{1,0:T(8,128)S(1)}, u32[]{:S(2)}, u32[]{:S(2)}) collective-permute-start(f32[96,256]{1,0:T(8,128)S(1)} %get-tuple-element.42), channel_id=1, source_target_pairs={{0,10},{1,11},{2,8},{3,9},{4,14},{5,15},{6,12},{7,13},{8,2},{9,3},... | collective-permute-start | bytes 294920 | tf_op jit(solution)/shard_map/ppermute | solution.py:275
  33.0 3.4 %collective-permute-done.13.refs_6_.refs_5_ = f32[96,256]{1,0:T(8,128)S(1)} collective-permute-done((f32[96,256]{1,0:T(8,128)S(1)}, f32[96,256]{1,0:T(8,128)S(1)}, u32[]{:S(2)}, u32[]{:S(2)}) %collective-permute-start.13) | collective-permute-done | bytes 98336 | tf_op jit(solution)/shard_map/ppermute | solution.py:275
  36.4 3.7 %collective-permute-done.14.refs_7_.refs_6_ = f32[96,256]{1,0:T(8,128)S(1)} collective-permute-done((f32[96,256]{1,0:T(8,128)S(1)}, f32[96,256]{1,0:T(8,128)S(1)}, u32[]{:S(2)}, u32[]{:S(2)}) %collective-permute-start.14) | collective-permute-done | bytes 98336 | tf_op jit(solution)/shard_map/ppermute | solution.py:275
  40.1 1.7 %collective-permute-start.18 = (f32[1,32,256]{2,1,0:T(8,128)S(1)}, f32[1,32,256]{2,1,0:T(8,128)S(1)}, u32[]{:S(2)}, u32[]{:S(2)}) collective-permute-start(f32[1,32,256]{2,1,0:T(8,128)S(1)} %bitcast.23), channel_id=1, source_target_pairs={{0,7},{1,6},{2,5},{3,4},{4,3},{5,2},{6,1},{7,0},{8,15},{9,14},{10,... | collective-permute-start | bytes 98312 | tf_op jit(solution)/shard_map/ppermute | solution.py:275
  42.0 1.4 %collective-permute-start.16 = (f32[1,32,256]{2,1,0:T(8,128)S(1)}, f32[1,32,256]{2,1,0:T(8,128)S(1)}, u32[]{:S(2)}, u32[]{:S(2)}) collective-permute-start(f32[1,32,256]{2,1,0:T(8,128)S(1)} %bitcast.25), channel_id=1, source_target_pairs={{0,3},{1,2},{2,1},{3,0},{4,7},{5,6},{6,5},{7,4},{8,11},{9,10},{10,... | collective-permute-start | bytes 98312 | tf_op jit(solution)/shard_map/ppermute | solution.py:275
  43.4 1.0 %collective-permute-done.18 = f32[1,32,256]{2,1,0:T(8,128)S(1)} collective-permute-done((f32[1,32,256]{2,1,0:T(8,128)S(1)}, f32[1,32,256]{2,1,0:T(8,128)S(1)}, u32[]{:S(2)}, u32[]{:S(2)}) %collective-permute-start.18) | collective-permute-done | bytes 32800 | tf_op jit(solution)/shard_map/ppermute | solution.py:275
  44.4 0.7 %collective-permute-done.17 = f32[1,32,256]{2,1,0:T(8,128)S(1)} collective-permute-done((f32[1,32,256]{2,1,0:T(8,128)S(1)}, f32[1,32,256]{2,1,0:T(8,128)S(1)}, u32[]{:S(2)}, u32[]{:S(2)}) %collective-permute-start.17) | collective-permute-done | bytes 32800 | tf_op jit(solution)/shard_map/ppermute | solution.py:275
  45.4 0.8 %collective-permute-start.19 = (f32[4,32,256]{2,1,0:T(8,128)S(1)}, f32[4,32,256]{2,1,0:T(8,128)S(1)}, u32[]{:S(2)}, u32[]{:S(2)}) collective-permute-start(f32[4,32,256]{2,1,0:T(8,128)S(1)} %pad_maximum_fusion.refs_0_), channel_id=1, source_target_pairs={{0,2},{1,3},{2,0},{3,1},{4,6},{5,7},{6,4},{7,5},{8,10},{9,11},{10,... | collective-permute-start | bytes 393224 | tf_op jit(solution)/shard_map/ppermute | solution.py:275
  46.2 0.9 %finish.1 = f32[128,256]{1,0:T(8,128)} custom-call(bf16[128,256]{1,0:T(8,128)(2,1)S(1)} %get-tuple-element.32.refs_0_, f32[128,256]{1,0:T(8,128)S(1)} %get-tuple-element.33.refs_1_, f32[256,256]{1,0:T(8,128)S(1)} %get-tuple-element.34.refs_0_.refs_2_, f32[256,256]{1,0:T(8,128)S(1)} %collective-permute-done.9.refs_1_.refs_3_, ...), custom_call_target="tpu_custom_call" | custom-call | flops 33554432 | bytes 655360 | tf_op jit(solution)/shard_map/finish/pallas_call | solution.py:213
  47.2 0.7 %place.1 = f32[256,256]{1,0:T(8,128)} custom-call(f32[4,32,256]{2,1,0:T(8,128)S(1)} %pad_maximum_fusion.refs_0_, f32[4,32,256]{2,1,0:T(8,128)S(1)} %collective-permute-done.19.refs_1_), custom_call_target="tpu_custom_call" | custom-call | bytes 524288 | tf_op jit(solution)/shard_map/place/pallas_call | solution.py:213
  (39 shorter events, 4.6 us)
Async XLA Ops:
  0.6 1.8 %copy-start = (f32[128,256]{1,0:T(8,128)S(1)}, f32[128,256]{1,0:T(8,128)}, u32[]{:S(2)}) copy-start(f32[128,256]{1,0:T(8,128)} %refs_2_.3) | copy-start | bytes 393220
  1.9 13.4 %copy-start.1 = (f32[256,256]{1,0:T(8,128)S(1)}, f32[256,256]{1,0:T(8,128)}, u32[]{:S(2)}) copy-start(f32[256,256]{1,0:T(8,128)} %refs_3_.2) | copy-start | bytes 786436
  1.9 3.1 %collective-permute-start.1 = (f32[8,16,256]{2,1,0:T(8,128)S(1)}, f32[8,16,256]{2,1,0:T(8,128)S(1)}, u32[]{:S(2)}, u32[]{:S(2)}) collective-permute-start(f32[8,16,256]{2,1,0:T(8,128)S(1)} %get-tuple-element.28), channel_id=1, source_target_pairs={{0,2},{1,3},{2,0},{3,1},{4,6},{5,7},{6,4},{7,5},{8,10},{9,11},{10,... | collective-permute-start | bytes 393224 | tf_op jit(solution)/shard_map/ppermute | solution.py:275
  2.4 9.8 %collective-permute-start = (f32[128,256]{1,0:T(8,128)S(1)}, f32[128,256]{1,0:T(8,128)S(1)}, u32[]{:S(2)}, u32[]{:S(2)}) collective-permute-start(f32[128,256]{1,0:T(8,128)S(1)} %copy-done), channel_id=1, source_target_pairs={{0,1},{1,0},{2,3},{3,2},{4,5},{5,4},{6,7},{7,6},{8,9},{9,8},{10,11... | collective-permute-start | bytes 393224 | tf_op jit(solution)/shard_map/ppermute | solution.py:237
  5.0 10.3 %copy-start.2 = (f32[128,256]{1,0:T(8,128)S(1)}, f32[128,256]{1,0:T(8,128)}, u32[]{:S(2)}) copy-start(f32[128,256]{1,0:T(8,128)} %refs_2_.2) | copy-start | bytes 393220
  5.1 9.3 %collective-permute-start.8 = (f32[2,16,256]{2,1,0:T(8,128)S(1)}, f32[2,16,256]{2,1,0:T(8,128)S(1)}, u32[]{:S(2)}, u32[]{:S(2)}) collective-permute-start(f32[2,16,256]{2,1,0:T(8,128)S(1)} %get-tuple-element.43), channel_id=1, source_target_pairs={{0,30},{1,31},{2,28},{3,29},{4,26},{5,27},{6,24},{7,25},{8,22},{9,... | collective-permute-start | bytes 98312 | tf_op jit(solution)/shard_map/ppermute | solution.py:275
  9.4 5.5 %collective-permute-start.7 = (f32[2,16,256]{2,1,0:T(8,128)S(1)}, f32[2,16,256]{2,1,0:T(8,128)S(1)}, u32[]{:S(2)}, u32[]{:S(2)}) collective-permute-start(f32[2,16,256]{2,1,0:T(8,128)S(1)} %get-tuple-element.44), channel_id=1, source_target_pairs={{0,26},{1,27},{2,24},{3,25},{4,30},{5,31},{6,28},{7,29},{8,18},{9,... | collective-permute-start | bytes 98312 | tf_op jit(solution)/shard_map/ppermute | solution.py:275
  9.6 6.7 %collective-permute-start.6 = (f32[2,16,256]{2,1,0:T(8,128)S(1)}, f32[2,16,256]{2,1,0:T(8,128)S(1)}, u32[]{:S(2)}, u32[]{:S(2)}) collective-permute-start(f32[2,16,256]{2,1,0:T(8,128)S(1)} %get-tuple-element.45), channel_id=1, source_target_pairs={{0,22},{1,23},{2,20},{3,21},{4,18},{5,19},{6,16},{7,17},{8,30},{9,... | collective-permute-start | bytes 98312 | tf_op jit(solution)/shard_map/ppermute | solution.py:275
  10.1 6.1 %collective-permute-start.5 = (f32[2,16,256]{2,1,0:T(8,128)S(1)}, f32[2,16,256]{2,1,0:T(8,128)S(1)}, u32[]{:S(2)}, u32[]{:S(2)}) collective-permute-start(f32[2,16,256]{2,1,0:T(8,128)S(1)} %get-tuple-element.46), channel_id=1, source_target_pairs={{0,18},{1,19},{2,16},{3,17},{4,22},{5,23},{6,20},{7,21},{8,26},{9,... | collective-permute-start | bytes 98312 | tf_op jit(solution)/shard_map/ppermute | solution.py:275
  12.2 5.4 %collective-permute-start.4 = (f32[2,16,256]{2,1,0:T(8,128)S(1)}, f32[2,16,256]{2,1,0:T(8,128)S(1)}, u32[]{:S(2)}, u32[]{:S(2)}) collective-permute-start(f32[2,16,256]{2,1,0:T(8,128)S(1)} %get-tuple-element.47), channel_id=1, source_target_pairs={{0,14},{1,15},{2,12},{3,13},{4,10},{5,11},{6,8},{7,9},{8,6},{9,7},... | collective-permute-start | bytes 98312 | tf_op jit(solution)/shard_map/ppermute | solution.py:275
  14.4 3.4 %collective-permute-start.3 = (f32[2,16,256]{2,1,0:T(8,128)S(1)}, f32[2,16,256]{2,1,0:T(8,128)S(1)}, u32[]{:S(2)}, u32[]{:S(2)}) collective-permute-start(f32[2,16,256]{2,1,0:T(8,128)S(1)} %get-tuple-element.48), channel_id=1, source_target_pairs={{0,10},{1,11},{2,8},{3,9},{4,14},{5,15},{6,12},{7,13},{8,2},{9,3},... | collective-permute-start | bytes 98312 | tf_op jit(solution)/shard_map/ppermute | solution.py:275
  14.9 3.3 %collective-permute-start.2 = (f32[2,16,256]{2,1,0:T(8,128)S(1)}, f32[2,16,256]{2,1,0:T(8,128)S(1)}, u32[]{:S(2)}, u32[]{:S(2)}) collective-permute-start(f32[2,16,256]{2,1,0:T(8,128)S(1)} %get-tuple-element.49), channel_id=1, source_target_pairs={{0,6},{1,7},{2,4},{3,5},{4,2},{5,3},{6,0},{7,1},{8,14},{9,15},{10,... | collective-permute-start | bytes 98312 | tf_op jit(solution)/shard_map/ppermute | solution.py:275
  15.6 2.7 %copy-start.3 = (f32[128,256]{1,0:T(8,128)S(1)}, f32[128,256]{1,0:T(8,128)}, u32[]{:S(2)}) copy-start(f32[128,256]{1,0:T(8,128)} %refs_3_.3) | copy-start | bytes 393220
  19.5 1.8 %collective-permute-start.9 = (f32[256,256]{1,0:T(8,128)S(1)}, f32[256,256]{1,0:T(8,128)S(1)}, u32[]{:S(2)}, u32[]{:S(2)}) collective-permute-start(f32[256,256]{1,0:T(8,128)S(1)} %get-tuple-element.35), channel_id=1, source_target_pairs={{0,2},{1,3},{2,0},{3,1},{4,6},{5,7},{6,4},{7,5},{8,10},{9,11},{10,... | collective-permute-start | bytes 786440 | tf_op jit(solution)/shard_map/ppermute | solution.py:275
  21.2 7.5 %collective-permute-start.10 = (f32[160,256]{1,0:T(8,128)S(1)}, f32[160,256]{1,0:T(8,128)S(1)}, u32[]{:S(2)}, u32[]{:S(2)}) collective-permute-start(f32[160,256]{1,0:T(8,128)S(1)} %get-tuple-element.37), channel_id=1, source_target_pairs={{0,6},{1,7},{2,4},{3,5},{4,2},{5,3},{6,0},{7,1},{8,14},{9,15},{10,... | collective-permute-start | bytes 491528 | tf_op jit(solution)/shard_map/ppermute | solution.py:275
  21.6 7.2 %collective-permute-start.11 = (f32[160,256]{1,0:T(8,128)S(1)}, f32[160,256]{1,0:T(8,128)S(1)}, u32[]{:S(2)}, u32[]{:S(2)}) collective-permute-start(f32[160,256]{1,0:T(8,128)S(1)} %get-tuple-element.38), channel_id=1, source_target_pairs={{0,1},{1,0},{2,3},{3,2},{4,5},{5,4},{6,7},{7,6},{8,9},{9,8},{10,11... | collective-permute-start | bytes 491528 | tf_op jit(solution)/shard_map/ppermute | solution.py:275
  22.8 5.9 %collective-permute-start.12 = (f32[32,256]{1,0:T(8,128)S(1)}, f32[32,256]{1,0:T(8,128)S(1)}, u32[]{:S(2)}, u32[]{:S(2)}) collective-permute-start(f32[32,256]{1,0:T(8,128)S(1)} %get-tuple-element.39), channel_id=1, source_target_pairs={{0,7},{1,6},{2,5},{3,4},{4,3},{5,2},{6,1},{7,0},{8,15},{9,14},{10,... | collective-permute-start | bytes 98312 | tf_op jit(solution)/shard_map/ppermute | solution.py:275
  28.8 7.6 %collective-permute-start.13 = (f32[96,256]{1,0:T(8,128)S(1)}, f32[96,256]{1,0:T(8,128)S(1)}, u32[]{:S(2)}, u32[]{:S(2)}) collective-permute-start(f32[96,256]{1,0:T(8,128)S(1)} %get-tuple-element.40), channel_id=1, source_target_pairs={{0,24},{1,25},{2,26},{3,27},{4,28},{5,29},{6,30},{7,31},{8,16},{9,... | collective-permute-start | bytes 294920 | tf_op jit(solution)/shard_map/ppermute | solution.py:275
  32.4 7.7 %collective-permute-start.14 = (f32[96,256]{1,0:T(8,128)S(1)}, f32[96,256]{1,0:T(8,128)S(1)}, u32[]{:S(2)}, u32[]{:S(2)}) collective-permute-start(f32[96,256]{1,0:T(8,128)S(1)} %get-tuple-element.41), channel_id=1, source_target_pairs={{0,18},{1,19},{2,16},{3,17},{4,22},{5,23},{6,20},{7,21},{8,26},{9,... | collective-permute-start | bytes 294920 | tf_op jit(solution)/shard_map/ppermute | solution.py:275
  32.4 7.7 %collective-permute-start.15 = (f32[96,256]{1,0:T(8,128)S(1)}, f32[96,256]{1,0:T(8,128)S(1)}, u32[]{:S(2)}, u32[]{:S(2)}) collective-permute-start(f32[96,256]{1,0:T(8,128)S(1)} %get-tuple-element.42), channel_id=1, source_target_pairs={{0,10},{1,11},{2,8},{3,9},{4,14},{5,15},{6,12},{7,13},{8,2},{9,3},... | collective-permute-start | bytes 294920 | tf_op jit(solution)/shard_map/ppermute | solution.py:275
  40.1 4.3 %collective-permute-start.18 = (f32[1,32,256]{2,1,0:T(8,128)S(1)}, f32[1,32,256]{2,1,0:T(8,128)S(1)}, u32[]{:S(2)}, u32[]{:S(2)}) collective-permute-start(f32[1,32,256]{2,1,0:T(8,128)S(1)} %bitcast.23), channel_id=1, source_target_pairs={{0,7},{1,6},{2,5},{3,4},{4,3},{5,2},{6,1},{7,0},{8,15},{9,14},{10,... | collective-permute-start | bytes 98312 | tf_op jit(solution)/shard_map/ppermute | solution.py:275
  41.8 3.3 %collective-permute-start.17 = (f32[1,32,256]{2,1,0:T(8,128)S(1)}, f32[1,32,256]{2,1,0:T(8,128)S(1)}, u32[]{:S(2)}, u32[]{:S(2)}) collective-permute-start(f32[1,32,256]{2,1,0:T(8,128)S(1)} %bitcast.24), channel_id=1, source_target_pairs={{0,6},{1,7},{2,4},{3,5},{4,2},{5,3},{6,0},{7,1},{8,14},{9,15},{10,... | collective-permute-start | bytes 98312 | tf_op jit(solution)/shard_map/ppermute | solution.py:275
  42.0 3.4 %collective-permute-start.16 = (f32[1,32,256]{2,1,0:T(8,128)S(1)}, f32[1,32,256]{2,1,0:T(8,128)S(1)}, u32[]{:S(2)}, u32[]{:S(2)}) collective-permute-start(f32[1,32,256]{2,1,0:T(8,128)S(1)} %bitcast.25), channel_id=1, source_target_pairs={{0,3},{1,2},{2,1},{3,0},{4,7},{5,6},{6,5},{7,4},{8,11},{9,10},{10,... | collective-permute-start | bytes 98312 | tf_op jit(solution)/shard_map/ppermute | solution.py:275
  45.4 1.8 %collective-permute-start.19 = (f32[4,32,256]{2,1,0:T(8,128)S(1)}, f32[4,32,256]{2,1,0:T(8,128)S(1)}, u32[]{:S(2)}, u32[]{:S(2)}) collective-permute-start(f32[4,32,256]{2,1,0:T(8,128)S(1)} %pad_maximum_fusion.refs_0_), channel_id=1, source_target_pairs={{0,2},{1,3},{2,0},{3,1},{4,6},{5,7},{6,4},{7,5},{8,10},{9,11},{10,... | collective-permute-start | bytes 393224 | tf_op jit(solution)/shard_map/ppermute | solution.py:275
  (2 other events, 1.4 us)

commit v2 on v1

--- a/solution.py
+++ b/solution.py
@@ -345,14 +345,16 @@
     }
     far_pieces = []
 
-    def pack(name, layout, scale=None):
+    def pack(name, layout, scale=None, after=()):
         used = sorted({leaf[0] for pieces in layout for leaf in leaves(pieces)})
         layout = [[renumber(piece, used) for piece in pieces] for pieces in layout]
         out = tuple(array((sum(map(rows_of, pieces)), width), F32) for pieces in layout)
         operands = [arrays[i] for i in used]
         traffic = 8 * width * sum(o.shape[0] for o in out)
-        return kernel(functools.partial(pack_kernel, layout, scale, len(used)), name, out, operands, traffic=traffic)
-
+        return kernel(functools.partial(pack_kernel, layout, scale, len(used)), name, out, operands, traffic=traffic, after=after)
+
+    all_outer = sum(1 << bit for bit in outer_bits) >> low
+    early = ()
     for bits in pairs + [outer_bits]:
         last = bits is outer_bits
         keeps = len(terms) if last else len(terms) >> len(bits)
@@ -369,21 +371,30 @@
                 arrays.append(leaving[0])
                 pieces.append((len(arrays) - 1, 0, rows))
             layout.append(pieces)
-        sent = pack("pack", layout)
-        came = []
-        for (_, mask), value, rides in zip(partners, sent, riders):
+        leaders = masks(outer_bits)[:1:-1] if bits is pairs[-1] else []
+        for mask in leaders:
+            way = mask >> low
+            going = [q for q in sorted(moving) if q & ~1 == way & all_outer]
+            riders.append([(q, come) for q in going for come, _ in moving[q]])
+            layout.append([piece for q in going for _, piece in moving[q]])
+        sent = pack("pack", layout, after=early)
+        came, count = [], len(partners)
+        partners = [mask for _, mask in partners] + leaders
+        for q in {q for rides in riders for q, _ in rides}:
+            del moving[q]
+        for i, (mask, value, rides) in enumerate(zip(partners, sent, riders)):
             arrays.append(swap(value, mask))
             number, first = len(arrays) - 1, 0
-            came.append([(number, j * share, share) for j in range(keeps)])
-            first = keeps * share
+            if i < count:
+                came.append([(number, j * share, share) for j in range(keeps)])
+                first = keeps * share
             for q, come in rides:
                 way = mask >> low
                 moving.setdefault(q ^ way, []).append((come ^ way, (number, first, per_peer)))
                 first += per_peer
             if blocks == 2 and mask == 1:
                 far_pieces.append((number, first, rows))
-            for q in {q for q, _ in rides}:
-                del moving[q]
+        early = tuple(arrays[len(arrays) - len(leaders) :]) if leaders else ()
         terms = [[terms[j]] + [pieces[j] for pieces in reversed(came)] for j in range(keeps)]
     if blocks > 2:
         for step in range(1, blocks):

time: 48.1 us -> 49.8 us (1.035)
  starting transfers between devices: 25.3 us -> 27 us
    ppermute x19 -> x21, starting transfers between devices: 22.7 us -> 24.4 us  [swap(): lax.ppermute(value, both, [(i, i ^ mask) for i in range(devices)])]
    ppermute x19 -> x21, waiting for transfers between devices: 16.4 us -> 16.4 us  [swap(): lax.ppermute(value, both, [(i, i ^ mask) for i in range(devices)])]
  transfers between devices with their start and end apart: 20 -> 22, of which waited for: 12 -> 12; matrix products, arithmetic and copies ran while one was open for 0% -> 0% of each run, Pallas kernels for 4% -> 4%
where the time goes in v2:
time: 49.8 us; the launch traced here: 49.6 us
  starting transfers between devices  27 us (54%)
  waiting for transfers between devices  16.4 us (33%)
  Pallas kernels  5.22 us (10%)
  between operations  0.73 us (1%)
    ppermute x21, starting transfers between devices, swap(): lax.ppermute(value, both, [(i, i ^ mask) for i in range(devices)])  24.4 us
    ppermute x21, waiting for transfers between devices, swap(): lax.ppermute(value, both, [(i, i ^ mask) for i in range(devices)])  16.4 us
    pallas_call x9, Pallas kernels, kernel(): pl.pallas_call(lambda *refs: body(*refs[:count], *refs[count + len(after)...  5.22 us
    ppermute x1, starting transfers between devices, shift(): return lax.ppermute(value, 'blk', pairs)  2.6 us
  transfers between devices with their start and end apart: 22, of which 12 were waited for; matrix products, arithmetic and copies ran while one was open for 0% of the time, Pallas kernels for 4%

profile of v2, /device:TPU:0, one launch (start us, length us, event | category | flops | bytes accessed | tf_op | source)
XLA Modules:
  0.0 49.6 jit_solution(5614721823315223506)
XLA Ops:
  0.6 1.3 %gather.1 = (f32[8,16,256]{2,1,0:T(8,128)S(1)}, f32[8,16,256]{2,1,0:T(8,128)S(1)}, bf16[128,256]{1,0:T(8,128)(2,1)S(1)}) custom-call(s32[1,16]{1,0:T(1,128)} %refs_0_.3, s32[1,256]{1,0:T(1,128)} %refs_1_.1, f32[128,256]{1,0:T(8,128)} %refs_2_.3), custom_call_target="tpu_custom_call" | custom-call | flops 16777216 | bytes 393216 | tf_op jit(solution)/shard_map/gather/pallas_call | solution.py:213
  2.4 2.6 %collective-permute-start = (f32[128,256]{1,0:T(8,128)S(1)}, f32[128,256]{1,0:T(8,128)S(1)}, u32[]{:S(2)}, u32[]{:S(2)}) collective-permute-start(f32[128,256]{1,0:T(8,128)S(1)} %copy-done), channel_id=1, source_target_pairs={{0,1},{1,0},{2,3},{3,2},{4,5},{5,4},{6,7},{7,6},{8,9},{9,8},{10,11... | collective-permute-start | bytes 393224 | tf_op jit(solution)/shard_map/ppermute | solution.py:237
  5.1 4.4 %collective-permute-start.8 = (f32[2,16,256]{2,1,0:T(8,128)S(1)}, f32[2,16,256]{2,1,0:T(8,128)S(1)}, u32[]{:S(2)}, u32[]{:S(2)}) collective-permute-start(f32[2,16,256]{2,1,0:T(8,128)S(1)} %get-tuple-element.47), channel_id=1, source_target_pairs={{0,30},{1,31},{2,28},{3,29},{4,26},{5,27},{6,24},{7,25},{8,22},{9,... | collective-permute-start | bytes 98312 | tf_op jit(solution)/shard_map/ppermute | solution.py:275
  10.1 2.1 %collective-permute-start.5 = (f32[2,16,256]{2,1,0:T(8,128)S(1)}, f32[2,16,256]{2,1,0:T(8,128)S(1)}, u32[]{:S(2)}, u32[]{:S(2)}) collective-permute-start(f32[2,16,256]{2,1,0:T(8,128)S(1)} %get-tuple-element.50), channel_id=1, source_target_pairs={{0,18},{1,19},{2,16},{3,17},{4,22},{5,23},{6,20},{7,21},{8,26},{9,... | collective-permute-start | bytes 98312 | tf_op jit(solution)/shard_map/ppermute | solution.py:275
  12.2 2.2 %collective-permute-start.4 = (f32[2,16,256]{2,1,0:T(8,128)S(1)}, f32[2,16,256]{2,1,0:T(8,128)S(1)}, u32[]{:S(2)}, u32[]{:S(2)}) collective-permute-start(f32[2,16,256]{2,1,0:T(8,128)S(1)} %get-tuple-element.51), channel_id=1, source_target_pairs={{0,14},{1,15},{2,12},{3,13},{4,10},{5,11},{6,8},{7,9},{8,6},{9,7},... | collective-permute-start | bytes 98312 | tf_op jit(solution)/shard_map/ppermute | solution.py:275
  16.3 1.4 %collective-permute-done.4.refs_8_ = f32[2,16,256]{2,1,0:T(8,128)S(1)} collective-permute-done((f32[2,16,256]{2,1,0:T(8,128)S(1)}, f32[2,16,256]{2,1,0:T(8,128)S(1)}, u32[]{:S(2)}, u32[]{:S(2)}) %collective-permute-start.4) | collective-permute-done | bytes 32800 | tf_op jit(solution)/shard_map/ppermute | solution.py:275
  18.3 1.2 %layer.1 = (f32[128,256]{1,0:T(8,128)S(1)}, bf16[2,128,256]{2,1,0:T(8,128)(2,1)S(1)}, f32[256,256]{1,0:T(8,128)S(1)}, f32[256,256]{1,0:T(8,128)S(1)}) custom-call(f32[128,256]{1,0:T(8,128)S(1)} %get-tuple-element.26.refs_0_, bf16[2,128,256]{2,1,0:T(8,128)(2,1)S(1)} %get-tuple-element.27.refs_1_, bf16[2,256,256]{2,1,0:T(8,128)(2,1)S(1)} %get-tuple-element.28.refs_2_, ...), custom_call_target="tpu_custom_call" | custom-call | flops 251658240 | bytes 1048576 | tf_op jit(solution)/shard_map/layer/pallas_call | solution.py:213
  19.5 0.6 %collective-permute-start.9 = (f32[256,256]{1,0:T(8,128)S(1)}, f32[256,256]{1,0:T(8,128)S(1)}, u32[]{:S(2)}, u32[]{:S(2)}) collective-permute-start(f32[256,256]{1,0:T(8,128)S(1)} %get-tuple-element.37), channel_id=1, source_target_pairs={{0,2},{1,3},{2,0},{3,1},{4,6},{5,7},{6,4},{7,5},{8,10},{9,11},{10,... | collective-permute-start | bytes 786440 | tf_op jit(solution)/shard_map/ppermute | solution.py:275
  20.0 0.8 %inner.1 = (f32[128,256]{1,0:T(8,128)S(1)}, f32[1,128,256]{2,1,0:T(8,128)S(1)}, f32[128,256]{1,0:T(8,128)}) custom-call(bf16[2,2,128,128]{3,2,1,0:T(8,128)(2,1)S(1)} %get-tuple-element.25.refs_0_, bf16[2,128,256]{2,1,0:T(8,128)(2,1)S(1)} %get-tuple-element.31.refs_1_, f32[128,256]{1,0:T(8,128)S(1)} %get-tuple-element.32.refs_2_), custom_call_target="tpu_custom_call" | custom-call | flops 50331648 | bytes 786432 | tf_op jit(solution)/shard_map/inner/pallas_call | solution.py:213
  21.6 1.3 %collective-permute-start.11 = (f32[160,256]{1,0:T(8,128)S(1)}, f32[160,256]{1,0:T(8,128)S(1)}, u32[]{:S(2)}, u32[]{:S(2)}) collective-permute-start(f32[160,256]{1,0:T(8,128)S(1)} %get-tuple-element.40), channel_id=1, source_target_pairs={{0,1},{1,0},{2,3},{3,2},{4,5},{5,4},{6,7},{7,6},{8,9},{9,8},{10,11... | collective-permute-start | bytes 491528 | tf_op jit(solution)/shard_map/ppermute | solution.py:275
  22.9 3.7 %collective-permute-start.12 = (f32[32,256]{1,0:T(8,128)S(1)}, f32[32,256]{1,0:T(8,128)S(1)}, u32[]{:S(2)}, u32[]{:S(2)}) collective-permute-start(f32[32,256]{1,0:T(8,128)S(1)} %get-tuple-element.41), channel_id=1, source_target_pairs={{0,24},{1,25},{2,26},{3,27},{4,28},{5,29},{6,30},{7,31},{8,16},{9,... | collective-permute-start | bytes 98312 | tf_op jit(solution)/shard_map/ppermute | solution.py:275
  26.5 0.9 %collective-permute-start.14 = (f32[32,256]{1,0:T(8,128)S(1)}, f32[32,256]{1,0:T(8,128)S(1)}, u32[]{:S(2)}, u32[]{:S(2)}) collective-permute-start(f32[32,256]{1,0:T(8,128)S(1)} %get-tuple-element.43), channel_id=1, source_target_pairs={{0,7},{1,6},{2,5},{3,4},{4,3},{5,2},{6,1},{7,0},{8,15},{9,14},{10,... | collective-permute-start | bytes 98312 | tf_op jit(solution)/shard_map/ppermute | solution.py:275
  27.4 1.1 %collective-permute-done.12.refs_5_.refs_6_ = f32[32,256]{1,0:T(8,128)S(1)} collective-permute-done((f32[32,256]{1,0:T(8,128)S(1)}, f32[32,256]{1,0:T(8,128)S(1)}, u32[]{:S(2)}, u32[]{:S(2)}) %collective-permute-start.12) | collective-permute-done | bytes 32800 | tf_op jit(solution)/shard_map/ppermute | solution.py:275
  28.6 2.5 %collective-permute-done.13.refs_6_.refs_7_ = f32[32,256]{1,0:T(8,128)S(1)} collective-permute-done((f32[32,256]{1,0:T(8,128)S(1)}, f32[32,256]{1,0:T(8,128)S(1)}, u32[]{:S(2)}, u32[]{:S(2)}) %collective-permute-start.13) | collective-permute-done | bytes 32800 | tf_op jit(solution)/shard_map/ppermute | solution.py:275
  31.3 3.7 %collective-permute-start.15 = (f32[64,256]{1,0:T(8,128)S(1)}, f32[64,256]{1,0:T(8,128)S(1)}, u32[]{:S(2)}, u32[]{:S(2)}) collective-permute-start(f32[64,256]{1,0:T(8,128)S(1)} %get-tuple-element.44), channel_id=1, source_target_pairs={{0,24},{1,25},{2,26},{3,27},{4,28},{5,29},{6,30},{7,31},{8,16},{9,... | collective-permute-start | bytes 196616 | tf_op jit(solution)/shard_map/ppermute | solution.py:275
  35.0 5.0 %collective-permute-done.15.refs_8_.refs_5_ = f32[64,256]{1,0:T(8,128)S(1)} collective-permute-done((f32[64,256]{1,0:T(8,128)S(1)}, f32[64,256]{1,0:T(8,128)S(1)}, u32[]{:S(2)}, u32[]{:S(2)}) %collective-permute-start.15) | collective-permute-done | bytes 65568 | tf_op jit(solution)/shard_map/ppermute | solution.py:275
  39.9 2.0 %collective-permute-done.16.refs_9_.refs_6_ = f32[64,256]{1,0:T(8,128)S(1)} collective-permute-done((f32[64,256]{1,0:T(8,128)S(1)}, f32[64,256]{1,0:T(8,128)S(1)}, u32[]{:S(2)}, u32[]{:S(2)}) %collective-permute-start.16) | collective-permute-done | bytes 65568 | tf_op jit(solution)/shard_map/ppermute | solution.py:275
  42.0 1.1 %collective-permute-start.20 = (f32[1,32,256]{2,1,0:T(8,128)S(1)}, f32[1,32,256]{2,1,0:T(8,128)S(1)}, u32[]{:S(2)}, u32[]{:S(2)}) collective-permute-start(f32[1,32,256]{2,1,0:T(8,128)S(1)} %bitcast.23), channel_id=1, source_target_pairs={{0,7},{1,6},{2,5},{3,4},{4,3},{5,2},{6,1},{7,0},{8,15},{9,14},{10,... | collective-permute-start | bytes 98312 | tf_op jit(solution)/shard_map/ppermute | solution.py:275
  43.1 0.9 %collective-permute-start.19 = (f32[1,32,256]{2,1,0:T(8,128)S(1)}, f32[1,32,256]{2,1,0:T(8,128)S(1)}, u32[]{:S(2)}, u32[]{:S(2)}) collective-permute-start(f32[1,32,256]{2,1,0:T(8,128)S(1)} %bitcast.24), channel_id=1, source_target_pairs={{0,6},{1,7},{2,4},{3,5},{4,2},{5,3},{6,0},{7,1},{8,14},{9,15},{10,... | collective-permute-start | bytes 98312 | tf_op jit(solution)/shard_map/ppermute | solution.py:275
  44.0 0.9 %collective-permute-start.18 = (f32[1,32,256]{2,1,0:T(8,128)S(1)}, f32[1,32,256]{2,1,0:T(8,128)S(1)}, u32[]{:S(2)}, u32[]{:S(2)}) collective-permute-start(f32[1,32,256]{2,1,0:T(8,128)S(1)} %bitcast.25), channel_id=1, source_target_pairs={{0,3},{1,2},{2,1},{3,0},{4,7},{5,6},{6,5},{7,4},{8,11},{9,10},{10,... | collective-permute-start | bytes 98312 | tf_op jit(solution)/shard_map/ppermute | solution.py:275
  44.8 1.6 %collective-permute-done.20 = f32[1,32,256]{2,1,0:T(8,128)S(1)} collective-permute-done((f32[1,32,256]{2,1,0:T(8,128)S(1)}, f32[1,32,256]{2,1,0:T(8,128)S(1)}, u32[]{:S(2)}, u32[]{:S(2)}) %collective-permute-start.20) | collective-permute-done | bytes 32800 | tf_op jit(solution)/shard_map/ppermute | solution.py:275
  46.4 1.1 %collective-permute-done.18 = f32[1,32,256]{2,1,0:T(8,128)S(1)} collective-permute-done((f32[1,32,256]{2,1,0:T(8,128)S(1)}, f32[1,32,256]{2,1,0:T(8,128)S(1)}, u32[]{:S(2)}, u32[]{:S(2)}) %collective-permute-start.18) | collective-permute-done | bytes 32800 | tf_op jit(solution)/shard_map/ppermute | solution.py:275
  47.7 0.9 %finish.1 = f32[128,256]{1,0:T(8,128)} custom-call(bf16[128,256]{1,0:T(8,128)(2,1)S(1)} %get-tuple-element.34.refs_0_, f32[128,256]{1,0:T(8,128)S(1)} %get-tuple-element.35.refs_1_, f32[256,256]{1,0:T(8,128)S(1)} %get-tuple-element.36.refs_0_.refs_2_, f32[256,256]{1,0:T(8,128)S(1)} %collective-permute-done.9.refs_1_.refs_3_, ...), custom_call_target="tpu_custom_call" | custom-call | flops 33554432 | bytes 655360 | tf_op jit(solution)/shard_map/finish/pallas_call | solution.py:213
  48.9 0.7 %place.1 = f32[256,256]{1,0:T(8,128)} custom-call(f32[4,32,256]{2,1,0:T(8,128)S(1)} %pad_maximum_fusion.refs_0_, f32[4,32,256]{2,1,0:T(8,128)S(1)} %collective-permute-done.21.refs_1_), custom_call_target="tpu_custom_call" | custom-call | bytes 524288 | tf_op jit(solution)/shard_map/place/pallas_call | solution.py:213
  (43 shorter events, 5.2 us)
Async XLA Ops:
  1.9 13.4 %copy-start.1 = (f32[256,256]{1,0:T(8,128)S(1)}, f32[256,256]{1,0:T(8,128)}, u32[]{:S(2)}) copy-start(f32[256,256]{1,0:T(8,128)} %refs_3_.2) | copy-start | bytes 786436
  1.9 3.1 %collective-permute-start.1 = (f32[8,16,256]{2,1,0:T(8,128)S(1)}, f32[8,16,256]{2,1,0:T(8,128)S(1)}, u32[]{:S(2)}, u32[]{:S(2)}) collective-permute-start(f32[8,16,256]{2,1,0:T(8,128)S(1)} %get-tuple-element.30), channel_id=1, source_target_pairs={{0,2},{1,3},{2,0},{3,1},{4,6},{5,7},{6,4},{7,5},{8,10},{9,11},{10,... | collective-permute-start | bytes 393224 | tf_op jit(solution)/shard_map/ppermute | solution.py:275
  2.4 9.8 %collective-permute-start = (f32[128,256]{1,0:T(8,128)S(1)}, f32[128,256]{1,0:T(8,128)S(1)}, u32[]{:S(2)}, u32[]{:S(2)}) collective-permute-start(f32[128,256]{1,0:T(8,128)S(1)} %copy-done), channel_id=1, source_target_pairs={{0,1},{1,0},{2,3},{3,2},{4,5},{5,4},{6,7},{7,6},{8,9},{9,8},{10,11... | collective-permute-start | bytes 393224 | tf_op jit(solution)/shard_map/ppermute | solution.py:237
  5.0 10.3 %copy-start.2 = (f32[128,256]{1,0:T(8,128)S(1)}, f32[128,256]{1,0:T(8,128)}, u32[]{:S(2)}) copy-start(f32[128,256]{1,0:T(8,128)} %refs_2_.2) | copy-start | bytes 393220
  5.1 9.3 %collective-permute-start.8 = (f32[2,16,256]{2,1,0:T(8,128)S(1)}, f32[2,16,256]{2,1,0:T(8,128)S(1)}, u32[]{:S(2)}, u32[]{:S(2)}) collective-permute-start(f32[2,16,256]{2,1,0:T(8,128)S(1)} %get-tuple-element.47), channel_id=1, source_target_pairs={{0,30},{1,31},{2,28},{3,29},{4,26},{5,27},{6,24},{7,25},{8,22},{9,... | collective-permute-start | bytes 98312 | tf_op jit(solution)/shard_map/ppermute | solution.py:275
  9.4 5.5 %collective-permute-start.7 = (f32[2,16,256]{2,1,0:T(8,128)S(1)}, f32[2,16,256]{2,1,0:T(8,128)S(1)}, u32[]{:S(2)}, u32[]{:S(2)}) collective-permute-start(f32[2,16,256]{2,1,0:T(8,128)S(1)} %get-tuple-element.48), channel_id=1, source_target_pairs={{0,26},{1,27},{2,24},{3,25},{4,30},{5,31},{6,28},{7,29},{8,18},{9,... | collective-permute-start | bytes 98312 | tf_op jit(solution)/shard_map/ppermute | solution.py:275
  9.6 6.7 %collective-permute-start.6 = (f32[2,16,256]{2,1,0:T(8,128)S(1)}, f32[2,16,256]{2,1,0:T(8,128)S(1)}, u32[]{:S(2)}, u32[]{:S(2)}) collective-permute-start(f32[2,16,256]{2,1,0:T(8,128)S(1)} %get-tuple-element.49), channel_id=1, source_target_pairs={{0,22},{1,23},{2,20},{3,21},{4,18},{5,19},{6,16},{7,17},{8,30},{9,... | collective-permute-start | bytes 98312 | tf_op jit(solution)/shard_map/ppermute | solution.py:275
  10.1 6.1 %collective-permute-start.5 = (f32[2,16,256]{2,1,0:T(8,128)S(1)}, f32[2,16,256]{2,1,0:T(8,128)S(1)}, u32[]{:S(2)}, u32[]{:S(2)}) collective-permute-start(f32[2,16,256]{2,1,0:T(8,128)S(1)} %get-tuple-element.50), channel_id=1, source_target_pairs={{0,18},{1,19},{2,16},{3,17},{4,22},{5,23},{6,20},{7,21},{8,26},{9,... | collective-permute-start | bytes 98312 | tf_op jit(solution)/shard_map/ppermute | solution.py:275
  12.2 5.4 %collective-permute-start.4 = (f32[2,16,256]{2,1,0:T(8,128)S(1)}, f32[2,16,256]{2,1,0:T(8,128)S(1)}, u32[]{:S(2)}, u32[]{:S(2)}) collective-permute-start(f32[2,16,256]{2,1,0:T(8,128)S(1)} %get-tuple-element.51), channel_id=1, source_target_pairs={{0,14},{1,15},{2,12},{3,13},{4,10},{5,11},{6,8},{7,9},{8,6},{9,7},... | collective-permute-start | bytes 98312 | tf_op jit(solution)/shard_map/ppermute | solution.py:275
  14.4 3.4 %collective-permute-start.3 = (f32[2,16,256]{2,1,0:T(8,128)S(1)}, f32[2,16,256]{2,1,0:T(8,128)S(1)}, u32[]{:S(2)}, u32[]{:S(2)}) collective-permute-start(f32[2,16,256]{2,1,0:T(8,128)S(1)} %get-tuple-element.52), channel_id=1, source_target_pairs={{0,10},{1,11},{2,8},{3,9},{4,14},{5,15},{6,12},{7,13},{8,2},{9,3},... | collective-permute-start | bytes 98312 | tf_op jit(solution)/shard_map/ppermute | solution.py:275
  14.9 3.3 %collective-permute-start.2 = (f32[2,16,256]{2,1,0:T(8,128)S(1)}, f32[2,16,256]{2,1,0:T(8,128)S(1)}, u32[]{:S(2)}, u32[]{:S(2)}) collective-permute-start(f32[2,16,256]{2,1,0:T(8,128)S(1)} %get-tuple-element.53), channel_id=1, source_target_pairs={{0,6},{1,7},{2,4},{3,5},{4,2},{5,3},{6,0},{7,1},{8,14},{9,15},{10,... | collective-permute-start | bytes 98312 | tf_op jit(solution)/shard_map/ppermute | solution.py:275
  19.5 1.8 %collective-permute-start.9 = (f32[256,256]{1,0:T(8,128)S(1)}, f32[256,256]{1,0:T(8,128)S(1)}, u32[]{:S(2)}, u32[]{:S(2)}) collective-permute-start(f32[256,256]{1,0:T(8,128)S(1)} %get-tuple-element.37), channel_id=1, source_target_pairs={{0,2},{1,3},{2,0},{3,1},{4,6},{5,7},{6,4},{7,5},{8,10},{9,11},{10,... | collective-permute-start | bytes 786440 | tf_op jit(solution)/shard_map/ppermute | solution.py:275
  21.2 9.9 %collective-permute-start.10 = (f32[160,256]{1,0:T(8,128)S(1)}, f32[160,256]{1,0:T(8,128)S(1)}, u32[]{:S(2)}, u32[]{:S(2)}) collective-permute-start(f32[160,256]{1,0:T(8,128)S(1)} %get-tuple-element.39), channel_id=1, source_target_pairs={{0,6},{1,7},{2,4},{3,5},{4,2},{5,3},{6,0},{7,1},{8,14},{9,15},{10,... | collective-permute-start | bytes 491528 | tf_op jit(solution)/shard_map/ppermute | solution.py:275
  21.6 9.5 %collective-permute-start.11 = (f32[160,256]{1,0:T(8,128)S(1)}, f32[160,256]{1,0:T(8,128)S(1)}, u32[]{:S(2)}, u32[]{:S(2)}) collective-permute-start(f32[160,256]{1,0:T(8,128)S(1)} %get-tuple-element.40), channel_id=1, source_target_pairs={{0,1},{1,0},{2,3},{3,2},{4,5},{5,4},{6,7},{7,6},{8,9},{9,8},{10,11... | collective-permute-start | bytes 491528 | tf_op jit(solution)/shard_map/ppermute | solution.py:275
  22.9 5.7 %collective-permute-start.12 = (f32[32,256]{1,0:T(8,128)S(1)}, f32[32,256]{1,0:T(8,128)S(1)}, u32[]{:S(2)}, u32[]{:S(2)}) collective-permute-start(f32[32,256]{1,0:T(8,128)S(1)} %get-tuple-element.41), channel_id=1, source_target_pairs={{0,24},{1,25},{2,26},{3,27},{4,28},{5,29},{6,30},{7,31},{8,16},{9,... | collective-permute-start | bytes 98312 | tf_op jit(solution)/shard_map/ppermute | solution.py:275
  26.5 4.6 %collective-permute-start.13 = (f32[32,256]{1,0:T(8,128)S(1)}, f32[32,256]{1,0:T(8,128)S(1)}, u32[]{:S(2)}, u32[]{:S(2)}) collective-permute-start(f32[32,256]{1,0:T(8,128)S(1)} %get-tuple-element.42), channel_id=1, source_target_pairs={{0,18},{1,19},{2,16},{3,17},{4,22},{5,23},{6,20},{7,21},{8,26},{9,... | collective-permute-start | bytes 98312 | tf_op jit(solution)/shard_map/ppermute | solution.py:275
  26.5 4.6 %collective-permute-start.14 = (f32[32,256]{1,0:T(8,128)S(1)}, f32[32,256]{1,0:T(8,128)S(1)}, u32[]{:S(2)}, u32[]{:S(2)}) collective-permute-start(f32[32,256]{1,0:T(8,128)S(1)} %get-tuple-element.43), channel_id=1, source_target_pairs={{0,7},{1,6},{2,5},{3,4},{4,3},{5,2},{6,1},{7,0},{8,15},{9,14},{10,... | collective-permute-start | bytes 98312 | tf_op jit(solution)/shard_map/ppermute | solution.py:275
  31.2 10.8 %collective-permute-start.17 = (f32[96,256]{1,0:T(8,128)S(1)}, f32[96,256]{1,0:T(8,128)S(1)}, u32[]{:S(2)}, u32[]{:S(2)}) collective-permute-start(f32[96,256]{1,0:T(8,128)S(1)} %get-tuple-element.46), channel_id=1, source_target_pairs={{0,10},{1,11},{2,8},{3,9},{4,14},{5,15},{6,12},{7,13},{8,2},{9,3},... | collective-permute-start | bytes 294920 | tf_op jit(solution)/shard_map/ppermute | solution.py:275
  31.3 8.6 %collective-permute-start.15 = (f32[64,256]{1,0:T(8,128)S(1)}, f32[64,256]{1,0:T(8,128)S(1)}, u32[]{:S(2)}, u32[]{:S(2)}) collective-permute-start(f32[64,256]{1,0:T(8,128)S(1)} %get-tuple-element.44), channel_id=1, source_target_pairs={{0,24},{1,25},{2,26},{3,27},{4,28},{5,29},{6,30},{7,31},{8,16},{9,... | collective-permute-start | bytes 196616 | tf_op jit(solution)/shard_map/ppermute | solution.py:275
  35.0 6.9 %collective-permute-start.16 = (f32[64,256]{1,0:T(8,128)S(1)}, f32[64,256]{1,0:T(8,128)S(1)}, u32[]{:S(2)}, u32[]{:S(2)}) collective-permute-start(f32[64,256]{1,0:T(8,128)S(1)} %get-tuple-element.45), channel_id=1, source_target_pairs={{0,18},{1,19},{2,16},{3,17},{4,22},{5,23},{6,20},{7,21},{8,26},{9,... | collective-permute-start | bytes 196616 | tf_op jit(solution)/shard_map/ppermute | solution.py:275
  42.0 4.5 %collective-permute-start.20 = (f32[1,32,256]{2,1,0:T(8,128)S(1)}, f32[1,32,256]{2,1,0:T(8,128)S(1)}, u32[]{:S(2)}, u32[]{:S(2)}) collective-permute-start(f32[1,32,256]{2,1,0:T(8,128)S(1)} %bitcast.23), channel_id=1, source_target_pairs={{0,7},{1,6},{2,5},{3,4},{4,3},{5,2},{6,1},{7,0},{8,15},{9,14},{10,... | collective-permute-start | bytes 98312 | tf_op jit(solution)/shard_map/ppermute | solution.py:275
  43.1 3.3 %collective-permute-start.19 = (f32[1,32,256]{2,1,0:T(8,128)S(1)}, f32[1,32,256]{2,1,0:T(8,128)S(1)}, u32[]{:S(2)}, u32[]{:S(2)}) collective-permute-start(f32[1,32,256]{2,1,0:T(8,128)S(1)} %bitcast.24), channel_id=1, source_target_pairs={{0,6},{1,7},{2,4},{3,5},{4,2},{5,3},{6,0},{7,1},{8,14},{9,15},{10,... | collective-permute-start | bytes 98312 | tf_op jit(solution)/shard_map/ppermute | solution.py:275
  44.0 3.5 %collective-permute-start.18 = (f32[1,32,256]{2,1,0:T(8,128)S(1)}, f32[1,32,256]{2,1,0:T(8,128)S(1)}, u32[]{:S(2)}, u32[]{:S(2)}) collective-permute-start(f32[1,32,256]{2,1,0:T(8,128)S(1)} %bitcast.25), channel_id=1, source_target_pairs={{0,3},{1,2},{2,1},{3,0},{4,7},{5,6},{6,5},{7,4},{8,11},{9,10},{10,... | collective-permute-start | bytes 98312 | tf_op jit(solution)/shard_map/ppermute | solution.py:275
  47.5 1.4 %collective-permute-start.21 = (f32[4,32,256]{2,1,0:T(8,128)S(1)}, f32[4,32,256]{2,1,0:T(8,128)S(1)}, u32[]{:S(2)}, u32[]{:S(2)}) collective-permute-start(f32[4,32,256]{2,1,0:T(8,128)S(1)} %pad_maximum_fusion.refs_0_), channel_id=1, source_target_pairs={{0,2},{1,3},{2,0},{3,1},{4,6},{5,7},{6,4},{7,5},{8,10},{9,11},{10,... | collective-permute-start | bytes 393224 | tf_op jit(solution)/shard_map/ppermute | solution.py:275
  (4 other events, 5.8 us)

commit v3 on v1

--- a/solution.py
+++ b/solution.py
@@ -102,7 +102,7 @@
 
 
 def layer_kernel(
-    order, parities, local_ref, cross_ref, weight_ref, cotangent_ref, own_ref, got_ref, *refs
+    order, parities, arrival, local_ref, cross_ref, weight_ref, cotangent_ref, own_ref, got_ref, *refs
 ):
     chips, per_peer = own_ref.shape[:2]
     arrived_refs, refs = refs[: chips - 1], refs[chips - 1 :]
@@ -111,7 +111,7 @@
     for mask in range(chips):
         for k in range(2):
             start = lax.bitwise_xor(peer, 2 * mask + (k ^ (mask > 0))) * per_peer
-            block = arrived_refs[mask - 1][k] if mask else (got_ref if k else own_ref)[0]
+            block = arrived_refs[arrival.index(mask - 1)][k] if mask else (got_ref if k else own_ref)[0]
             slots_ref[pl.ds(pl.multiple_of(start, per_peer), per_peer), :] = block
     cross = cross_ref[0], cross_ref[1]
     weight = weight_ref[0], weight_ref[1]
@@ -298,6 +298,8 @@
     got = swap(give, 1 << low)
     packed = jnp.stack([own, got], axis=1)
     arrived = [swap(packed[mask], 2 * mask + 1 << low) for mask in range(1, groups // 2)]
+    arrival = list(range(groups // 2 - 1))
+    arrival.append(arrival.pop(groups // 4 - 1))
     local, cross, tile_parts, weight_parts = kernel(
         prepare_kernel,
         "prepare",
@@ -315,11 +317,11 @@
     half = width // 2
     held = array((slots // 2 + (half if aligned else 0), width), F32)
     value, spread, keep, give, *partial = kernel(
-        functools.partial(layer_kernel, order, parities),
+        functools.partial(layer_kernel, order, parities, arrival),
         "layer",
         (array((rows, width), F32), array((2, rows, width), BF16), held, held)
         + (() if aligned else (array((width, width), F32),)),
-        (local, cross, weight_parts, cotangent, own, got, *arrived),
+        (local, cross, weight_parts, cotangent, own, got, *(arrived[i] for i in arrival)),
         scratch=(pltpu.VMEM((slots, width), F32), pltpu.VMEM((width, width), F32)),
         flops=15 * work,
         traffic=4 * (4 * rows + 2 * slots) * width,
@@ -358,6 +360,8 @@
         keeps = len(terms) if last else len(terms) >> len(bits)
         layout, riders = [], []
         partners = list(enumerate(masks(bits, straight)))[:0:-1]
+        if last:
+            partners.sort(key=lambda partner: partner[0] != 2)
         for i, mask in partners:
             pieces = list(terms) if last else terms[i * keeps : (i + 1) * keeps]
             way, across = mask >> low, mask & (core - 1)
@@ -370,11 +374,11 @@
                 pieces.append((len(arrays) - 1, 0, rows))
             layout.append(pieces)
         sent = pack("pack", layout)
-        came = []
-        for (_, mask), value, rides in zip(partners, sent, riders):
+        came = {}
+        for (i, mask), value, rides in zip(partners, sent, riders):
             arrays.append(swap(value, mask))
             number, first = len(arrays) - 1, 0
-            came.append([(number, j * share, share) for j in range(keeps)])
+            came[i] = [(number, j * share, share) for j in range(keeps)]
             first = keeps * share
             for q, come in rides:
                 way = mask >> low
@@ -384,7 +388,7 @@
                 far_pieces.append((number, first, rows))
             for q in {q for q, _ in rides}:
                 del moving[q]
-        terms = [[terms[j]] + [pieces[j] for pieces in reversed(came)] for j in range(keeps)]
+        terms = [[terms[j]] + [came[i][j] for i in sorted(came)] for j in range(keeps)]
     if blocks > 2:
         for step in range(1, blocks):
             arrays.append(shift(leaving[step - 1], step))

time: 48.1 us -> 47.7 us (level)
  starting transfers between devices: 25.3 us -> 23.9 us
  waiting for transfers between devices: 16.4 us -> 17.6 us
    ppermute x19, starting transfers between devices: 22.7 us -> 21.3 us  [swap(): lax.ppermute(value, both, [(i, i ^ mask) for i in range(devices)])]
    ppermute x19, waiting for transfers between devices: 16.4 us -> 17.6 us  [swap(): lax.ppermute(value, both, [(i, i ^ mask) for i in range(devices)])]
  transfers between devices with their start and end apart: 20 -> 20, of which waited for: 12 -> 11; matrix products, arithmetic and copies ran while one was open for 0% -> 0% of each run, Pallas kernels for 4% -> 4%
where the time goes in v3:
time: 47.7 us; the launch traced here: 47.5 us
  starting transfers between devices  23.9 us (50%)
  waiting for transfers between devices  17.6 us (37%)
  Pallas kernels  5.22 us (11%)
  between operations  0.74 us (2%)
    ppermute x19, starting transfers between devices, swap(): lax.ppermute(value, both, [(i, i ^ mask) for i in range(devices)])  21.3 us
    ppermute x19, waiting for transfers between devices, swap(): lax.ppermute(value, both, [(i, i ^ mask) for i in range(devices)])  17.6 us
    pallas_call x9, Pallas kernels, kernel(): pl.pallas_call(lambda *refs: body(*refs[:count], *refs[count + len(after)...  5.22 us
    ppermute x1, starting transfers between devices, shift(): return lax.ppermute(value, 'blk', pairs)  2.6 us
  transfers between devices with their start and end apart: 20, of which 11 were waited for; matrix products, arithmetic and copies ran while one was open for 0% of the time, Pallas kernels for 4%

profile of v3, /device:TPU:0, one launch (start us, length us, event | category | flops | bytes accessed | tf_op | source)
XLA Modules:
  0.0 47.5 jit_solution(14815829435747698405)
XLA Ops:
  0.6 1.3 %gather.1 = (f32[8,16,256]{2,1,0:T(8,128)S(1)}, f32[8,16,256]{2,1,0:T(8,128)S(1)}, bf16[128,256]{1,0:T(8,128)(2,1)S(1)}) custom-call(s32[1,16]{1,0:T(1,128)} %refs_0_.3, s32[1,256]{1,0:T(1,128)} %refs_1_.1, f32[128,256]{1,0:T(8,128)} %refs_2_.3), custom_call_target="tpu_custom_call" | custom-call | flops 16777216 | bytes 393216 | tf_op jit(solution)/shard_map/gather/pallas_call | solution.py:213
  2.4 2.6 %collective-permute-start = (f32[128,256]{1,0:T(8,128)S(1)}, f32[128,256]{1,0:T(8,128)S(1)}, u32[]{:S(2)}, u32[]{:S(2)}) collective-permute-start(f32[128,256]{1,0:T(8,128)S(1)} %copy-done), channel_id=1, source_target_pairs={{0,1},{1,0},{2,3},{3,2},{4,5},{5,4},{6,7},{7,6},{8,9},{9,8},{10,11... | collective-permute-start | bytes 393224 | tf_op jit(solution)/shard_map/ppermute | solution.py:237
  5.1 2.4 %collective-permute-start.8 = (f32[2,16,256]{2,1,0:T(8,128)S(1)}, f32[2,16,256]{2,1,0:T(8,128)S(1)}, u32[]{:S(2)}, u32[]{:S(2)}) collective-permute-start(f32[2,16,256]{2,1,0:T(8,128)S(1)} %get-tuple-element.43), channel_id=1, source_target_pairs={{0,18},{1,19},{2,16},{3,17},{4,22},{5,23},{6,20},{7,21},{8,26},{9,... | collective-permute-start | bytes 98312 | tf_op jit(solution)/shard_map/ppermute | solution.py:275
  7.5 2.2 %collective-permute-start.7 = (f32[2,16,256]{2,1,0:T(8,128)S(1)}, f32[2,16,256]{2,1,0:T(8,128)S(1)}, u32[]{:S(2)}, u32[]{:S(2)}) collective-permute-start(f32[2,16,256]{2,1,0:T(8,128)S(1)} %get-tuple-element.44), channel_id=1, source_target_pairs={{0,30},{1,31},{2,28},{3,29},{4,26},{5,27},{6,24},{7,25},{8,22},{9,... | collective-permute-start | bytes 98312 | tf_op jit(solution)/shard_map/ppermute | solution.py:275
  9.7 2.2 %collective-permute-start.6 = (f32[2,16,256]{2,1,0:T(8,128)S(1)}, f32[2,16,256]{2,1,0:T(8,128)S(1)}, u32[]{:S(2)}, u32[]{:S(2)}) collective-permute-start(f32[2,16,256]{2,1,0:T(8,128)S(1)} %get-tuple-element.45), channel_id=1, source_target_pairs={{0,26},{1,27},{2,24},{3,25},{4,30},{5,31},{6,28},{7,29},{8,18},{9,... | collective-permute-start | bytes 98312 | tf_op jit(solution)/shard_map/ppermute | solution.py:275
  12.0 2.5 %collective-permute-start.4 = (f32[2,16,256]{2,1,0:T(8,128)S(1)}, f32[2,16,256]{2,1,0:T(8,128)S(1)}, u32[]{:S(2)}, u32[]{:S(2)}) collective-permute-start(f32[2,16,256]{2,1,0:T(8,128)S(1)} %get-tuple-element.47), channel_id=1, source_target_pairs={{0,14},{1,15},{2,12},{3,13},{4,10},{5,11},{6,8},{7,9},{8,6},{9,7},... | collective-permute-start | bytes 98312 | tf_op jit(solution)/shard_map/ppermute | solution.py:275
  14.5 0.6 %collective-permute-start.2 = (f32[2,16,256]{2,1,0:T(8,128)S(1)}, f32[2,16,256]{2,1,0:T(8,128)S(1)}, u32[]{:S(2)}, u32[]{:S(2)}) collective-permute-start(f32[2,16,256]{2,1,0:T(8,128)S(1)} %get-tuple-element.49), channel_id=1, source_target_pairs={{0,6},{1,7},{2,4},{3,5},{4,2},{5,3},{6,0},{7,1},{8,14},{9,15},{10,... | collective-permute-start | bytes 98312 | tf_op jit(solution)/shard_map/ppermute | solution.py:275
  15.5 1.7 %collective-permute-done.5.refs_9_ = f32[2,16,256]{2,1,0:T(8,128)S(1)} collective-permute-done((f32[2,16,256]{2,1,0:T(8,128)S(1)}, f32[2,16,256]{2,1,0:T(8,128)S(1)}, u32[]{:S(2)}, u32[]{:S(2)}) %collective-permute-start.5) | collective-permute-done | bytes 32800 | tf_op jit(solution)/shard_map/ppermute | solution.py:275
  17.2 0.6 %collective-permute-done.3.refs_7_ = f32[2,16,256]{2,1,0:T(8,128)S(1)} collective-permute-done((f32[2,16,256]{2,1,0:T(8,128)S(1)}, f32[2,16,256]{2,1,0:T(8,128)S(1)}, u32[]{:S(2)}, u32[]{:S(2)}) %collective-permute-start.3) | collective-permute-done | bytes 32800 | tf_op jit(solution)/shard_map/ppermute | solution.py:275
  18.0 1.2 %layer.1 = (f32[128,256]{1,0:T(8,128)S(1)}, bf16[2,128,256]{2,1,0:T(8,128)(2,1)S(1)}, f32[256,256]{1,0:T(8,128)S(1)}, f32[256,256]{1,0:T(8,128)S(1)}) custom-call(f32[128,256]{1,0:T(8,128)S(1)} %get-tuple-element.24.refs_0_, bf16[2,128,256]{2,1,0:T(8,128)(2,1)S(1)} %get-tuple-element.25.refs_1_, bf16[2,256,256]{2,1,0:T(8,128)(2,1)S(1)} %get-tuple-element.26.refs_2_, ...), custom_call_target="tpu_custom_call" | custom-call | flops 251658240 | bytes 1048576 | tf_op jit(solution)/shard_map/layer/pallas_call | solution.py:213
  19.6 0.8 %inner.1 = (f32[128,256]{1,0:T(8,128)S(1)}, f32[1,128,256]{2,1,0:T(8,128)S(1)}, f32[128,256]{1,0:T(8,128)}) custom-call(bf16[2,2,128,128]{3,2,1,0:T(8,128)(2,1)S(1)} %get-tuple-element.23.refs_0_, bf16[2,128,256]{2,1,0:T(8,128)(2,1)S(1)} %get-tuple-element.29.refs_1_, f32[128,256]{1,0:T(8,128)S(1)} %get-tuple-element.30.refs_2_), custom_call_target="tpu_custom_call" | custom-call | flops 50331648 | bytes 786432 | tf_op jit(solution)/shard_map/inner/pallas_call | solution.py:213
  21.4 1.3 %collective-permute-start.11 = (f32[160,256]{1,0:T(8,128)S(1)}, f32[160,256]{1,0:T(8,128)S(1)}, u32[]{:S(2)}, u32[]{:S(2)}) collective-permute-start(f32[160,256]{1,0:T(8,128)S(1)} %get-tuple-element.38), channel_id=1, source_target_pairs={{0,1},{1,0},{2,3},{3,2},{4,5},{5,4},{6,7},{7,6},{8,9},{9,8},{10,11... | collective-permute-start | bytes 491528 | tf_op jit(solution)/shard_map/ppermute | solution.py:275
  22.7 1.1 %collective-permute-start.12 = (f32[32,256]{1,0:T(8,128)S(1)}, f32[32,256]{1,0:T(8,128)S(1)}, u32[]{:S(2)}, u32[]{:S(2)}) collective-permute-start(f32[32,256]{1,0:T(8,128)S(1)} %get-tuple-element.39), channel_id=1, source_target_pairs={{0,7},{1,6},{2,5},{3,4},{4,3},{5,2},{6,1},{7,0},{8,15},{9,14},{10,... | collective-permute-start | bytes 98312 | tf_op jit(solution)/shard_map/ppermute | solution.py:275
  23.8 4.6 %collective-permute-done.12.refs_2_ = f32[32,256]{1,0:T(8,128)S(1)} collective-permute-done((f32[32,256]{1,0:T(8,128)S(1)}, f32[32,256]{1,0:T(8,128)S(1)}, u32[]{:S(2)}, u32[]{:S(2)}) %collective-permute-start.12) | collective-permute-done | bytes 32800 | tf_op jit(solution)/shard_map/ppermute | solution.py:275
  28.4 2.8 %collective-permute-start.13 = (f32[96,256]{1,0:T(8,128)S(1)}, f32[96,256]{1,0:T(8,128)S(1)}, u32[]{:S(2)}, u32[]{:S(2)}) collective-permute-start(f32[96,256]{1,0:T(8,128)S(1)} %get-tuple-element.40), channel_id=1, source_target_pairs={{0,18},{1,19},{2,16},{3,17},{4,22},{5,23},{6,20},{7,21},{8,26},{9,... | collective-permute-start | bytes 294920 | tf_op jit(solution)/shard_map/ppermute | solution.py:275
  31.2 1.4 %collective-permute-start.14 = (f32[96,256]{1,0:T(8,128)S(1)}, f32[96,256]{1,0:T(8,128)S(1)}, u32[]{:S(2)}, u32[]{:S(2)}) collective-permute-start(f32[96,256]{1,0:T(8,128)S(1)} %get-tuple-element.41), channel_id=1, source_target_pairs={{0,24},{1,25},{2,26},{3,27},{4,28},{5,29},{6,30},{7,31},{8,16},{9,... | collective-permute-start | bytes 294920 | tf_op jit(solution)/shard_map/ppermute | solution.py:275
  32.6 5.6 %collective-permute-done.13.refs_6_.refs_5_ = f32[96,256]{1,0:T(8,128)S(1)} collective-permute-done((f32[96,256]{1,0:T(8,128)S(1)}, f32[96,256]{1,0:T(8,128)S(1)}, u32[]{:S(2)}, u32[]{:S(2)}) %collective-permute-start.13) | collective-permute-done | bytes 98336 | tf_op jit(solution)/shard_map/ppermute | solution.py:275
  38.6 1.5 %collective-permute-done.15.refs_8_.refs_7_ = f32[96,256]{1,0:T(8,128)S(1)} collective-permute-done((f32[96,256]{1,0:T(8,128)S(1)}, f32[96,256]{1,0:T(8,128)S(1)}, u32[]{:S(2)}, u32[]{:S(2)}) %collective-permute-start.15) | collective-permute-done | bytes 98336 | tf_op jit(solution)/shard_map/ppermute | solution.py:275
  40.1 1.6 %collective-permute-start.18 = (f32[1,32,256]{2,1,0:T(8,128)S(1)}, f32[1,32,256]{2,1,0:T(8,128)S(1)}, u32[]{:S(2)}, u32[]{:S(2)}) collective-permute-start(f32[1,32,256]{2,1,0:T(8,128)S(1)} %bitcast.23), channel_id=1, source_target_pairs={{0,7},{1,6},{2,5},{3,4},{4,3},{5,2},{6,1},{7,0},{8,15},{9,14},{10,... | collective-permute-start | bytes 98312 | tf_op jit(solution)/shard_map/ppermute | solution.py:275
  41.7 1.4 %collective-permute-start.16 = (f32[1,32,256]{2,1,0:T(8,128)S(1)}, f32[1,32,256]{2,1,0:T(8,128)S(1)}, u32[]{:S(2)}, u32[]{:S(2)}) collective-permute-start(f32[1,32,256]{2,1,0:T(8,128)S(1)} %bitcast.25), channel_id=1, source_target_pairs={{0,3},{1,2},{2,1},{3,0},{4,7},{5,6},{6,5},{7,4},{8,11},{9,10},{10,... | collective-permute-start | bytes 98312 | tf_op jit(solution)/shard_map/ppermute | solution.py:275
  43.1 1.3 %collective-permute-done.18 = f32[1,32,256]{2,1,0:T(8,128)S(1)} collective-permute-done((f32[1,32,256]{2,1,0:T(8,128)S(1)}, f32[1,32,256]{2,1,0:T(8,128)S(1)}, u32[]{:S(2)}, u32[]{:S(2)}) %collective-permute-start.18) | collective-permute-done | bytes 32800 | tf_op jit(solution)/shard_map/ppermute | solution.py:275
  44.4 0.9 %collective-permute-done.17 = f32[1,32,256]{2,1,0:T(8,128)S(1)} collective-permute-done((f32[1,32,256]{2,1,0:T(8,128)S(1)}, f32[1,32,256]{2,1,0:T(8,128)S(1)}, u32[]{:S(2)}, u32[]{:S(2)}) %collective-permute-start.17) | collective-permute-done | bytes 32800 | tf_op jit(solution)/shard_map/ppermute | solution.py:275
  45.5 0.9 %finish.1 = f32[128,256]{1,0:T(8,128)} custom-call(bf16[128,256]{1,0:T(8,128)(2,1)S(1)} %get-tuple-element.32.refs_0_, f32[128,256]{1,0:T(8,128)S(1)} %get-tuple-element.33.refs_1_, f32[256,256]{1,0:T(8,128)S(1)} %get-tuple-element.34.refs_0_.refs_2_, f32[256,256]{1,0:T(8,128)S(1)} %collective-permute-done.9.refs_1_.refs_3_, ...), custom_call_target="tpu_custom_call" | custom-call | flops 33554432 | bytes 655360 | tf_op jit(solution)/shard_map/finish/pallas_call | solution.py:213
  46.8 0.7 %place.1 = f32[256,256]{1,0:T(8,128)} custom-call(f32[4,32,256]{2,1,0:T(8,128)S(1)} %pad_maximum_fusion.refs_0_, f32[4,32,256]{2,1,0:T(8,128)S(1)} %collective-permute-done.19.refs_1_), custom_call_target="tpu_custom_call" | custom-call | bytes 524288 | tf_op jit(solution)/shard_map/place/pallas_call | solution.py:213
  (39 shorter events, 3.5 us)
Async XLA Ops:
  0.6 1.8 %copy-start = (f32[128,256]{1,0:T(8,128)S(1)}, f32[128,256]{1,0:T(8,128)}, u32[]{:S(2)}) copy-start(f32[128,256]{1,0:T(8,128)} %refs_2_.3) | copy-start | bytes 393220
  1.9 13.3 %copy-start.1 = (f32[256,256]{1,0:T(8,128)S(1)}, f32[256,256]{1,0:T(8,128)}, u32[]{:S(2)}) copy-start(f32[256,256]{1,0:T(8,128)} %refs_3_.2) | copy-start | bytes 786436
  1.9 3.1 %collective-permute-start.1 = (f32[8,16,256]{2,1,0:T(8,128)S(1)}, f32[8,16,256]{2,1,0:T(8,128)S(1)}, u32[]{:S(2)}, u32[]{:S(2)}) collective-permute-start(f32[8,16,256]{2,1,0:T(8,128)S(1)} %get-tuple-element.28), channel_id=1, source_target_pairs={{0,2},{1,3},{2,0},{3,1},{4,6},{5,7},{6,4},{7,5},{8,10},{9,11},{10,... | collective-permute-start | bytes 393224 | tf_op jit(solution)/shard_map/ppermute | solution.py:275
  2.4 9.5 %collective-permute-start = (f32[128,256]{1,0:T(8,128)S(1)}, f32[128,256]{1,0:T(8,128)S(1)}, u32[]{:S(2)}, u32[]{:S(2)}) collective-permute-start(f32[128,256]{1,0:T(8,128)S(1)} %copy-done), channel_id=1, source_target_pairs={{0,1},{1,0},{2,3},{3,2},{4,5},{5,4},{6,7},{7,6},{8,9},{9,8},{10,11... | collective-permute-start | bytes 393224 | tf_op jit(solution)/shard_map/ppermute | solution.py:237
  5.0 10.1 %copy-start.2 = (f32[128,256]{1,0:T(8,128)S(1)}, f32[128,256]{1,0:T(8,128)}, u32[]{:S(2)}) copy-start(f32[128,256]{1,0:T(8,128)} %refs_2_.2) | copy-start | bytes 393220
  5.1 9.4 %collective-permute-start.8 = (f32[2,16,256]{2,1,0:T(8,128)S(1)}, f32[2,16,256]{2,1,0:T(8,128)S(1)}, u32[]{:S(2)}, u32[]{:S(2)}) collective-permute-start(f32[2,16,256]{2,1,0:T(8,128)S(1)} %get-tuple-element.43), channel_id=1, source_target_pairs={{0,18},{1,19},{2,16},{3,17},{4,22},{5,23},{6,20},{7,21},{8,26},{9,... | collective-permute-start | bytes 98312 | tf_op jit(solution)/shard_map/ppermute | solution.py:275
  7.5 7.0 %collective-permute-start.7 = (f32[2,16,256]{2,1,0:T(8,128)S(1)}, f32[2,16,256]{2,1,0:T(8,128)S(1)}, u32[]{:S(2)}, u32[]{:S(2)}) collective-permute-start(f32[2,16,256]{2,1,0:T(8,128)S(1)} %get-tuple-element.44), channel_id=1, source_target_pairs={{0,30},{1,31},{2,28},{3,29},{4,26},{5,27},{6,24},{7,25},{8,22},{9,... | collective-permute-start | bytes 98312 | tf_op jit(solution)/shard_map/ppermute | solution.py:275
  9.7 5.8 %collective-permute-start.6 = (f32[2,16,256]{2,1,0:T(8,128)S(1)}, f32[2,16,256]{2,1,0:T(8,128)S(1)}, u32[]{:S(2)}, u32[]{:S(2)}) collective-permute-start(f32[2,16,256]{2,1,0:T(8,128)S(1)} %get-tuple-element.45), channel_id=1, source_target_pairs={{0,26},{1,27},{2,24},{3,25},{4,30},{5,31},{6,28},{7,29},{8,18},{9,... | collective-permute-start | bytes 98312 | tf_op jit(solution)/shard_map/ppermute | solution.py:275
  12.0 5.2 %collective-permute-start.5 = (f32[2,16,256]{2,1,0:T(8,128)S(1)}, f32[2,16,256]{2,1,0:T(8,128)S(1)}, u32[]{:S(2)}, u32[]{:S(2)}) collective-permute-start(f32[2,16,256]{2,1,0:T(8,128)S(1)} %get-tuple-element.46), channel_id=1, source_target_pairs={{0,22},{1,23},{2,20},{3,21},{4,18},{5,19},{6,16},{7,17},{8,30},{9,... | collective-permute-start | bytes 98312 | tf_op jit(solution)/shard_map/ppermute | solution.py:275
  12.0 5.2 %collective-permute-start.4 = (f32[2,16,256]{2,1,0:T(8,128)S(1)}, f32[2,16,256]{2,1,0:T(8,128)S(1)}, u32[]{:S(2)}, u32[]{:S(2)}) collective-permute-start(f32[2,16,256]{2,1,0:T(8,128)S(1)} %get-tuple-element.47), channel_id=1, source_target_pairs={{0,14},{1,15},{2,12},{3,13},{4,10},{5,11},{6,8},{7,9},{8,6},{9,7},... | collective-permute-start | bytes 98312 | tf_op jit(solution)/shard_map/ppermute | solution.py:275
  14.5 3.3 %collective-permute-start.3 = (f32[2,16,256]{2,1,0:T(8,128)S(1)}, f32[2,16,256]{2,1,0:T(8,128)S(1)}, u32[]{:S(2)}, u32[]{:S(2)}) collective-permute-start(f32[2,16,256]{2,1,0:T(8,128)S(1)} %get-tuple-element.48), channel_id=1, source_target_pairs={{0,10},{1,11},{2,8},{3,9},{4,14},{5,15},{6,12},{7,13},{8,2},{9,3},... | collective-permute-start | bytes 98312 | tf_op jit(solution)/shard_map/ppermute | solution.py:275
  14.5 3.5 %collective-permute-start.2 = (f32[2,16,256]{2,1,0:T(8,128)S(1)}, f32[2,16,256]{2,1,0:T(8,128)S(1)}, u32[]{:S(2)}, u32[]{:S(2)}) collective-permute-start(f32[2,16,256]{2,1,0:T(8,128)S(1)} %get-tuple-element.49), channel_id=1, source_target_pairs={{0,6},{1,7},{2,4},{3,5},{4,2},{5,3},{6,0},{7,1},{8,14},{9,15},{10,... | collective-permute-start | bytes 98312 | tf_op jit(solution)/shard_map/ppermute | solution.py:275
  15.2 2.8 %copy-start.3 = (f32[128,256]{1,0:T(8,128)S(1)}, f32[128,256]{1,0:T(8,128)}, u32[]{:S(2)}) copy-start(f32[128,256]{1,0:T(8,128)} %refs_3_.3) | copy-start | bytes 393220
  19.2 1.6 %collective-permute-start.9 = (f32[256,256]{1,0:T(8,128)S(1)}, f32[256,256]{1,0:T(8,128)S(1)}, u32[]{:S(2)}, u32[]{:S(2)}) collective-permute-start(f32[256,256]{1,0:T(8,128)S(1)} %get-tuple-element.35), channel_id=1, source_target_pairs={{0,2},{1,3},{2,0},{3,1},{4,6},{5,7},{6,4},{7,5},{8,10},{9,11},{10,... | collective-permute-start | bytes 786440 | tf_op jit(solution)/shard_map/ppermute | solution.py:275
  20.8 7.6 %collective-permute-start.10 = (f32[160,256]{1,0:T(8,128)S(1)}, f32[160,256]{1,0:T(8,128)S(1)}, u32[]{:S(2)}, u32[]{:S(2)}) collective-permute-start(f32[160,256]{1,0:T(8,128)S(1)} %get-tuple-element.37), channel_id=1, source_target_pairs={{0,6},{1,7},{2,4},{3,5},{4,2},{5,3},{6,0},{7,1},{8,14},{9,15},{10,... | collective-permute-start | bytes 491528 | tf_op jit(solution)/shard_map/ppermute | solution.py:275
  21.4 7.0 %collective-permute-start.11 = (f32[160,256]{1,0:T(8,128)S(1)}, f32[160,256]{1,0:T(8,128)S(1)}, u32[]{:S(2)}, u32[]{:S(2)}) collective-permute-start(f32[160,256]{1,0:T(8,128)S(1)} %get-tuple-element.38), channel_id=1, source_target_pairs={{0,1},{1,0},{2,3},{3,2},{4,5},{5,4},{6,7},{7,6},{8,9},{9,8},{10,11... | collective-permute-start | bytes 491528 | tf_op jit(solution)/shard_map/ppermute | solution.py:275
  22.7 5.7 %collective-permute-start.12 = (f32[32,256]{1,0:T(8,128)S(1)}, f32[32,256]{1,0:T(8,128)S(1)}, u32[]{:S(2)}, u32[]{:S(2)}) collective-permute-start(f32[32,256]{1,0:T(8,128)S(1)} %get-tuple-element.39), channel_id=1, source_target_pairs={{0,7},{1,6},{2,5},{3,4},{4,3},{5,2},{6,1},{7,0},{8,15},{9,14},{10,... | collective-permute-start | bytes 98312 | tf_op jit(solution)/shard_map/ppermute | solution.py:275
  28.4 9.7 %collective-permute-start.13 = (f32[96,256]{1,0:T(8,128)S(1)}, f32[96,256]{1,0:T(8,128)S(1)}, u32[]{:S(2)}, u32[]{:S(2)}) collective-permute-start(f32[96,256]{1,0:T(8,128)S(1)} %get-tuple-element.40), channel_id=1, source_target_pairs={{0,18},{1,19},{2,16},{3,17},{4,22},{5,23},{6,20},{7,21},{8,26},{9,... | collective-permute-start | bytes 294920 | tf_op jit(solution)/shard_map/ppermute | solution.py:275
  31.2 7.4 %collective-permute-start.14 = (f32[96,256]{1,0:T(8,128)S(1)}, f32[96,256]{1,0:T(8,128)S(1)}, u32[]{:S(2)}, u32[]{:S(2)}) collective-permute-start(f32[96,256]{1,0:T(8,128)S(1)} %get-tuple-element.41), channel_id=1, source_target_pairs={{0,24},{1,25},{2,26},{3,27},{4,28},{5,29},{6,30},{7,31},{8,16},{9,... | collective-permute-start | bytes 294920 | tf_op jit(solution)/shard_map/ppermute | solution.py:275
  32.6 7.5 %collective-permute-start.15 = (f32[96,256]{1,0:T(8,128)S(1)}, f32[96,256]{1,0:T(8,128)S(1)}, u32[]{:S(2)}, u32[]{:S(2)}) collective-permute-start(f32[96,256]{1,0:T(8,128)S(1)} %get-tuple-element.42), channel_id=1, source_target_pairs={{0,10},{1,11},{2,8},{3,9},{4,14},{5,15},{6,12},{7,13},{8,2},{9,3},... | collective-permute-start | bytes 294920 | tf_op jit(solution)/shard_map/ppermute | solution.py:275
  40.1 4.3 %collective-permute-start.18 = (f32[1,32,256]{2,1,0:T(8,128)S(1)}, f32[1,32,256]{2,1,0:T(8,128)S(1)}, u32[]{:S(2)}, u32[]{:S(2)}) collective-permute-start(f32[1,32,256]{2,1,0:T(8,128)S(1)} %bitcast.23), channel_id=1, source_target_pairs={{0,7},{1,6},{2,5},{3,4},{4,3},{5,2},{6,1},{7,0},{8,15},{9,14},{10,... | collective-permute-start | bytes 98312 | tf_op jit(solution)/shard_map/ppermute | solution.py:275
  41.7 3.7 %collective-permute-start.17 = (f32[1,32,256]{2,1,0:T(8,128)S(1)}, f32[1,32,256]{2,1,0:T(8,128)S(1)}, u32[]{:S(2)}, u32[]{:S(2)}) collective-permute-start(f32[1,32,256]{2,1,0:T(8,128)S(1)} %bitcast.24), channel_id=1, source_target_pairs={{0,6},{1,7},{2,4},{3,5},{4,2},{5,3},{6,0},{7,1},{8,14},{9,15},{10,... | collective-permute-start | bytes 98312 | tf_op jit(solution)/shard_map/ppermute | solution.py:275
  41.7 3.7 %collective-permute-start.16 = (f32[1,32,256]{2,1,0:T(8,128)S(1)}, f32[1,32,256]{2,1,0:T(8,128)S(1)}, u32[]{:S(2)}, u32[]{:S(2)}) collective-permute-start(f32[1,32,256]{2,1,0:T(8,128)S(1)} %bitcast.25), channel_id=1, source_target_pairs={{0,3},{1,2},{2,1},{3,0},{4,7},{5,6},{6,5},{7,4},{8,11},{9,10},{10,... | collective-permute-start | bytes 98312 | tf_op jit(solution)/shard_map/ppermute | solution.py:275
  45.4 1.4 %collective-permute-start.19 = (f32[4,32,256]{2,1,0:T(8,128)S(1)}, f32[4,32,256]{2,1,0:T(8,128)S(1)}, u32[]{:S(2)}, u32[]{:S(2)}) collective-permute-start(f32[4,32,256]{2,1,0:T(8,128)S(1)} %pad_maximum_fusion.refs_0_), channel_id=1, source_target_pairs={{0,2},{1,3},{2,0},{3,1},{4,6},{5,7},{6,4},{7,5},{8,10},{9,11},{10,... | collective-permute-start | bytes 393224 | tf_op jit(solution)/shard_map/ppermute | solution.py:275
  (2 other events, 1.4 us)

commit v4 on v3

--- a/solution.py
+++ b/solution.py
@@ -361,7 +361,7 @@
         layout, riders = [], []
         partners = list(enumerate(masks(bits, straight)))[:0:-1]
         if last:
-            partners.sort(key=lambda partner: partner[0] != 2)
+            partners.sort(key=lambda partner: (2, 1, 3).index(partner[0]))
         for i, mask in partners:
             pieces = list(terms) if last else terms[i * keeps : (i + 1) * keeps]
             way, across = mask >> low, mask & (core - 1)

time: 47.7 us -> 48.3 us (1.013)
  waiting for transfers between devices: 17.6 us -> 18.5 us
    ppermute x19, waiting for transfers between devices: 17.6 us -> 18.4 us  [swap(): lax.ppermute(value, both, [(i, i ^ mask) for i in range(devices)])]
where the time goes in v4:
time: 48.3 us; the launch traced here: 48.1 us
  starting transfers between devices  23.7 us (49%)
  waiting for transfers between devices  18.5 us (38%)
  Pallas kernels  5.22 us (11%)
  between operations  0.74 us (2%)
    ppermute x19, starting transfers between devices, swap(): lax.ppermute(value, both, [(i, i ^ mask) for i in range(devices)])  21.1 us
    ppermute x19, waiting for transfers between devices, swap(): lax.ppermute(value, both, [(i, i ^ mask) for i in range(devices)])  18.4 us
    pallas_call x9, Pallas kernels, kernel(): pl.pallas_call(lambda *refs: body(*refs[:count], *refs[count + len(after)...  5.22 us
    ppermute x1, starting transfers between devices, shift(): return lax.ppermute(value, 'blk', pairs)  2.6 us
  transfers between devices with their start and end apart: 20, of which 11 were waited for; matrix products, arithmetic and copies ran while one was open for 0% of the time, Pallas kernels for 4%

profile of v4, /device:TPU:0, one launch (start us, length us, event | category | flops | bytes accessed | tf_op | source)
XLA Modules:
  0.0 48.1 jit_solution(16933225450349768636)
XLA Ops:
  0.6 1.3 %gather.1 = (f32[8,16,256]{2,1,0:T(8,128)S(1)}, f32[8,16,256]{2,1,0:T(8,128)S(1)}, bf16[128,256]{1,0:T(8,128)(2,1)S(1)}) custom-call(s32[1,16]{1,0:T(1,128)} %refs_0_.3, s32[1,256]{1,0:T(1,128)} %refs_1_.1, f32[128,256]{1,0:T(8,128)} %refs_2_.3), custom_call_target="tpu_custom_call" | custom-call | flops 16777216 | bytes 393216 | tf_op jit(solution)/shard_map/gather/pallas_call | solution.py:213
  2.4 2.6 %collective-permute-start = (f32[128,256]{1,0:T(8,128)S(1)}, f32[128,256]{1,0:T(8,128)S(1)}, u32[]{:S(2)}, u32[]{:S(2)}) collective-permute-start(f32[128,256]{1,0:T(8,128)S(1)} %copy-done), channel_id=1, source_target_pairs={{0,1},{1,0},{2,3},{3,2},{4,5},{5,4},{6,7},{7,6},{8,9},{9,8},{10,11... | collective-permute-start | bytes 393224 | tf_op jit(solution)/shard_map/ppermute | solution.py:237
  5.1 2.4 %collective-permute-start.8 = (f32[2,16,256]{2,1,0:T(8,128)S(1)}, f32[2,16,256]{2,1,0:T(8,128)S(1)}, u32[]{:S(2)}, u32[]{:S(2)}) collective-permute-start(f32[2,16,256]{2,1,0:T(8,128)S(1)} %get-tuple-element.43), channel_id=1, source_target_pairs={{0,18},{1,19},{2,16},{3,17},{4,22},{5,23},{6,20},{7,21},{8,26},{9,... | collective-permute-start | bytes 98312 | tf_op jit(solution)/shard_map/ppermute | solution.py:275
  7.5 2.2 %collective-permute-start.7 = (f32[2,16,256]{2,1,0:T(8,128)S(1)}, f32[2,16,256]{2,1,0:T(8,128)S(1)}, u32[]{:S(2)}, u32[]{:S(2)}) collective-permute-start(f32[2,16,256]{2,1,0:T(8,128)S(1)} %get-tuple-element.44), channel_id=1, source_target_pairs={{0,30},{1,31},{2,28},{3,29},{4,26},{5,27},{6,24},{7,25},{8,22},{9,... | collective-permute-start | bytes 98312 | tf_op jit(solution)/shard_map/ppermute | solution.py:275
  9.7 2.2 %collective-permute-start.6 = (f32[2,16,256]{2,1,0:T(8,128)S(1)}, f32[2,16,256]{2,1,0:T(8,128)S(1)}, u32[]{:S(2)}, u32[]{:S(2)}) collective-permute-start(f32[2,16,256]{2,1,0:T(8,128)S(1)} %get-tuple-element.45), channel_id=1, source_target_pairs={{0,26},{1,27},{2,24},{3,25},{4,30},{5,31},{6,28},{7,29},{8,18},{9,... | collective-permute-start | bytes 98312 | tf_op jit(solution)/shard_map/ppermute | solution.py:275
  12.0 2.5 %collective-permute-start.4 = (f32[2,16,256]{2,1,0:T(8,128)S(1)}, f32[2,16,256]{2,1,0:T(8,128)S(1)}, u32[]{:S(2)}, u32[]{:S(2)}) collective-permute-start(f32[2,16,256]{2,1,0:T(8,128)S(1)} %get-tuple-element.47), channel_id=1, source_target_pairs={{0,14},{1,15},{2,12},{3,13},{4,10},{5,11},{6,8},{7,9},{8,6},{9,7},... | collective-permute-start | bytes 98312 | tf_op jit(solution)/shard_map/ppermute | solution.py:275
  14.5 0.6 %collective-permute-start.2 = (f32[2,16,256]{2,1,0:T(8,128)S(1)}, f32[2,16,256]{2,1,0:T(8,128)S(1)}, u32[]{:S(2)}, u32[]{:S(2)}) collective-permute-start(f32[2,16,256]{2,1,0:T(8,128)S(1)} %get-tuple-element.49), channel_id=1, source_target_pairs={{0,6},{1,7},{2,4},{3,5},{4,2},{5,3},{6,0},{7,1},{8,14},{9,15},{10,... | collective-permute-start | bytes 98312 | tf_op jit(solution)/shard_map/ppermute | solution.py:275
  15.5 1.7 %collective-permute-done.5.refs_9_ = f32[2,16,256]{2,1,0:T(8,128)S(1)} collective-permute-done((f32[2,16,256]{2,1,0:T(8,128)S(1)}, f32[2,16,256]{2,1,0:T(8,128)S(1)}, u32[]{:S(2)}, u32[]{:S(2)}) %collective-permute-start.5) | collective-permute-done | bytes 32800 | tf_op jit(solution)/shard_map/ppermute | solution.py:275
  17.2 0.6 %collective-permute-done.3.refs_7_ = f32[2,16,256]{2,1,0:T(8,128)S(1)} collective-permute-done((f32[2,16,256]{2,1,0:T(8,128)S(1)}, f32[2,16,256]{2,1,0:T(8,128)S(1)}, u32[]{:S(2)}, u32[]{:S(2)}) %collective-permute-start.3) | collective-permute-done | bytes 32800 | tf_op jit(solution)/shard_map/ppermute | solution.py:275
  18.0 1.2 %layer.1 = (f32[128,256]{1,0:T(8,128)S(1)}, bf16[2,128,256]{2,1,0:T(8,128)(2,1)S(1)}, f32[256,256]{1,0:T(8,128)S(1)}, f32[256,256]{1,0:T(8,128)S(1)}) custom-call(f32[128,256]{1,0:T(8,128)S(1)} %get-tuple-element.24.refs_0_, bf16[2,128,256]{2,1,0:T(8,128)(2,1)S(1)} %get-tuple-element.25.refs_1_, bf16[2,256,256]{2,1,0:T(8,128)(2,1)S(1)} %get-tuple-element.26.refs_2_, ...), custom_call_target="tpu_custom_call" | custom-call | flops 251658240 | bytes 1048576 | tf_op jit(solution)/shard_map/layer/pallas_call | solution.py:213
  19.6 0.8 %inner.1 = (f32[128,256]{1,0:T(8,128)S(1)}, f32[1,128,256]{2,1,0:T(8,128)S(1)}, f32[128,256]{1,0:T(8,128)}) custom-call(bf16[2,2,128,128]{3,2,1,0:T(8,128)(2,1)S(1)} %get-tuple-element.23.refs_0_, bf16[2,128,256]{2,1,0:T(8,128)(2,1)S(1)} %get-tuple-element.29.refs_1_, f32[128,256]{1,0:T(8,128)S(1)} %get-tuple-element.30.refs_2_), custom_call_target="tpu_custom_call" | custom-call | flops 50331648 | bytes 786432 | tf_op jit(solution)/shard_map/inner/pallas_call | solution.py:213
  21.4 1.3 %collective-permute-start.11 = (f32[160,256]{1,0:T(8,128)S(1)}, f32[160,256]{1,0:T(8,128)S(1)}, u32[]{:S(2)}, u32[]{:S(2)}) collective-permute-start(f32[160,256]{1,0:T(8,128)S(1)} %get-tuple-element.38), channel_id=1, source_target_pairs={{0,1},{1,0},{2,3},{3,2},{4,5},{5,4},{6,7},{7,6},{8,9},{9,8},{10,11... | collective-permute-start | bytes 491528 | tf_op jit(solution)/shard_map/ppermute | solution.py:275
  22.7 1.1 %collective-permute-start.12 = (f32[32,256]{1,0:T(8,128)S(1)}, f32[32,256]{1,0:T(8,128)S(1)}, u32[]{:S(2)}, u32[]{:S(2)}) collective-permute-start(f32[32,256]{1,0:T(8,128)S(1)} %get-tuple-element.39), channel_id=1, source_target_pairs={{0,7},{1,6},{2,5},{3,4},{4,3},{5,2},{6,1},{7,0},{8,15},{9,14},{10,... | collective-permute-start | bytes 98312 | tf_op jit(solution)/shard_map/ppermute | solution.py:275
  23.8 4.6 %collective-permute-done.12.refs_2_ = f32[32,256]{1,0:T(8,128)S(1)} collective-permute-done((f32[32,256]{1,0:T(8,128)S(1)}, f32[32,256]{1,0:T(8,128)S(1)}, u32[]{:S(2)}, u32[]{:S(2)}) %collective-permute-start.12) | collective-permute-done | bytes 32800 | tf_op jit(solution)/shard_map/ppermute | solution.py:275
  28.4 2.8 %collective-permute-start.13 = (f32[96,256]{1,0:T(8,128)S(1)}, f32[96,256]{1,0:T(8,128)S(1)}, u32[]{:S(2)}, u32[]{:S(2)}) collective-permute-start(f32[96,256]{1,0:T(8,128)S(1)} %get-tuple-element.40), channel_id=1, source_target_pairs={{0,18},{1,19},{2,16},{3,17},{4,22},{5,23},{6,20},{7,21},{8,26},{9,... | collective-permute-start | bytes 294920 | tf_op jit(solution)/shard_map/ppermute | solution.py:275
  31.2 1.5 %collective-permute-start.15 = (f32[96,256]{1,0:T(8,128)S(1)}, f32[96,256]{1,0:T(8,128)S(1)}, u32[]{:S(2)}, u32[]{:S(2)}) collective-permute-start(f32[96,256]{1,0:T(8,128)S(1)} %get-tuple-element.42), channel_id=1, source_target_pairs={{0,24},{1,25},{2,26},{3,27},{4,28},{5,29},{6,30},{7,31},{8,16},{9,... | collective-permute-start | bytes 294920 | tf_op jit(solution)/shard_map/ppermute | solution.py:275
  32.7 3.4 %collective-permute-done.13.refs_6_.refs_5_ = f32[96,256]{1,0:T(8,128)S(1)} collective-permute-done((f32[96,256]{1,0:T(8,128)S(1)}, f32[96,256]{1,0:T(8,128)S(1)}, u32[]{:S(2)}, u32[]{:S(2)}) %collective-permute-start.13) | collective-permute-done | bytes 98336 | tf_op jit(solution)/shard_map/ppermute | solution.py:275
  36.4 3.8 %collective-permute-done.15.refs_8_.refs_7_ = f32[96,256]{1,0:T(8,128)S(1)} collective-permute-done((f32[96,256]{1,0:T(8,128)S(1)}, f32[96,256]{1,0:T(8,128)S(1)}, u32[]{:S(2)}, u32[]{:S(2)}) %collective-permute-start.15) | collective-permute-done | bytes 98336 | tf_op jit(solution)/shard_map/ppermute | solution.py:275
  40.3 1.2 %collective-permute-start.18 = (f32[1,32,256]{2,1,0:T(8,128)S(1)}, f32[1,32,256]{2,1,0:T(8,128)S(1)}, u32[]{:S(2)}, u32[]{:S(2)}) collective-permute-start(f32[1,32,256]{2,1,0:T(8,128)S(1)} %bitcast.23), channel_id=1, source_target_pairs={{0,7},{1,6},{2,5},{3,4},{4,3},{5,2},{6,1},{7,0},{8,15},{9,14},{10,... | collective-permute-start | bytes 98312 | tf_op jit(solution)/shard_map/ppermute | solution.py:275
  41.5 1.0 %collective-permute-start.17 = (f32[1,32,256]{2,1,0:T(8,128)S(1)}, f32[1,32,256]{2,1,0:T(8,128)S(1)}, u32[]{:S(2)}, u32[]{:S(2)}) collective-permute-start(f32[1,32,256]{2,1,0:T(8,128)S(1)} %bitcast.24), channel_id=1, source_target_pairs={{0,6},{1,7},{2,4},{3,5},{4,2},{5,3},{6,0},{7,1},{8,14},{9,15},{10,... | collective-permute-start | bytes 98312 | tf_op jit(solution)/shard_map/ppermute | solution.py:275
  42.9 2.0 %collective-permute-done.18 = f32[1,32,256]{2,1,0:T(8,128)S(1)} collective-permute-done((f32[1,32,256]{2,1,0:T(8,128)S(1)}, f32[1,32,256]{2,1,0:T(8,128)S(1)}, u32[]{:S(2)}, u32[]{:S(2)}) %collective-permute-start.18) | collective-permute-done | bytes 32800 | tf_op jit(solution)/shard_map/ppermute | solution.py:275
  44.9 1.1 %collective-permute-done.16 = f32[1,32,256]{2,1,0:T(8,128)S(1)} collective-permute-done((f32[1,32,256]{2,1,0:T(8,128)S(1)}, f32[1,32,256]{2,1,0:T(8,128)S(1)}, u32[]{:S(2)}, u32[]{:S(2)}) %collective-permute-start.16) | collective-permute-done | bytes 32800 | tf_op jit(solution)/shard_map/ppermute | solution.py:275
  46.2 0.9 %finish.1 = f32[128,256]{1,0:T(8,128)} custom-call(bf16[128,256]{1,0:T(8,128)(2,1)S(1)} %get-tuple-element.32.refs_0_, f32[128,256]{1,0:T(8,128)S(1)} %get-tuple-element.33.refs_1_, f32[256,256]{1,0:T(8,128)S(1)} %get-tuple-element.34.refs_0_.refs_2_, f32[256,256]{1,0:T(8,128)S(1)} %collective-permute-done.9.refs_1_.refs_3_, ...), custom_call_target="tpu_custom_call" | custom-call | flops 33554432 | bytes 655360 | tf_op jit(solution)/shard_map/finish/pallas_call | solution.py:213
  47.4 0.7 %place.1 = f32[256,256]{1,0:T(8,128)} custom-call(f32[4,32,256]{2,1,0:T(8,128)S(1)} %pad_maximum_fusion.refs_0_, f32[4,32,256]{2,1,0:T(8,128)S(1)} %collective-permute-done.19.refs_1_), custom_call_target="tpu_custom_call" | custom-call | bytes 524288 | tf_op jit(solution)/shard_map/place/pallas_call | solution.py:213
  (39 shorter events, 3.7 us)
Async XLA Ops:
  0.6 1.8 %copy-start = (f32[128,256]{1,0:T(8,128)S(1)}, f32[128,256]{1,0:T(8,128)}, u32[]{:S(2)}) copy-start(f32[128,256]{1,0:T(8,128)} %refs_2_.3) | copy-start | bytes 393220
  1.9 13.3 %copy-start.1 = (f32[256,256]{1,0:T(8,128)S(1)}, f32[256,256]{1,0:T(8,128)}, u32[]{:S(2)}) copy-start(f32[256,256]{1,0:T(8,128)} %refs_3_.2) | copy-start | bytes 786436
  1.9 3.1 %collective-permute-start.1 = (f32[8,16,256]{2,1,0:T(8,128)S(1)}, f32[8,16,256]{2,1,0:T(8,128)S(1)}, u32[]{:S(2)}, u32[]{:S(2)}) collective-permute-start(f32[8,16,256]{2,1,0:T(8,128)S(1)} %get-tuple-element.28), channel_id=1, source_target_pairs={{0,2},{1,3},{2,0},{3,1},{4,6},{5,7},{6,4},{7,5},{8,10},{9,11},{10,... | collective-permute-start | bytes 393224 | tf_op jit(solution)/shard_map/ppermute | solution.py:275
  2.4 9.5 %collective-permute-start = (f32[128,256]{1,0:T(8,128)S(1)}, f32[128,256]{1,0:T(8,128)S(1)}, u32[]{:S(2)}, u32[]{:S(2)}) collective-permute-start(f32[128,256]{1,0:T(8,128)S(1)} %copy-done), channel_id=1, source_target_pairs={{0,1},{1,0},{2,3},{3,2},{4,5},{5,4},{6,7},{7,6},{8,9},{9,8},{10,11... | collective-permute-start | bytes 393224 | tf_op jit(solution)/shard_map/ppermute | solution.py:237
  5.0 10.1 %copy-start.2 = (f32[128,256]{1,0:T(8,128)S(1)}, f32[128,256]{1,0:T(8,128)}, u32[]{:S(2)}) copy-start(f32[128,256]{1,0:T(8,128)} %refs_2_.2) | copy-start | bytes 393220
  5.1 9.4 %collective-permute-start.8 = (f32[2,16,256]{2,1,0:T(8,128)S(1)}, f32[2,16,256]{2,1,0:T(8,128)S(1)}, u32[]{:S(2)}, u32[]{:S(2)}) collective-permute-start(f32[2,16,256]{2,1,0:T(8,128)S(1)} %get-tuple-element.43), channel_id=1, source_target_pairs={{0,18},{1,19},{2,16},{3,17},{4,22},{5,23},{6,20},{7,21},{8,26},{9,... | collective-permute-start | bytes 98312 | tf_op jit(solution)/shard_map/ppermute | solution.py:275
  7.5 7.0 %collective-permute-start.7 = (f32[2,16,256]{2,1,0:T(8,128)S(1)}, f32[2,16,256]{2,1,0:T(8,128)S(1)}, u32[]{:S(2)}, u32[]{:S(2)}) collective-permute-start(f32[2,16,256]{2,1,0:T(8,128)S(1)} %get-tuple-element.44), channel_id=1, source_target_pairs={{0,30},{1,31},{2,28},{3,29},{4,26},{5,27},{6,24},{7,25},{8,22},{9,... | collective-permute-start | bytes 98312 | tf_op jit(solution)/shard_map/ppermute | solution.py:275
  9.7 5.8 %collective-permute-start.6 = (f32[2,16,256]{2,1,0:T(8,128)S(1)}, f32[2,16,256]{2,1,0:T(8,128)S(1)}, u32[]{:S(2)}, u32[]{:S(2)}) collective-permute-start(f32[2,16,256]{2,1,0:T(8,128)S(1)} %get-tuple-element.45), channel_id=1, source_target_pairs={{0,26},{1,27},{2,24},{3,25},{4,30},{5,31},{6,28},{7,29},{8,18},{9,... | collective-permute-start | bytes 98312 | tf_op jit(solution)/shard_map/ppermute | solution.py:275
  12.0 5.2 %collective-permute-start.5 = (f32[2,16,256]{2,1,0:T(8,128)S(1)}, f32[2,16,256]{2,1,0:T(8,128)S(1)}, u32[]{:S(2)}, u32[]{:S(2)}) collective-permute-start(f32[2,16,256]{2,1,0:T(8,128)S(1)} %get-tuple-element.46), channel_id=1, source_target_pairs={{0,22},{1,23},{2,20},{3,21},{4,18},{5,19},{6,16},{7,17},{8,30},{9,... | collective-permute-start | bytes 98312 | tf_op jit(solution)/shard_map/ppermute | solution.py:275
  12.0 5.2 %collective-permute-start.4 = (f32[2,16,256]{2,1,0:T(8,128)S(1)}, f32[2,16,256]{2,1,0:T(8,128)S(1)}, u32[]{:S(2)}, u32[]{:S(2)}) collective-permute-start(f32[2,16,256]{2,1,0:T(8,128)S(1)} %get-tuple-element.47), channel_id=1, source_target_pairs={{0,14},{1,15},{2,12},{3,13},{4,10},{5,11},{6,8},{7,9},{8,6},{9,7},... | collective-permute-start | bytes 98312 | tf_op jit(solution)/shard_map/ppermute | solution.py:275
  14.5 3.3 %collective-permute-start.3 = (f32[2,16,256]{2,1,0:T(8,128)S(1)}, f32[2,16,256]{2,1,0:T(8,128)S(1)}, u32[]{:S(2)}, u32[]{:S(2)}) collective-permute-start(f32[2,16,256]{2,1,0:T(8,128)S(1)} %get-tuple-element.48), channel_id=1, source_target_pairs={{0,10},{1,11},{2,8},{3,9},{4,14},{5,15},{6,12},{7,13},{8,2},{9,3},... | collective-permute-start | bytes 98312 | tf_op jit(solution)/shard_map/ppermute | solution.py:275
  14.5 3.5 %collective-permute-start.2 = (f32[2,16,256]{2,1,0:T(8,128)S(1)}, f32[2,16,256]{2,1,0:T(8,128)S(1)}, u32[]{:S(2)}, u32[]{:S(2)}) collective-permute-start(f32[2,16,256]{2,1,0:T(8,128)S(1)} %get-tuple-element.49), channel_id=1, source_target_pairs={{0,6},{1,7},{2,4},{3,5},{4,2},{5,3},{6,0},{7,1},{8,14},{9,15},{10,... | collective-permute-start | bytes 98312 | tf_op jit(solution)/shard_map/ppermute | solution.py:275
  15.2 2.8 %copy-start.3 = (f32[128,256]{1,0:T(8,128)S(1)}, f32[128,256]{1,0:T(8,128)}, u32[]{:S(2)}) copy-start(f32[128,256]{1,0:T(8,128)} %refs_3_.3) | copy-start | bytes 393220
  19.2 1.6 %collective-permute-start.9 = (f32[256,256]{1,0:T(8,128)S(1)}, f32[256,256]{1,0:T(8,128)S(1)}, u32[]{:S(2)}, u32[]{:S(2)}) collective-permute-start(f32[256,256]{1,0:T(8,128)S(1)} %get-tuple-element.35), channel_id=1, source_target_pairs={{0,2},{1,3},{2,0},{3,1},{4,6},{5,7},{6,4},{7,5},{8,10},{9,11},{10,... | collective-permute-start | bytes 786440 | tf_op jit(solution)/shard_map/ppermute | solution.py:275
  20.8 7.6 %collective-permute-start.10 = (f32[160,256]{1,0:T(8,128)S(1)}, f32[160,256]{1,0:T(8,128)S(1)}, u32[]{:S(2)}, u32[]{:S(2)}) collective-permute-start(f32[160,256]{1,0:T(8,128)S(1)} %get-tuple-element.37), channel_id=1, source_target_pairs={{0,6},{1,7},{2,4},{3,5},{4,2},{5,3},{6,0},{7,1},{8,14},{9,15},{10,... | collective-permute-start | bytes 491528 | tf_op jit(solution)/shard_map/ppermute | solution.py:275
  21.4 7.0 %collective-permute-start.11 = (f32[160,256]{1,0:T(8,128)S(1)}, f32[160,256]{1,0:T(8,128)S(1)}, u32[]{:S(2)}, u32[]{:S(2)}) collective-permute-start(f32[160,256]{1,0:T(8,128)S(1)} %get-tuple-element.38), channel_id=1, source_target_pairs={{0,1},{1,0},{2,3},{3,2},{4,5},{5,4},{6,7},{7,6},{8,9},{9,8},{10,11... | collective-permute-start | bytes 491528 | tf_op jit(solution)/shard_map/ppermute | solution.py:275
  22.7 5.7 %collective-permute-start.12 = (f32[32,256]{1,0:T(8,128)S(1)}, f32[32,256]{1,0:T(8,128)S(1)}, u32[]{:S(2)}, u32[]{:S(2)}) collective-permute-start(f32[32,256]{1,0:T(8,128)S(1)} %get-tuple-element.39), channel_id=1, source_target_pairs={{0,7},{1,6},{2,5},{3,4},{4,3},{5,2},{6,1},{7,0},{8,15},{9,14},{10,... | collective-permute-start | bytes 98312 | tf_op jit(solution)/shard_map/ppermute | solution.py:275
  28.4 7.7 %collective-permute-start.13 = (f32[96,256]{1,0:T(8,128)S(1)}, f32[96,256]{1,0:T(8,128)S(1)}, u32[]{:S(2)}, u32[]{:S(2)}) collective-permute-start(f32[96,256]{1,0:T(8,128)S(1)} %get-tuple-element.40), channel_id=1, source_target_pairs={{0,18},{1,19},{2,16},{3,17},{4,22},{5,23},{6,20},{7,21},{8,26},{9,... | collective-permute-start | bytes 294920 | tf_op jit(solution)/shard_map/ppermute | solution.py:275
  31.2 5.2 %collective-permute-start.14 = (f32[96,256]{1,0:T(8,128)S(1)}, f32[96,256]{1,0:T(8,128)S(1)}, u32[]{:S(2)}, u32[]{:S(2)}) collective-permute-start(f32[96,256]{1,0:T(8,128)S(1)} %get-tuple-element.41), channel_id=1, source_target_pairs={{0,10},{1,11},{2,8},{3,9},{4,14},{5,15},{6,12},{7,13},{8,2},{9,3},... | collective-permute-start | bytes 294920 | tf_op jit(solution)/shard_map/ppermute | solution.py:275
  31.2 9.1 %collective-permute-start.15 = (f32[96,256]{1,0:T(8,128)S(1)}, f32[96,256]{1,0:T(8,128)S(1)}, u32[]{:S(2)}, u32[]{:S(2)}) collective-permute-start(f32[96,256]{1,0:T(8,128)S(1)} %get-tuple-element.42), channel_id=1, source_target_pairs={{0,24},{1,25},{2,26},{3,27},{4,28},{5,29},{6,30},{7,31},{8,16},{9,... | collective-permute-start | bytes 294920 | tf_op jit(solution)/shard_map/ppermute | solution.py:275
  40.3 4.6 %collective-permute-start.18 = (f32[1,32,256]{2,1,0:T(8,128)S(1)}, f32[1,32,256]{2,1,0:T(8,128)S(1)}, u32[]{:S(2)}, u32[]{:S(2)}) collective-permute-start(f32[1,32,256]{2,1,0:T(8,128)S(1)} %bitcast.23), channel_id=1, source_target_pairs={{0,7},{1,6},{2,5},{3,4},{4,3},{5,2},{6,1},{7,0},{8,15},{9,14},{10,... | collective-permute-start | bytes 98312 | tf_op jit(solution)/shard_map/ppermute | solution.py:275
  41.5 3.4 %collective-permute-start.17 = (f32[1,32,256]{2,1,0:T(8,128)S(1)}, f32[1,32,256]{2,1,0:T(8,128)S(1)}, u32[]{:S(2)}, u32[]{:S(2)}) collective-permute-start(f32[1,32,256]{2,1,0:T(8,128)S(1)} %bitcast.24), channel_id=1, source_target_pairs={{0,6},{1,7},{2,4},{3,5},{4,2},{5,3},{6,0},{7,1},{8,14},{9,15},{10,... | collective-permute-start | bytes 98312 | tf_op jit(solution)/shard_map/ppermute | solution.py:275
  42.5 3.4 %collective-permute-start.16 = (f32[1,32,256]{2,1,0:T(8,128)S(1)}, f32[1,32,256]{2,1,0:T(8,128)S(1)}, u32[]{:S(2)}, u32[]{:S(2)}) collective-permute-start(f32[1,32,256]{2,1,0:T(8,128)S(1)} %bitcast.25), channel_id=1, source_target_pairs={{0,3},{1,2},{2,1},{3,0},{4,7},{5,6},{6,5},{7,4},{8,11},{9,10},{10,... | collective-permute-start | bytes 98312 | tf_op jit(solution)/shard_map/ppermute | solution.py:275
  46.0 1.4 %collective-permute-start.19 = (f32[4,32,256]{2,1,0:T(8,128)S(1)}, f32[4,32,256]{2,1,0:T(8,128)S(1)}, u32[]{:S(2)}, u32[]{:S(2)}) collective-permute-start(f32[4,32,256]{2,1,0:T(8,128)S(1)} %pad_maximum_fusion.refs_0_), channel_id=1, source_target_pairs={{0,2},{1,3},{2,0},{3,1},{4,6},{5,7},{6,4},{7,5},{8,10},{9,11},{10,... | collective-permute-start | bytes 393224 | tf_op jit(solution)/shard_map/ppermute | solution.py:275
  (2 other events, 1.4 us)

commit v5 on v3

--- a/solution.py
+++ b/solution.py
@@ -25,11 +25,14 @@
 
 def dot3(a, b, dims=((1,), (0,))):
     (a_high, a_low), (b_high, b_low) = a, b
-    return (product(a_low, b_high, dims) + product(a_high, b_low, dims)) + product(a_high, b_high, dims)
+    left = jnp.concatenate([a_low, a_high, a_high], axis=dims[0][0])
+    right = jnp.concatenate([b_high, b_low, b_high], axis=dims[1][0])
+    return product(left, right, dims)
 
 
 def dot_onehot(a, b, dims):
-    return product(a, b[1], dims) + product(a, b[0], dims)
+    left = jnp.concatenate([a, a], axis=dims[0][0])
+    return product(left, jnp.concatenate([b[1], b[0]], axis=dims[1][0]), dims)
 
 
 def tree(terms):

time: 47.7 us -> 47.5 us (level)
  no operation moved by 1% of the time
where the time goes in v5:
time: 47.5 us; the launch traced here: 47.3 us
  starting transfers between devices  23.8 us (50%)
  waiting for transfers between devices  17.7 us (37%)
  Pallas kernels  4.96 us (10%)
  between operations  0.74 us (2%)
    ppermute x19, starting transfers between devices, swap(): lax.ppermute(value, both, [(i, i ^ mask) for i in range(devices)])  21.2 us
    ppermute x19, waiting for transfers between devices, swap(): lax.ppermute(value, both, [(i, i ^ mask) for i in range(devices)])  17.7 us
    pallas_call x9, Pallas kernels, kernel(): pl.pallas_call(lambda *refs: body(*refs[:count], *refs[count + len(after)...  4.96 us
    ppermute x1, starting transfers between devices, shift(): return lax.ppermute(value, 'blk', pairs)  2.6 us
  transfers between devices with their start and end apart: 20, of which 11 were waited for; matrix products, arithmetic and copies ran while one was open for 0% of the time, Pallas kernels for 4%

profile of v5, /device:TPU:0, one launch (start us, length us, event | category | flops | bytes accessed | tf_op | source)
XLA Modules:
  0.0 47.3 jit_solution(3811341227172912388)
XLA Ops:
  0.6 1.2 %gather.1 = (f32[8,16,256]{2,1,0:T(8,128)S(1)}, f32[8,16,256]{2,1,0:T(8,128)S(1)}, bf16[128,256]{1,0:T(8,128)(2,1)S(1)}) custom-call(s32[1,16]{1,0:T(1,128)} %refs_0_.3, s32[1,256]{1,0:T(1,128)} %refs_1_.1, f32[128,256]{1,0:T(8,128)} %refs_2_.3), custom_call_target="tpu_custom_call" | custom-call | flops 16777216 | bytes 393216 | tf_op jit(solution)/shard_map/gather/pallas_call | solution.py:216
  2.4 2.6 %collective-permute-start = (f32[128,256]{1,0:T(8,128)S(1)}, f32[128,256]{1,0:T(8,128)S(1)}, u32[]{:S(2)}, u32[]{:S(2)}) collective-permute-start(f32[128,256]{1,0:T(8,128)S(1)} %copy-done), channel_id=1, source_target_pairs={{0,1},{1,0},{2,3},{3,2},{4,5},{5,4},{6,7},{7,6},{8,9},{9,8},{10,11... | collective-permute-start | bytes 393224 | tf_op jit(solution)/shard_map/ppermute | solution.py:240
  5.0 2.4 %collective-permute-start.8 = (f32[2,16,256]{2,1,0:T(8,128)S(1)}, f32[2,16,256]{2,1,0:T(8,128)S(1)}, u32[]{:S(2)}, u32[]{:S(2)}) collective-permute-start(f32[2,16,256]{2,1,0:T(8,128)S(1)} %get-tuple-element.43), channel_id=1, source_target_pairs={{0,18},{1,19},{2,16},{3,17},{4,22},{5,23},{6,20},{7,21},{8,26},{9,... | collective-permute-start | bytes 98312 | tf_op jit(solution)/shard_map/ppermute | solution.py:278
  7.5 2.2 %collective-permute-start.7 = (f32[2,16,256]{2,1,0:T(8,128)S(1)}, f32[2,16,256]{2,1,0:T(8,128)S(1)}, u32[]{:S(2)}, u32[]{:S(2)}) collective-permute-start(f32[2,16,256]{2,1,0:T(8,128)S(1)} %get-tuple-element.44), channel_id=1, source_target_pairs={{0,30},{1,31},{2,28},{3,29},{4,26},{5,27},{6,24},{7,25},{8,22},{9,... | collective-permute-start | bytes 98312 | tf_op jit(solution)/shard_map/ppermute | solution.py:278
  9.7 2.2 %collective-permute-start.6 = (f32[2,16,256]{2,1,0:T(8,128)S(1)}, f32[2,16,256]{2,1,0:T(8,128)S(1)}, u32[]{:S(2)}, u32[]{:S(2)}) collective-permute-start(f32[2,16,256]{2,1,0:T(8,128)S(1)} %get-tuple-element.45), channel_id=1, source_target_pairs={{0,26},{1,27},{2,24},{3,25},{4,30},{5,31},{6,28},{7,29},{8,18},{9,... | collective-permute-start | bytes 98312 | tf_op jit(solution)/shard_map/ppermute | solution.py:278
  11.9 2.5 %collective-permute-start.4 = (f32[2,16,256]{2,1,0:T(8,128)S(1)}, f32[2,16,256]{2,1,0:T(8,128)S(1)}, u32[]{:S(2)}, u32[]{:S(2)}) collective-permute-start(f32[2,16,256]{2,1,0:T(8,128)S(1)} %get-tuple-element.47), channel_id=1, source_target_pairs={{0,14},{1,15},{2,12},{3,13},{4,10},{5,11},{6,8},{7,9},{8,6},{9,7},... | collective-permute-start | bytes 98312 | tf_op jit(solution)/shard_map/ppermute | solution.py:278
  14.5 0.6 %collective-permute-start.2 = (f32[2,16,256]{2,1,0:T(8,128)S(1)}, f32[2,16,256]{2,1,0:T(8,128)S(1)}, u32[]{:S(2)}, u32[]{:S(2)}) collective-permute-start(f32[2,16,256]{2,1,0:T(8,128)S(1)} %get-tuple-element.49), channel_id=1, source_target_pairs={{0,6},{1,7},{2,4},{3,5},{4,2},{5,3},{6,0},{7,1},{8,14},{9,15},{10,... | collective-permute-start | bytes 98312 | tf_op jit(solution)/shard_map/ppermute | solution.py:278
  15.4 1.7 %collective-permute-done.5.refs_9_ = f32[2,16,256]{2,1,0:T(8,128)S(1)} collective-permute-done((f32[2,16,256]{2,1,0:T(8,128)S(1)}, f32[2,16,256]{2,1,0:T(8,128)S(1)}, u32[]{:S(2)}, u32[]{:S(2)}) %collective-permute-start.5) | collective-permute-done | bytes 32800 | tf_op jit(solution)/shard_map/ppermute | solution.py:278
  17.2 0.6 %collective-permute-done.3.refs_7_ = f32[2,16,256]{2,1,0:T(8,128)S(1)} collective-permute-done((f32[2,16,256]{2,1,0:T(8,128)S(1)}, f32[2,16,256]{2,1,0:T(8,128)S(1)}, u32[]{:S(2)}, u32[]{:S(2)}) %collective-permute-start.3) | collective-permute-done | bytes 32800 | tf_op jit(solution)/shard_map/ppermute | solution.py:278
  18.0 1.0 %layer.1 = (f32[128,256]{1,0:T(8,128)S(1)}, bf16[2,128,256]{2,1,0:T(8,128)(2,1)S(1)}, f32[256,256]{1,0:T(8,128)S(1)}, f32[256,256]{1,0:T(8,128)S(1)}) custom-call(f32[128,256]{1,0:T(8,128)S(1)} %get-tuple-element.24.refs_0_, bf16[2,128,256]{2,1,0:T(8,128)(2,1)S(1)} %get-tuple-element.25.refs_1_, bf16[2,256,256]{2,1,0:T(8,128)(2,1)S(1)} %get-tuple-element.26.refs_2_, ...), custom_call_target="tpu_custom_call" | custom-call | flops 251658240 | bytes 1048576 | tf_op jit(solution)/shard_map/layer/pallas_call | solution.py:216
  19.4 0.8 %inner.1 = (f32[128,256]{1,0:T(8,128)S(1)}, f32[1,128,256]{2,1,0:T(8,128)S(1)}, f32[128,256]{1,0:T(8,128)}) custom-call(bf16[2,2,128,128]{3,2,1,0:T(8,128)(2,1)S(1)} %get-tuple-element.23.refs_0_, bf16[2,128,256]{2,1,0:T(8,128)(2,1)S(1)} %get-tuple-element.29.refs_1_, f32[128,256]{1,0:T(8,128)S(1)} %get-tuple-element.30.refs_2_), custom_call_target="tpu_custom_call" | custom-call | flops 50331648 | bytes 786432 | tf_op jit(solution)/shard_map/inner/pallas_call | solution.py:216
  21.2 1.3 %collective-permute-start.11 = (f32[160,256]{1,0:T(8,128)S(1)}, f32[160,256]{1,0:T(8,128)S(1)}, u32[]{:S(2)}, u32[]{:S(2)}) collective-permute-start(f32[160,256]{1,0:T(8,128)S(1)} %get-tuple-element.38), channel_id=1, source_target_pairs={{0,1},{1,0},{2,3},{3,2},{4,5},{5,4},{6,7},{7,6},{8,9},{9,8},{10,11... | collective-permute-start | bytes 491528 | tf_op jit(solution)/shard_map/ppermute | solution.py:278
  22.5 1.1 %collective-permute-start.12 = (f32[32,256]{1,0:T(8,128)S(1)}, f32[32,256]{1,0:T(8,128)S(1)}, u32[]{:S(2)}, u32[]{:S(2)}) collective-permute-start(f32[32,256]{1,0:T(8,128)S(1)} %get-tuple-element.39), channel_id=1, source_target_pairs={{0,7},{1,6},{2,5},{3,4},{4,3},{5,2},{6,1},{7,0},{8,15},{9,14},{10,... | collective-permute-start | bytes 98312 | tf_op jit(solution)/shard_map/ppermute | solution.py:278
  23.6 4.6 %collective-permute-done.12.refs_2_ = f32[32,256]{1,0:T(8,128)S(1)} collective-permute-done((f32[32,256]{1,0:T(8,128)S(1)}, f32[32,256]{1,0:T(8,128)S(1)}, u32[]{:S(2)}, u32[]{:S(2)}) %collective-permute-start.12) | collective-permute-done | bytes 32800 | tf_op jit(solution)/shard_map/ppermute | solution.py:278
  28.2 2.8 %collective-permute-start.13 = (f32[96,256]{1,0:T(8,128)S(1)}, f32[96,256]{1,0:T(8,128)S(1)}, u32[]{:S(2)}, u32[]{:S(2)}) collective-permute-start(f32[96,256]{1,0:T(8,128)S(1)} %get-tuple-element.40), channel_id=1, source_target_pairs={{0,18},{1,19},{2,16},{3,17},{4,22},{5,23},{6,20},{7,21},{8,26},{9,... | collective-permute-start | bytes 294920 | tf_op jit(solution)/shard_map/ppermute | solution.py:278
  31.0 1.3 %collective-permute-start.14 = (f32[96,256]{1,0:T(8,128)S(1)}, f32[96,256]{1,0:T(8,128)S(1)}, u32[]{:S(2)}, u32[]{:S(2)}) collective-permute-start(f32[96,256]{1,0:T(8,128)S(1)} %get-tuple-element.41), channel_id=1, source_target_pairs={{0,24},{1,25},{2,26},{3,27},{4,28},{5,29},{6,30},{7,31},{8,16},{9,... | collective-permute-start | bytes 294920 | tf_op jit(solution)/shard_map/ppermute | solution.py:278
  32.3 5.6 %collective-permute-done.13.refs_6_.refs_5_ = f32[96,256]{1,0:T(8,128)S(1)} collective-permute-done((f32[96,256]{1,0:T(8,128)S(1)}, f32[96,256]{1,0:T(8,128)S(1)}, u32[]{:S(2)}, u32[]{:S(2)}) %collective-permute-start.13) | collective-permute-done | bytes 98336 | tf_op jit(solution)/shard_map/ppermute | solution.py:278
  38.4 1.6 %collective-permute-done.15.refs_8_.refs_7_ = f32[96,256]{1,0:T(8,128)S(1)} collective-permute-done((f32[96,256]{1,0:T(8,128)S(1)}, f32[96,256]{1,0:T(8,128)S(1)}, u32[]{:S(2)}, u32[]{:S(2)}) %collective-permute-start.15) | collective-permute-done | bytes 98336 | tf_op jit(solution)/shard_map/ppermute | solution.py:278
  40.0 1.5 %collective-permute-start.18 = (f32[1,32,256]{2,1,0:T(8,128)S(1)}, f32[1,32,256]{2,1,0:T(8,128)S(1)}, u32[]{:S(2)}, u32[]{:S(2)}) collective-permute-start(f32[1,32,256]{2,1,0:T(8,128)S(1)} %bitcast.23), channel_id=1, source_target_pairs={{0,7},{1,6},{2,5},{3,4},{4,3},{5,2},{6,1},{7,0},{8,15},{9,14},{10,... | collective-permute-start | bytes 98312 | tf_op jit(solution)/shard_map/ppermute | solution.py:278
  41.5 1.5 %collective-permute-start.16 = (f32[1,32,256]{2,1,0:T(8,128)S(1)}, f32[1,32,256]{2,1,0:T(8,128)S(1)}, u32[]{:S(2)}, u32[]{:S(2)}) collective-permute-start(f32[1,32,256]{2,1,0:T(8,128)S(1)} %bitcast.25), channel_id=1, source_target_pairs={{0,3},{1,2},{2,1},{3,0},{4,7},{5,6},{6,5},{7,4},{8,11},{9,10},{10,... | collective-permute-start | bytes 98312 | tf_op jit(solution)/shard_map/ppermute | solution.py:278
  43.0 1.4 %collective-permute-done.18 = f32[1,32,256]{2,1,0:T(8,128)S(1)} collective-permute-done((f32[1,32,256]{2,1,0:T(8,128)S(1)}, f32[1,32,256]{2,1,0:T(8,128)S(1)}, u32[]{:S(2)}, u32[]{:S(2)}) %collective-permute-start.18) | collective-permute-done | bytes 32800 | tf_op jit(solution)/shard_map/ppermute | solution.py:278
  44.4 0.8 %collective-permute-done.17 = f32[1,32,256]{2,1,0:T(8,128)S(1)} collective-permute-done((f32[1,32,256]{2,1,0:T(8,128)S(1)}, f32[1,32,256]{2,1,0:T(8,128)S(1)}, u32[]{:S(2)}, u32[]{:S(2)}) %collective-permute-start.17) | collective-permute-done | bytes 32800 | tf_op jit(solution)/shard_map/ppermute | solution.py:278
  45.4 0.9 %finish.1 = f32[128,256]{1,0:T(8,128)} custom-call(bf16[128,256]{1,0:T(8,128)(2,1)S(1)} %get-tuple-element.32.refs_0_, f32[128,256]{1,0:T(8,128)S(1)} %get-tuple-element.33.refs_1_, f32[256,256]{1,0:T(8,128)S(1)} %get-tuple-element.34.refs_0_.refs_2_, f32[256,256]{1,0:T(8,128)S(1)} %collective-permute-done.9.refs_1_.refs_3_, ...), custom_call_target="tpu_custom_call" | custom-call | flops 33554432 | bytes 655360 | tf_op jit(solution)/shard_map/finish/pallas_call | solution.py:216
  46.6 0.7 %place.1 = f32[256,256]{1,0:T(8,128)} custom-call(f32[4,32,256]{2,1,0:T(8,128)S(1)} %pad_maximum_fusion.refs_0_, f32[4,32,256]{2,1,0:T(8,128)S(1)} %collective-permute-done.19.refs_1_), custom_call_target="tpu_custom_call" | custom-call | bytes 524288 | tf_op jit(solution)/shard_map/place/pallas_call | solution.py:216
  (39 shorter events, 3.5 us)
Async XLA Ops:
  0.6 1.8 %copy-start = (f32[128,256]{1,0:T(8,128)S(1)}, f32[128,256]{1,0:T(8,128)}, u32[]{:S(2)}) copy-start(f32[128,256]{1,0:T(8,128)} %refs_2_.3) | copy-start | bytes 393220
  1.9 13.3 %copy-start.1 = (f32[256,256]{1,0:T(8,128)S(1)}, f32[256,256]{1,0:T(8,128)}, u32[]{:S(2)}) copy-start(f32[256,256]{1,0:T(8,128)} %refs_3_.2) | copy-start | bytes 786436
  1.9 3.1 %collective-permute-start.1 = (f32[8,16,256]{2,1,0:T(8,128)S(1)}, f32[8,16,256]{2,1,0:T(8,128)S(1)}, u32[]{:S(2)}, u32[]{:S(2)}) collective-permute-start(f32[8,16,256]{2,1,0:T(8,128)S(1)} %get-tuple-element.28), channel_id=1, source_target_pairs={{0,2},{1,3},{2,0},{3,1},{4,6},{5,7},{6,4},{7,5},{8,10},{9,11},{10,... | collective-permute-start | bytes 393224 | tf_op jit(solution)/shard_map/ppermute | solution.py:278
  2.4 9.5 %collective-permute-start = (f32[128,256]{1,0:T(8,128)S(1)}, f32[128,256]{1,0:T(8,128)S(1)}, u32[]{:S(2)}, u32[]{:S(2)}) collective-permute-start(f32[128,256]{1,0:T(8,128)S(1)} %copy-done), channel_id=1, source_target_pairs={{0,1},{1,0},{2,3},{3,2},{4,5},{5,4},{6,7},{7,6},{8,9},{9,8},{10,11... | collective-permute-start | bytes 393224 | tf_op jit(solution)/shard_map/ppermute | solution.py:240
  5.0 10.1 %copy-start.2 = (f32[128,256]{1,0:T(8,128)S(1)}, f32[128,256]{1,0:T(8,128)}, u32[]{:S(2)}) copy-start(f32[128,256]{1,0:T(8,128)} %refs_2_.2) | copy-start | bytes 393220
  5.0 9.4 %collective-permute-start.8 = (f32[2,16,256]{2,1,0:T(8,128)S(1)}, f32[2,16,256]{2,1,0:T(8,128)S(1)}, u32[]{:S(2)}, u32[]{:S(2)}) collective-permute-start(f32[2,16,256]{2,1,0:T(8,128)S(1)} %get-tuple-element.43), channel_id=1, source_target_pairs={{0,18},{1,19},{2,16},{3,17},{4,22},{5,23},{6,20},{7,21},{8,26},{9,... | collective-permute-start | bytes 98312 | tf_op jit(solution)/shard_map/ppermute | solution.py:278
  7.5 7.0 %collective-permute-start.7 = (f32[2,16,256]{2,1,0:T(8,128)S(1)}, f32[2,16,256]{2,1,0:T(8,128)S(1)}, u32[]{:S(2)}, u32[]{:S(2)}) collective-permute-start(f32[2,16,256]{2,1,0:T(8,128)S(1)} %get-tuple-element.44), channel_id=1, source_target_pairs={{0,30},{1,31},{2,28},{3,29},{4,26},{5,27},{6,24},{7,25},{8,22},{9,... | collective-permute-start | bytes 98312 | tf_op jit(solution)/shard_map/ppermute | solution.py:278
  9.7 5.7 %collective-permute-start.6 = (f32[2,16,256]{2,1,0:T(8,128)S(1)}, f32[2,16,256]{2,1,0:T(8,128)S(1)}, u32[]{:S(2)}, u32[]{:S(2)}) collective-permute-start(f32[2,16,256]{2,1,0:T(8,128)S(1)} %get-tuple-element.45), channel_id=1, source_target_pairs={{0,26},{1,27},{2,24},{3,25},{4,30},{5,31},{6,28},{7,29},{8,18},{9,... | collective-permute-start | bytes 98312 | tf_op jit(solution)/shard_map/ppermute | solution.py:278
  11.9 5.2 %collective-permute-start.5 = (f32[2,16,256]{2,1,0:T(8,128)S(1)}, f32[2,16,256]{2,1,0:T(8,128)S(1)}, u32[]{:S(2)}, u32[]{:S(2)}) collective-permute-start(f32[2,16,256]{2,1,0:T(8,128)S(1)} %get-tuple-element.46), channel_id=1, source_target_pairs={{0,22},{1,23},{2,20},{3,21},{4,18},{5,19},{6,16},{7,17},{8,30},{9,... | collective-permute-start | bytes 98312 | tf_op jit(solution)/shard_map/ppermute | solution.py:278
  11.9 5.2 %collective-permute-start.4 = (f32[2,16,256]{2,1,0:T(8,128)S(1)}, f32[2,16,256]{2,1,0:T(8,128)S(1)}, u32[]{:S(2)}, u32[]{:S(2)}) collective-permute-start(f32[2,16,256]{2,1,0:T(8,128)S(1)} %get-tuple-element.47), channel_id=1, source_target_pairs={{0,14},{1,15},{2,12},{3,13},{4,10},{5,11},{6,8},{7,9},{8,6},{9,7},... | collective-permute-start | bytes 98312 | tf_op jit(solution)/shard_map/ppermute | solution.py:278
  14.5 3.3 %collective-permute-start.3 = (f32[2,16,256]{2,1,0:T(8,128)S(1)}, f32[2,16,256]{2,1,0:T(8,128)S(1)}, u32[]{:S(2)}, u32[]{:S(2)}) collective-permute-start(f32[2,16,256]{2,1,0:T(8,128)S(1)} %get-tuple-element.48), channel_id=1, source_target_pairs={{0,10},{1,11},{2,8},{3,9},{4,14},{5,15},{6,12},{7,13},{8,2},{9,3},... | collective-permute-start | bytes 98312 | tf_op jit(solution)/shard_map/ppermute | solution.py:278
  14.5 3.5 %collective-permute-start.2 = (f32[2,16,256]{2,1,0:T(8,128)S(1)}, f32[2,16,256]{2,1,0:T(8,128)S(1)}, u32[]{:S(2)}, u32[]{:S(2)}) collective-permute-start(f32[2,16,256]{2,1,0:T(8,128)S(1)} %get-tuple-element.49), channel_id=1, source_target_pairs={{0,6},{1,7},{2,4},{3,5},{4,2},{5,3},{6,0},{7,1},{8,14},{9,15},{10,... | collective-permute-start | bytes 98312 | tf_op jit(solution)/shard_map/ppermute | solution.py:278
  15.2 2.8 %copy-start.3 = (f32[128,256]{1,0:T(8,128)S(1)}, f32[128,256]{1,0:T(8,128)}, u32[]{:S(2)}) copy-start(f32[128,256]{1,0:T(8,128)} %refs_3_.3) | copy-start | bytes 393220
  19.0 1.6 %collective-permute-start.9 = (f32[256,256]{1,0:T(8,128)S(1)}, f32[256,256]{1,0:T(8,128)S(1)}, u32[]{:S(2)}, u32[]{:S(2)}) collective-permute-start(f32[256,256]{1,0:T(8,128)S(1)} %get-tuple-element.35), channel_id=1, source_target_pairs={{0,2},{1,3},{2,0},{3,1},{4,6},{5,7},{6,4},{7,5},{8,10},{9,11},{10,... | collective-permute-start | bytes 786440 | tf_op jit(solution)/shard_map/ppermute | solution.py:278
  20.7 7.6 %collective-permute-start.10 = (f32[160,256]{1,0:T(8,128)S(1)}, f32[160,256]{1,0:T(8,128)S(1)}, u32[]{:S(2)}, u32[]{:S(2)}) collective-permute-start(f32[160,256]{1,0:T(8,128)S(1)} %get-tuple-element.37), channel_id=1, source_target_pairs={{0,6},{1,7},{2,4},{3,5},{4,2},{5,3},{6,0},{7,1},{8,14},{9,15},{10,... | collective-permute-start | bytes 491528 | tf_op jit(solution)/shard_map/ppermute | solution.py:278
  21.2 7.0 %collective-permute-start.11 = (f32[160,256]{1,0:T(8,128)S(1)}, f32[160,256]{1,0:T(8,128)S(1)}, u32[]{:S(2)}, u32[]{:S(2)}) collective-permute-start(f32[160,256]{1,0:T(8,128)S(1)} %get-tuple-element.38), channel_id=1, source_target_pairs={{0,1},{1,0},{2,3},{3,2},{4,5},{5,4},{6,7},{7,6},{8,9},{9,8},{10,11... | collective-permute-start | bytes 491528 | tf_op jit(solution)/shard_map/ppermute | solution.py:278
  22.5 5.7 %collective-permute-start.12 = (f32[32,256]{1,0:T(8,128)S(1)}, f32[32,256]{1,0:T(8,128)S(1)}, u32[]{:S(2)}, u32[]{:S(2)}) collective-permute-start(f32[32,256]{1,0:T(8,128)S(1)} %get-tuple-element.39), channel_id=1, source_target_pairs={{0,7},{1,6},{2,5},{3,4},{4,3},{5,2},{6,1},{7,0},{8,15},{9,14},{10,... | collective-permute-start | bytes 98312 | tf_op jit(solution)/shard_map/ppermute | solution.py:278
  28.2 9.7 %collective-permute-start.13 = (f32[96,256]{1,0:T(8,128)S(1)}, f32[96,256]{1,0:T(8,128)S(1)}, u32[]{:S(2)}, u32[]{:S(2)}) collective-permute-start(f32[96,256]{1,0:T(8,128)S(1)} %get-tuple-element.40), channel_id=1, source_target_pairs={{0,18},{1,19},{2,16},{3,17},{4,22},{5,23},{6,20},{7,21},{8,26},{9,... | collective-permute-start | bytes 294920 | tf_op jit(solution)/shard_map/ppermute | solution.py:278
  31.0 7.4 %collective-permute-start.14 = (f32[96,256]{1,0:T(8,128)S(1)}, f32[96,256]{1,0:T(8,128)S(1)}, u32[]{:S(2)}, u32[]{:S(2)}) collective-permute-start(f32[96,256]{1,0:T(8,128)S(1)} %get-tuple-element.41), channel_id=1, source_target_pairs={{0,24},{1,25},{2,26},{3,27},{4,28},{5,29},{6,30},{7,31},{8,16},{9,... | collective-permute-start | bytes 294920 | tf_op jit(solution)/shard_map/ppermute | solution.py:278
  32.3 7.7 %collective-permute-start.15 = (f32[96,256]{1,0:T(8,128)S(1)}, f32[96,256]{1,0:T(8,128)S(1)}, u32[]{:S(2)}, u32[]{:S(2)}) collective-permute-start(f32[96,256]{1,0:T(8,128)S(1)} %get-tuple-element.42), channel_id=1, source_target_pairs={{0,10},{1,11},{2,8},{3,9},{4,14},{5,15},{6,12},{7,13},{8,2},{9,3},... | collective-permute-start | bytes 294920 | tf_op jit(solution)/shard_map/ppermute | solution.py:278
  40.0 4.4 %collective-permute-start.18 = (f32[1,32,256]{2,1,0:T(8,128)S(1)}, f32[1,32,256]{2,1,0:T(8,128)S(1)}, u32[]{:S(2)}, u32[]{:S(2)}) collective-permute-start(f32[1,32,256]{2,1,0:T(8,128)S(1)} %bitcast.23), channel_id=1, source_target_pairs={{0,7},{1,6},{2,5},{3,4},{4,3},{5,2},{6,1},{7,0},{8,15},{9,14},{10,... | collective-permute-start | bytes 98312 | tf_op jit(solution)/shard_map/ppermute | solution.py:278
  41.5 3.7 %collective-permute-start.17 = (f32[1,32,256]{2,1,0:T(8,128)S(1)}, f32[1,32,256]{2,1,0:T(8,128)S(1)}, u32[]{:S(2)}, u32[]{:S(2)}) collective-permute-start(f32[1,32,256]{2,1,0:T(8,128)S(1)} %bitcast.24), channel_id=1, source_target_pairs={{0,6},{1,7},{2,4},{3,5},{4,2},{5,3},{6,0},{7,1},{8,14},{9,15},{10,... | collective-permute-start | bytes 98312 | tf_op jit(solution)/shard_map/ppermute | solution.py:278
  41.5 3.7 %collective-permute-start.16 = (f32[1,32,256]{2,1,0:T(8,128)S(1)}, f32[1,32,256]{2,1,0:T(8,128)S(1)}, u32[]{:S(2)}, u32[]{:S(2)}) collective-permute-start(f32[1,32,256]{2,1,0:T(8,128)S(1)} %bitcast.25), channel_id=1, source_target_pairs={{0,3},{1,2},{2,1},{3,0},{4,7},{5,6},{6,5},{7,4},{8,11},{9,10},{10,... | collective-permute-start | bytes 98312 | tf_op jit(solution)/shard_map/ppermute | solution.py:278
  45.2 1.4 %collective-permute-start.19 = (f32[4,32,256]{2,1,0:T(8,128)S(1)}, f32[4,32,256]{2,1,0:T(8,128)S(1)}, u32[]{:S(2)}, u32[]{:S(2)}) collective-permute-start(f32[4,32,256]{2,1,0:T(8,128)S(1)} %pad_maximum_fusion.refs_0_), channel_id=1, source_target_pairs={{0,2},{1,3},{2,0},{3,1},{4,6},{5,7},{6,4},{7,5},{8,10},{9,11},{10,... | collective-permute-start | bytes 393224 | tf_op jit(solution)/shard_map/ppermute | solution.py:278
  (2 other events, 1.4 us)

commit v6 on v5

--- a/solution.py
+++ b/solution.py
@@ -254,20 +254,19 @@
     core = 1 << low
     outer_bits = list(range(high, devices.bit_length() - 1))
 
-    def masks(bits, straight=()):
+    def masks(bits):
         plain = [sum((i >> j & 1) << bit for j, bit in enumerate(bits)) for i in range(1 << len(bits))]
         if bits is outer_bits:
             return [mask ^ core * (i.bit_count() % 2) for i, mask in enumerate(plain)]
-        return [mask if mask in (0, core) or mask in straight else mask ^ core for mask in plain]
-
-    def order_of(straight=()):
+        return [mask if mask in (0, core) else mask ^ core for mask in plain]
+
+    def order_of():
         order = [0]
         for bits in reversed([[low]] + pairs):
-            order = [mask ^ place for mask in masks(bits, straight) for place in order]
+            order = [mask ^ place for mask in masks(bits) for place in order]
         return order
 
-    straight = (1,) if blocks == 2 else ()
-    order, gather_order = order_of(straight), order_of()
+    order = order_of()
     way_bits = [sum(1 << bit - low - 1 for bit in bits if bit > low) for bits in pairs]
     parities = [
         (sum(bool(chip & bits) for bits in way_bits) + (chip >> high - low - 1).bit_count()) % 2
@@ -350,19 +349,19 @@
     }
     far_pieces = []
 
-    def pack(name, layout, scale=None):
+    def pack(name, layout, scale=None, after=()):
         used = sorted({leaf[0] for pieces in layout for leaf in leaves(pieces)})
         layout = [[renumber(piece, used) for piece in pieces] for pieces in layout]
         out = tuple(array((sum(map(rows_of, pieces)), width), F32) for pieces in layout)
         operands = [arrays[i] for i in used]
         traffic = 8 * width * sum(o.shape[0] for o in out)
-        return kernel(functools.partial(pack_kernel, layout, scale, len(used)), name, out, operands, traffic=traffic)
+        return kernel(functools.partial(pack_kernel, layout, scale, len(used)), name, out, operands, traffic=traffic, after=after)
 
     for bits in pairs + [outer_bits]:
         last = bits is outer_bits
         keeps = len(terms) if last else len(terms) >> len(bits)
         layout, riders = [], []
-        partners = list(enumerate(masks(bits, straight)))[:0:-1]
+        partners = list(enumerate(masks(bits)))[:0:-1]
         if last:
             partners.sort(key=lambda partner: partner[0] != 2)
         for i, mask in partners:
@@ -372,9 +371,6 @@
             going = [q for q in sorted(moving) if not across and q & all_ways == way & all_ways]
             riders.append([(q, come) for q in going for come, _ in moving[q]])
             pieces += [piece for q in going for _, piece in moving[q]]
-            if blocks == 2 and mask == 1:
-                arrays.append(leaving[0])
-                pieces.append((len(arrays) - 1, 0, rows))
             layout.append(pieces)
         sent = pack("pack", layout)
         came = {}
@@ -387,30 +383,27 @@
                 way = mask >> low
                 moving.setdefault(q ^ way, []).append((come ^ way, (number, first, per_peer)))
                 first += per_peer
-            if blocks == 2 and mask == 1:
-                far_pieces.append((number, first, rows))
             for q in {q for q, _ in rides}:
                 del moving[q]
         terms = [[terms[j]] + [came[i][j] for i in sorted(came)] for j in range(keeps)]
-    if blocks > 2:
-        for step in range(1, blocks):
-            arrays.append(shift(leaving[step - 1], step))
-            far_pieces.append((len(arrays) - 1, 0, rows))
-
-    sums = pack("sum", [terms], nodes ** (-0.5))[0].reshape(1, share, width)
+    for step in range(1, blocks):
+        arrays.append(shift(leaving[step - 1], step))
+        far_pieces.append((len(arrays) - 1, 0, rows))
+
+    sums = pack("sum", [terms], nodes ** (-0.5), [arrays[piece[0]] for piece in far_pieces])[0].reshape(1, share, width)
     for bits in reversed(pairs):
         sums = jnp.concatenate([swap(sums, mask) for mask in masks(bits)])
     other = swap(sums, 1 << low)
     if aligned:
         grad_weight = kernel(
-            functools.partial(place_kernel, gather_order),
+            functools.partial(place_kernel, order),
             "place",
             array((width, width), F32),
             (sums, other),
             traffic=8 * width * width,
         )
     else:
-        places = jnp.array([gather_order.index(i) for i in range(chunks)])[chunk_number(chunks) ^ jnp.arange(chunks)]
+        places = jnp.array([order.index(i) for i in range(chunks)])[chunk_number(chunks) ^ jnp.arange(chunks)]
         grad_weight = jnp.concatenate([sums, other])[places].reshape(width, width)
 
     came = moving[0]

time: 47.5 us -> 47.9 us (level)
  starting transfers between devices: 23.8 us -> 25.4 us
  waiting for transfers between devices: 17.7 us -> 16.6 us
    ppermute x1 -> x2, starting transfers between devices: 2.6 us -> 3.85 us  [shift(): return lax.ppermute(value, 'blk', pairs)]
    ppermute x19, waiting for transfers between devices: 17.7 us -> 16.6 us  [swap(): lax.ppermute(value, both, [(i, i ^ mask) for i in range(devices)])]
  transfers between devices with their start and end apart: 20 -> 21, of which waited for: 11 -> 12; matrix products, arithmetic and copies ran while one was open for 0% -> 0% of each run, Pallas kernels for 4% -> 4%
where the time goes in v6:
time: 47.9 us; the launch traced here: 47.8 us
  starting transfers between devices  25.4 us (53%)
  waiting for transfers between devices  16.6 us (35%)
  Pallas kernels  4.95 us (10%)
  between operations  0.74 us (2%)
    ppermute x19, starting transfers between devices, swap(): lax.ppermute(value, both, [(i, i ^ mask) for i in range(devices)])  21.5 us
    ppermute x19, waiting for transfers between devices, swap(): lax.ppermute(value, both, [(i, i ^ mask) for i in range(devices)])  16.6 us
    pallas_call x9, Pallas kernels, kernel(): pl.pallas_call(lambda *refs: body(*refs[:count], *refs[count + len(after)...  4.95 us
    ppermute x2, starting transfers between devices, shift(): return lax.ppermute(value, 'blk', pairs)  3.85 us
  transfers between devices with their start and end apart: 21, of which 12 were waited for; matrix products, arithmetic and copies ran while one was open for 0% of the time, Pallas kernels for 4%

profile of v6, /device:TPU:0, one launch (start us, length us, event | category | flops | bytes accessed | tf_op | source)
XLA Modules:
  0.0 47.8 jit_solution(13673869569944492063)
XLA Ops:
  0.6 1.2 %gather.1 = (f32[8,16,256]{2,1,0:T(8,128)S(1)}, f32[8,16,256]{2,1,0:T(8,128)S(1)}, bf16[128,256]{1,0:T(8,128)(2,1)S(1)}) custom-call(s32[1,16]{1,0:T(1,128)} %refs_0_.3, s32[1,256]{1,0:T(1,128)} %refs_1_.1, f32[128,256]{1,0:T(8,128)} %refs_2_.3), custom_call_target="tpu_custom_call" | custom-call | flops 16777216 | bytes 393216 | tf_op jit(solution)/shard_map/gather/pallas_call | solution.py:216
  2.4 2.6 %collective-permute-start = (f32[128,256]{1,0:T(8,128)S(1)}, f32[128,256]{1,0:T(8,128)S(1)}, u32[]{:S(2)}, u32[]{:S(2)}) collective-permute-start(f32[128,256]{1,0:T(8,128)S(1)} %copy-done), channel_id=1, source_target_pairs={{0,1},{1,0},{2,3},{3,2},{4,5},{5,4},{6,7},{7,6},{8,9},{9,8},{10,11... | collective-permute-start | bytes 393224 | tf_op jit(solution)/shard_map/ppermute | solution.py:240
  5.0 2.4 %collective-permute-start.8 = (f32[2,16,256]{2,1,0:T(8,128)S(1)}, f32[2,16,256]{2,1,0:T(8,128)S(1)}, u32[]{:S(2)}, u32[]{:S(2)}) collective-permute-start(f32[2,16,256]{2,1,0:T(8,128)S(1)} %get-tuple-element.43), channel_id=1, source_target_pairs={{0,18},{1,19},{2,16},{3,17},{4,22},{5,23},{6,20},{7,21},{8,26},{9,... | collective-permute-start | bytes 98312 | tf_op jit(solution)/shard_map/ppermute | solution.py:277
  7.5 2.2 %collective-permute-start.7 = (f32[2,16,256]{2,1,0:T(8,128)S(1)}, f32[2,16,256]{2,1,0:T(8,128)S(1)}, u32[]{:S(2)}, u32[]{:S(2)}) collective-permute-start(f32[2,16,256]{2,1,0:T(8,128)S(1)} %get-tuple-element.44), channel_id=1, source_target_pairs={{0,30},{1,31},{2,28},{3,29},{4,26},{5,27},{6,24},{7,25},{8,22},{9,... | collective-permute-start | bytes 98312 | tf_op jit(solution)/shard_map/ppermute | solution.py:277
  9.7 2.2 %collective-permute-start.6 = (f32[2,16,256]{2,1,0:T(8,128)S(1)}, f32[2,16,256]{2,1,0:T(8,128)S(1)}, u32[]{:S(2)}, u32[]{:S(2)}) collective-permute-start(f32[2,16,256]{2,1,0:T(8,128)S(1)} %get-tuple-element.45), channel_id=1, source_target_pairs={{0,26},{1,27},{2,24},{3,25},{4,30},{5,31},{6,28},{7,29},{8,18},{9,... | collective-permute-start | bytes 98312 | tf_op jit(solution)/shard_map/ppermute | solution.py:277
  11.9 2.5 %collective-permute-start.4 = (f32[2,16,256]{2,1,0:T(8,128)S(1)}, f32[2,16,256]{2,1,0:T(8,128)S(1)}, u32[]{:S(2)}, u32[]{:S(2)}) collective-permute-start(f32[2,16,256]{2,1,0:T(8,128)S(1)} %get-tuple-element.47), channel_id=1, source_target_pairs={{0,14},{1,15},{2,12},{3,13},{4,10},{5,11},{6,8},{7,9},{8,6},{9,7},... | collective-permute-start | bytes 98312 | tf_op jit(solution)/shard_map/ppermute | solution.py:277
  15.4 1.7 %collective-permute-done.5.refs_9_ = f32[2,16,256]{2,1,0:T(8,128)S(1)} collective-permute-done((f32[2,16,256]{2,1,0:T(8,128)S(1)}, f32[2,16,256]{2,1,0:T(8,128)S(1)}, u32[]{:S(2)}, u32[]{:S(2)}) %collective-permute-start.5) | collective-permute-done | bytes 32800 | tf_op jit(solution)/shard_map/ppermute | solution.py:277
  18.0 1.0 %layer.1 = (f32[128,256]{1,0:T(8,128)S(1)}, bf16[2,128,256]{2,1,0:T(8,128)(2,1)S(1)}, f32[256,256]{1,0:T(8,128)S(1)}, f32[256,256]{1,0:T(8,128)S(1)}) custom-call(f32[128,256]{1,0:T(8,128)S(1)} %get-tuple-element.24.refs_0_, bf16[2,128,256]{2,1,0:T(8,128)(2,1)S(1)} %get-tuple-element.25.refs_1_, bf16[2,256,256]{2,1,0:T(8,128)(2,1)S(1)} %get-tuple-element.26.refs_2_, ...), custom_call_target="tpu_custom_call" | custom-call | flops 251658240 | bytes 1048576 | tf_op jit(solution)/shard_map/layer/pallas_call | solution.py:216
  19.4 1.2 %collective-permute-done.9.refs_1_.refs_3_ = f32[256,256]{1,0:T(8,128)S(1)} collective-permute-done((f32[256,256]{1,0:T(8,128)S(1)}, f32[256,256]{1,0:T(8,128)S(1)}, u32[]{:S(2)}, u32[]{:S(2)}) %collective-permute-start.9) | collective-permute-done | bytes 262176 | tf_op jit(solution)/shard_map/ppermute | solution.py:277
  21.2 1.9 %collective-permute-start.11 = (f32[32,256]{1,0:T(8,128)S(1)}, f32[32,256]{1,0:T(8,128)S(1)}, u32[]{:S(2)}, u32[]{:S(2)}) collective-permute-start(f32[32,256]{1,0:T(8,128)S(1)} %get-tuple-element.37), channel_id=1, source_target_pairs={{0,7},{1,6},{2,5},{3,4},{4,3},{5,2},{6,1},{7,0},{8,15},{9,14},{10,... | collective-permute-start | bytes 98312 | tf_op jit(solution)/shard_map/ppermute | solution.py:277
  23.8 0.8 %inner.1 = (f32[128,256]{1,0:T(8,128)S(1)}, f32[1,128,256]{2,1,0:T(8,128)S(1)}, f32[128,256]{1,0:T(8,128)}) custom-call(bf16[2,2,128,128]{3,2,1,0:T(8,128)(2,1)S(1)} %get-tuple-element.23.refs_0_, bf16[2,128,256]{2,1,0:T(8,128)(2,1)S(1)} %get-tuple-element.29.refs_1_, f32[128,256]{1,0:T(8,128)S(1)} %get-tuple-element.30.refs_2_), custom_call_target="tpu_custom_call" | custom-call | flops 50331648 | bytes 786432 | tf_op jit(solution)/shard_map/inner/pallas_call | solution.py:216
  24.6 1.3 %collective-permute-start.16 = (f32[128,256]{1,0:T(8,128)S(1)}, f32[128,256]{1,0:T(8,128)S(1)}, u32[]{:S(2)}, u32[]{:S(2)}) collective-permute-start(f32[128,256]{1,0:T(8,128)S(1)} %bitcast.26), channel_id=1, source_target_pairs={{0,1},{1,0},{2,3},{3,2},{4,5},{5,4},{6,7},{7,6},{8,9},{9,8},{10,11... | collective-permute-start | bytes 393224 | tf_op jit(solution)/shard_map/ppermute | solution.py:240
  25.9 2.4 %collective-permute-done.11.refs_2_ = f32[32,256]{1,0:T(8,128)S(1)} collective-permute-done((f32[32,256]{1,0:T(8,128)S(1)}, f32[32,256]{1,0:T(8,128)S(1)}, u32[]{:S(2)}, u32[]{:S(2)}) %collective-permute-start.11) | collective-permute-done | bytes 32800 | tf_op jit(solution)/shard_map/ppermute | solution.py:277
  28.2 2.9 %collective-permute-start.13 = (f32[96,256]{1,0:T(8,128)S(1)}, f32[96,256]{1,0:T(8,128)S(1)}, u32[]{:S(2)}, u32[]{:S(2)}) collective-permute-start(f32[96,256]{1,0:T(8,128)S(1)} %get-tuple-element.39), channel_id=1, source_target_pairs={{0,18},{1,19},{2,16},{3,17},{4,22},{5,23},{6,20},{7,21},{8,26},{9,... | collective-permute-start | bytes 294920 | tf_op jit(solution)/shard_map/ppermute | solution.py:277
  31.1 1.3 %collective-permute-start.14 = (f32[96,256]{1,0:T(8,128)S(1)}, f32[96,256]{1,0:T(8,128)S(1)}, u32[]{:S(2)}, u32[]{:S(2)}) collective-permute-start(f32[96,256]{1,0:T(8,128)S(1)} %get-tuple-element.40), channel_id=1, source_target_pairs={{0,24},{1,25},{2,26},{3,27},{4,28},{5,29},{6,30},{7,31},{8,16},{9,... | collective-permute-start | bytes 294920 | tf_op jit(solution)/shard_map/ppermute | solution.py:277
  32.4 5.6 %collective-permute-done.13.refs_5_ = f32[96,256]{1,0:T(8,128)S(1)} collective-permute-done((f32[96,256]{1,0:T(8,128)S(1)}, f32[96,256]{1,0:T(8,128)S(1)}, u32[]{:S(2)}, u32[]{:S(2)}) %collective-permute-start.13) | collective-permute-done | bytes 98336 | tf_op jit(solution)/shard_map/ppermute | solution.py:277
  38.5 1.4 %collective-permute-done.15.refs_7_ = f32[96,256]{1,0:T(8,128)S(1)} collective-permute-done((f32[96,256]{1,0:T(8,128)S(1)}, f32[96,256]{1,0:T(8,128)S(1)}, u32[]{:S(2)}, u32[]{:S(2)}) %collective-permute-start.15) | collective-permute-done | bytes 98336 | tf_op jit(solution)/shard_map/ppermute | solution.py:277
  39.9 0.9 %collective-permute-start.19 = (f32[1,32,256]{2,1,0:T(8,128)S(1)}, f32[1,32,256]{2,1,0:T(8,128)S(1)}, u32[]{:S(2)}, u32[]{:S(2)}) collective-permute-start(f32[1,32,256]{2,1,0:T(8,128)S(1)} %bitcast.22), channel_id=1, source_target_pairs={{0,7},{1,6},{2,5},{3,4},{4,3},{5,2},{6,1},{7,0},{8,15},{9,14},{10,... | collective-permute-start | bytes 98312 | tf_op jit(solution)/shard_map/ppermute | solution.py:277
  40.9 1.3 %collective-permute-start.18 = (f32[1,32,256]{2,1,0:T(8,128)S(1)}, f32[1,32,256]{2,1,0:T(8,128)S(1)}, u32[]{:S(2)}, u32[]{:S(2)}) collective-permute-start(f32[1,32,256]{2,1,0:T(8,128)S(1)} %bitcast.23), channel_id=1, source_target_pairs={{0,6},{1,7},{2,4},{3,5},{4,2},{5,3},{6,0},{7,1},{8,14},{9,15},{10,... | collective-permute-start | bytes 98312 | tf_op jit(solution)/shard_map/ppermute | solution.py:277
  42.2 0.8 %collective-permute-start.17 = (f32[1,32,256]{2,1,0:T(8,128)S(1)}, f32[1,32,256]{2,1,0:T(8,128)S(1)}, u32[]{:S(2)}, u32[]{:S(2)}) collective-permute-start(f32[1,32,256]{2,1,0:T(8,128)S(1)} %bitcast.24), channel_id=1, source_target_pairs={{0,3},{1,2},{2,1},{3,0},{4,7},{5,6},{6,5},{7,4},{8,11},{9,10},{10,... | collective-permute-start | bytes 98312 | tf_op jit(solution)/shard_map/ppermute | solution.py:277
  43.0 1.3 %collective-permute-done.19 = f32[1,32,256]{2,1,0:T(8,128)S(1)} collective-permute-done((f32[1,32,256]{2,1,0:T(8,128)S(1)}, f32[1,32,256]{2,1,0:T(8,128)S(1)}, u32[]{:S(2)}, u32[]{:S(2)}) %collective-permute-start.19) | collective-permute-done | bytes 32800 | tf_op jit(solution)/shard_map/ppermute | solution.py:277
  44.5 1.2 %collective-permute-done.17 = f32[1,32,256]{2,1,0:T(8,128)S(1)} collective-permute-done((f32[1,32,256]{2,1,0:T(8,128)S(1)}, f32[1,32,256]{2,1,0:T(8,128)S(1)}, u32[]{:S(2)}, u32[]{:S(2)}) %collective-permute-start.17) | collective-permute-done | bytes 32800 | tf_op jit(solution)/shard_map/ppermute | solution.py:277
  45.8 0.9 %finish.1 = f32[128,256]{1,0:T(8,128)} custom-call(bf16[128,256]{1,0:T(8,128)(2,1)S(1)} %get-tuple-element.32.refs_0_, f32[128,256]{1,0:T(8,128)S(1)} %get-tuple-element.33.refs_1_, f32[256,256]{1,0:T(8,128)S(1)} %get-tuple-element.34.refs_0_.refs_2_, f32[256,256]{1,0:T(8,128)S(1)} %collective-permute-done.9.refs_1_.refs_3_, ...), custom_call_target="tpu_custom_call" | custom-call | flops 33554432 | bytes 655360 | tf_op jit(solution)/shard_map/finish/pallas_call | solution.py:216
  47.0 0.7 %place.1 = f32[256,256]{1,0:T(8,128)} custom-call(f32[4,32,256]{2,1,0:T(8,128)S(1)} %pad_maximum_fusion.refs_0_, f32[4,32,256]{2,1,0:T(8,128)S(1)} %collective-permute-done.20.refs_1_), custom_call_target="tpu_custom_call" | custom-call | bytes 524288 | tf_op jit(solution)/shard_map/place/pallas_call | solution.py:216
  (41 shorter events, 5.1 us)
Async XLA Ops:
  1.9 13.3 %copy-start.1 = (f32[256,256]{1,0:T(8,128)S(1)}, f32[256,256]{1,0:T(8,128)}, u32[]{:S(2)}) copy-start(f32[256,256]{1,0:T(8,128)} %refs_3_.2) | copy-start | bytes 786436
  1.9 3.1 %collective-permute-start.1 = (f32[8,16,256]{2,1,0:T(8,128)S(1)}, f32[8,16,256]{2,1,0:T(8,128)S(1)}, u32[]{:S(2)}, u32[]{:S(2)}) collective-permute-start(f32[8,16,256]{2,1,0:T(8,128)S(1)} %get-tuple-element.28), channel_id=1, source_target_pairs={{0,2},{1,3},{2,0},{3,1},{4,6},{5,7},{6,4},{7,5},{8,10},{9,11},{10,... | collective-permute-start | bytes 393224 | tf_op jit(solution)/shard_map/ppermute | solution.py:277
  2.4 9.5 %collective-permute-start = (f32[128,256]{1,0:T(8,128)S(1)}, f32[128,256]{1,0:T(8,128)S(1)}, u32[]{:S(2)}, u32[]{:S(2)}) collective-permute-start(f32[128,256]{1,0:T(8,128)S(1)} %copy-done), channel_id=1, source_target_pairs={{0,1},{1,0},{2,3},{3,2},{4,5},{5,4},{6,7},{7,6},{8,9},{9,8},{10,11... | collective-permute-start | bytes 393224 | tf_op jit(solution)/shard_map/ppermute | solution.py:240
  5.0 10.1 %copy-start.2 = (f32[128,256]{1,0:T(8,128)S(1)}, f32[128,256]{1,0:T(8,128)}, u32[]{:S(2)}) copy-start(f32[128,256]{1,0:T(8,128)} %refs_2_.2) | copy-start | bytes 393220
  5.0 9.4 %collective-permute-start.8 = (f32[2,16,256]{2,1,0:T(8,128)S(1)}, f32[2,16,256]{2,1,0:T(8,128)S(1)}, u32[]{:S(2)}, u32[]{:S(2)}) collective-permute-start(f32[2,16,256]{2,1,0:T(8,128)S(1)} %get-tuple-element.43), channel_id=1, source_target_pairs={{0,18},{1,19},{2,16},{3,17},{4,22},{5,23},{6,20},{7,21},{8,26},{9,... | collective-permute-start | bytes 98312 | tf_op jit(solution)/shard_map/ppermute | solution.py:277
  7.5 7.0 %collective-permute-start.7 = (f32[2,16,256]{2,1,0:T(8,128)S(1)}, f32[2,16,256]{2,1,0:T(8,128)S(1)}, u32[]{:S(2)}, u32[]{:S(2)}) collective-permute-start(f32[2,16,256]{2,1,0:T(8,128)S(1)} %get-tuple-element.44), channel_id=1, source_target_pairs={{0,30},{1,31},{2,28},{3,29},{4,26},{5,27},{6,24},{7,25},{8,22},{9,... | collective-permute-start | bytes 98312 | tf_op jit(solution)/shard_map/ppermute | solution.py:277
  9.7 5.7 %collective-permute-start.6 = (f32[2,16,256]{2,1,0:T(8,128)S(1)}, f32[2,16,256]{2,1,0:T(8,128)S(1)}, u32[]{:S(2)}, u32[]{:S(2)}) collective-permute-start(f32[2,16,256]{2,1,0:T(8,128)S(1)} %get-tuple-element.45), channel_id=1, source_target_pairs={{0,26},{1,27},{2,24},{3,25},{4,30},{5,31},{6,28},{7,29},{8,18},{9,... | collective-permute-start | bytes 98312 | tf_op jit(solution)/shard_map/ppermute | solution.py:277
  11.9 5.2 %collective-permute-start.5 = (f32[2,16,256]{2,1,0:T(8,128)S(1)}, f32[2,16,256]{2,1,0:T(8,128)S(1)}, u32[]{:S(2)}, u32[]{:S(2)}) collective-permute-start(f32[2,16,256]{2,1,0:T(8,128)S(1)} %get-tuple-element.46), channel_id=1, source_target_pairs={{0,22},{1,23},{2,20},{3,21},{4,18},{5,19},{6,16},{7,17},{8,30},{9,... | collective-permute-start | bytes 98312 | tf_op jit(solution)/shard_map/ppermute | solution.py:277
  11.9 5.2 %collective-permute-start.4 = (f32[2,16,256]{2,1,0:T(8,128)S(1)}, f32[2,16,256]{2,1,0:T(8,128)S(1)}, u32[]{:S(2)}, u32[]{:S(2)}) collective-permute-start(f32[2,16,256]{2,1,0:T(8,128)S(1)} %get-tuple-element.47), channel_id=1, source_target_pairs={{0,14},{1,15},{2,12},{3,13},{4,10},{5,11},{6,8},{7,9},{8,6},{9,7},... | collective-permute-start | bytes 98312 | tf_op jit(solution)/shard_map/ppermute | solution.py:277
  14.5 3.3 %collective-permute-start.3 = (f32[2,16,256]{2,1,0:T(8,128)S(1)}, f32[2,16,256]{2,1,0:T(8,128)S(1)}, u32[]{:S(2)}, u32[]{:S(2)}) collective-permute-start(f32[2,16,256]{2,1,0:T(8,128)S(1)} %get-tuple-element.48), channel_id=1, source_target_pairs={{0,10},{1,11},{2,8},{3,9},{4,14},{5,15},{6,12},{7,13},{8,2},{9,3},... | collective-permute-start | bytes 98312 | tf_op jit(solution)/shard_map/ppermute | solution.py:277
  14.5 3.5 %collective-permute-start.2 = (f32[2,16,256]{2,1,0:T(8,128)S(1)}, f32[2,16,256]{2,1,0:T(8,128)S(1)}, u32[]{:S(2)}, u32[]{:S(2)}) collective-permute-start(f32[2,16,256]{2,1,0:T(8,128)S(1)} %get-tuple-element.49), channel_id=1, source_target_pairs={{0,6},{1,7},{2,4},{3,5},{4,2},{5,3},{6,0},{7,1},{8,14},{9,15},{10,... | collective-permute-start | bytes 98312 | tf_op jit(solution)/shard_map/ppermute | solution.py:277
  15.2 2.8 %copy-start.3 = (f32[128,256]{1,0:T(8,128)S(1)}, f32[128,256]{1,0:T(8,128)}, u32[]{:S(2)}) copy-start(f32[128,256]{1,0:T(8,128)} %refs_3_.3) | copy-start | bytes 393220
  19.0 1.6 %collective-permute-start.9 = (f32[256,256]{1,0:T(8,128)S(1)}, f32[256,256]{1,0:T(8,128)S(1)}, u32[]{:S(2)}, u32[]{:S(2)}) collective-permute-start(f32[256,256]{1,0:T(8,128)S(1)} %get-tuple-element.35), channel_id=1, source_target_pairs={{0,2},{1,3},{2,0},{3,1},{4,6},{5,7},{6,4},{7,5},{8,10},{9,11},{10,... | collective-permute-start | bytes 786440 | tf_op jit(solution)/shard_map/ppermute | solution.py:277
  20.6 7.6 %collective-permute-start.10 = (f32[160,256]{1,0:T(8,128)S(1)}, f32[160,256]{1,0:T(8,128)S(1)}, u32[]{:S(2)}, u32[]{:S(2)}) collective-permute-start(f32[160,256]{1,0:T(8,128)S(1)} %get-tuple-element.36), channel_id=1, source_target_pairs={{0,6},{1,7},{2,4},{3,5},{4,2},{5,3},{6,0},{7,1},{8,14},{9,15},{10,... | collective-permute-start | bytes 491528 | tf_op jit(solution)/shard_map/ppermute | solution.py:277
  21.2 7.0 %collective-permute-start.11 = (f32[32,256]{1,0:T(8,128)S(1)}, f32[32,256]{1,0:T(8,128)S(1)}, u32[]{:S(2)}, u32[]{:S(2)}) collective-permute-start(f32[32,256]{1,0:T(8,128)S(1)} %get-tuple-element.37), channel_id=1, source_target_pairs={{0,7},{1,6},{2,5},{3,4},{4,3},{5,2},{6,1},{7,0},{8,15},{9,14},{10,... | collective-permute-start | bytes 98312 | tf_op jit(solution)/shard_map/ppermute | solution.py:277
  23.1 5.1 %collective-permute-start.12 = (f32[32,256]{1,0:T(8,128)S(1)}, f32[32,256]{1,0:T(8,128)S(1)}, u32[]{:S(2)}, u32[]{:S(2)}) collective-permute-start(f32[32,256]{1,0:T(8,128)S(1)} %get-tuple-element.38), channel_id=1, source_target_pairs={{0,3},{1,2},{2,1},{3,0},{4,7},{5,6},{6,5},{7,4},{8,11},{9,10},{10,... | collective-permute-start | bytes 98312 | tf_op jit(solution)/shard_map/ppermute | solution.py:277
  24.6 7.8 %collective-permute-start.16 = (f32[128,256]{1,0:T(8,128)S(1)}, f32[128,256]{1,0:T(8,128)S(1)}, u32[]{:S(2)}, u32[]{:S(2)}) collective-permute-start(f32[128,256]{1,0:T(8,128)S(1)} %bitcast.26), channel_id=1, source_target_pairs={{0,1},{1,0},{2,3},{3,2},{4,5},{5,4},{6,7},{7,6},{8,9},{9,8},{10,11... | collective-permute-start | bytes 393224 | tf_op jit(solution)/shard_map/ppermute | solution.py:240
  28.2 9.8 %collective-permute-start.13 = (f32[96,256]{1,0:T(8,128)S(1)}, f32[96,256]{1,0:T(8,128)S(1)}, u32[]{:S(2)}, u32[]{:S(2)}) collective-permute-start(f32[96,256]{1,0:T(8,128)S(1)} %get-tuple-element.39), channel_id=1, source_target_pairs={{0,18},{1,19},{2,16},{3,17},{4,22},{5,23},{6,20},{7,21},{8,26},{9,... | collective-permute-start | bytes 294920 | tf_op jit(solution)/shard_map/ppermute | solution.py:277
  31.1 7.4 %collective-permute-start.14 = (f32[96,256]{1,0:T(8,128)S(1)}, f32[96,256]{1,0:T(8,128)S(1)}, u32[]{:S(2)}, u32[]{:S(2)}) collective-permute-start(f32[96,256]{1,0:T(8,128)S(1)} %get-tuple-element.40), channel_id=1, source_target_pairs={{0,24},{1,25},{2,26},{3,27},{4,28},{5,29},{6,30},{7,31},{8,16},{9,... | collective-permute-start | bytes 294920 | tf_op jit(solution)/shard_map/ppermute | solution.py:277
  32.4 7.5 %collective-permute-start.15 = (f32[96,256]{1,0:T(8,128)S(1)}, f32[96,256]{1,0:T(8,128)S(1)}, u32[]{:S(2)}, u32[]{:S(2)}) collective-permute-start(f32[96,256]{1,0:T(8,128)S(1)} %get-tuple-element.41), channel_id=1, source_target_pairs={{0,10},{1,11},{2,8},{3,9},{4,14},{5,15},{6,12},{7,13},{8,2},{9,3},... | collective-permute-start | bytes 294920 | tf_op jit(solution)/shard_map/ppermute | solution.py:277
  39.9 4.3 %collective-permute-start.19 = (f32[1,32,256]{2,1,0:T(8,128)S(1)}, f32[1,32,256]{2,1,0:T(8,128)S(1)}, u32[]{:S(2)}, u32[]{:S(2)}) collective-permute-start(f32[1,32,256]{2,1,0:T(8,128)S(1)} %bitcast.22), channel_id=1, source_target_pairs={{0,7},{1,6},{2,5},{3,4},{4,3},{5,2},{6,1},{7,0},{8,15},{9,14},{10,... | collective-permute-start | bytes 98312 | tf_op jit(solution)/shard_map/ppermute | solution.py:277
  40.9 3.6 %collective-permute-start.18 = (f32[1,32,256]{2,1,0:T(8,128)S(1)}, f32[1,32,256]{2,1,0:T(8,128)S(1)}, u32[]{:S(2)}, u32[]{:S(2)}) collective-permute-start(f32[1,32,256]{2,1,0:T(8,128)S(1)} %bitcast.23), channel_id=1, source_target_pairs={{0,6},{1,7},{2,4},{3,5},{4,2},{5,3},{6,0},{7,1},{8,14},{9,15},{10,... | collective-permute-start | bytes 98312 | tf_op jit(solution)/shard_map/ppermute | solution.py:277
  42.2 3.4 %collective-permute-start.17 = (f32[1,32,256]{2,1,0:T(8,128)S(1)}, f32[1,32,256]{2,1,0:T(8,128)S(1)}, u32[]{:S(2)}, u32[]{:S(2)}) collective-permute-start(f32[1,32,256]{2,1,0:T(8,128)S(1)} %bitcast.24), channel_id=1, source_target_pairs={{0,3},{1,2},{2,1},{3,0},{4,7},{5,6},{6,5},{7,4},{8,11},{9,10},{10,... | collective-permute-start | bytes 98312 | tf_op jit(solution)/shard_map/ppermute | solution.py:277
  45.6 1.4 %collective-permute-start.20 = (f32[4,32,256]{2,1,0:T(8,128)S(1)}, f32[4,32,256]{2,1,0:T(8,128)S(1)}, u32[]{:S(2)}, u32[]{:S(2)}) collective-permute-start(f32[4,32,256]{2,1,0:T(8,128)S(1)} %pad_maximum_fusion.refs_0_), channel_id=1, source_target_pairs={{0,2},{1,3},{2,0},{3,1},{4,6},{5,7},{6,4},{7,5},{8,10},{9,11},{10,... | collective-permute-start | bytes 393224 | tf_op jit(solution)/shard_map/ppermute | solution.py:277
  (3 other events, 3.2 us)

commit v7 on v5

--- a/solution.py
+++ b/solution.py
@@ -302,7 +302,8 @@
     packed = jnp.stack([own, got], axis=1)
     arrived = [swap(packed[mask], 2 * mask + 1 << low) for mask in range(1, groups // 2)]
     arrival = list(range(groups // 2 - 1))
-    arrival.append(arrival.pop(groups // 4 - 1))
+    two, three = groups // 4 - 1, 3 * groups // 8 - 1
+    arrival = [i for i in arrival if i not in (two, three)] + [three, two]
     local, cross, tile_parts, weight_parts = kernel(
         prepare_kernel,
         "prepare",

time: 47.5 us -> 47.5 us (level)
  no operation moved by 1% of the time
where the time goes in v7:
time: 47.5 us; the launch traced here: 47.3 us
  starting transfers between devices  23.8 us (50%)
  waiting for transfers between devices  17.7 us (37%)
  Pallas kernels  4.96 us (10%)
  between operations  0.74 us (2%)
    ppermute x19, starting transfers between devices, swap(): lax.ppermute(value, both, [(i, i ^ mask) for i in range(devices)])  21.2 us
    ppermute x19, waiting for transfers between devices, swap(): lax.ppermute(value, both, [(i, i ^ mask) for i in range(devices)])  17.7 us
    pallas_call x9, Pallas kernels, kernel(): pl.pallas_call(lambda *refs: body(*refs[:count], *refs[count + len(after)...  4.96 us
    ppermute x1, starting transfers between devices, shift(): return lax.ppermute(value, 'blk', pairs)  2.6 us
  transfers between devices with their start and end apart: 20, of which 11 were waited for; matrix products, arithmetic and copies ran while one was open for 0% of the time, Pallas kernels for 4%

profile of v7, /device:TPU:0, one launch (start us, length us, event | category | flops | bytes accessed | tf_op | source)
XLA Modules:
  0.0 47.3 jit_solution(4308381374746461101)
XLA Ops:
  0.6 1.2 %gather.1 = (f32[8,16,256]{2,1,0:T(8,128)S(1)}, f32[8,16,256]{2,1,0:T(8,128)S(1)}, bf16[128,256]{1,0:T(8,128)(2,1)S(1)}) custom-call(s32[1,16]{1,0:T(1,128)} %refs_0_.3, s32[1,256]{1,0:T(1,128)} %refs_1_.1, f32[128,256]{1,0:T(8,128)} %refs_2_.3), custom_call_target="tpu_custom_call" | custom-call | flops 16777216 | bytes 393216 | tf_op jit(solution)/shard_map/gather/pallas_call | solution.py:216
  2.4 2.6 %collective-permute-start = (f32[128,256]{1,0:T(8,128)S(1)}, f32[128,256]{1,0:T(8,128)S(1)}, u32[]{:S(2)}, u32[]{:S(2)}) collective-permute-start(f32[128,256]{1,0:T(8,128)S(1)} %copy-done), channel_id=1, source_target_pairs={{0,1},{1,0},{2,3},{3,2},{4,5},{5,4},{6,7},{7,6},{8,9},{9,8},{10,11... | collective-permute-start | bytes 393224 | tf_op jit(solution)/shard_map/ppermute | solution.py:240
  5.0 2.4 %collective-permute-start.8 = (f32[2,16,256]{2,1,0:T(8,128)S(1)}, f32[2,16,256]{2,1,0:T(8,128)S(1)}, u32[]{:S(2)}, u32[]{:S(2)}) collective-permute-start(f32[2,16,256]{2,1,0:T(8,128)S(1)} %get-tuple-element.43), channel_id=1, source_target_pairs={{0,18},{1,19},{2,16},{3,17},{4,22},{5,23},{6,20},{7,21},{8,26},{9,... | collective-permute-start | bytes 98312 | tf_op jit(solution)/shard_map/ppermute | solution.py:278
  7.5 1.3 %collective-permute-start.7 = (f32[2,16,256]{2,1,0:T(8,128)S(1)}, f32[2,16,256]{2,1,0:T(8,128)S(1)}, u32[]{:S(2)}, u32[]{:S(2)}) collective-permute-start(f32[2,16,256]{2,1,0:T(8,128)S(1)} %get-tuple-element.44), channel_id=1, source_target_pairs={{0,26},{1,27},{2,24},{3,25},{4,30},{5,31},{6,28},{7,29},{8,18},{9,... | collective-permute-start | bytes 98312 | tf_op jit(solution)/shard_map/ppermute | solution.py:278
  8.8 3.2 %collective-permute-start.6 = (f32[2,16,256]{2,1,0:T(8,128)S(1)}, f32[2,16,256]{2,1,0:T(8,128)S(1)}, u32[]{:S(2)}, u32[]{:S(2)}) collective-permute-start(f32[2,16,256]{2,1,0:T(8,128)S(1)} %get-tuple-element.45), channel_id=1, source_target_pairs={{0,30},{1,31},{2,28},{3,29},{4,26},{5,27},{6,24},{7,25},{8,22},{9,... | collective-permute-start | bytes 98312 | tf_op jit(solution)/shard_map/ppermute | solution.py:278
  11.9 2.5 %collective-permute-start.4 = (f32[2,16,256]{2,1,0:T(8,128)S(1)}, f32[2,16,256]{2,1,0:T(8,128)S(1)}, u32[]{:S(2)}, u32[]{:S(2)}) collective-permute-start(f32[2,16,256]{2,1,0:T(8,128)S(1)} %get-tuple-element.47), channel_id=1, source_target_pairs={{0,14},{1,15},{2,12},{3,13},{4,10},{5,11},{6,8},{7,9},{8,6},{9,7},... | collective-permute-start | bytes 98312 | tf_op jit(solution)/shard_map/ppermute | solution.py:278
  14.5 0.6 %collective-permute-start.2 = (f32[2,16,256]{2,1,0:T(8,128)S(1)}, f32[2,16,256]{2,1,0:T(8,128)S(1)}, u32[]{:S(2)}, u32[]{:S(2)}) collective-permute-start(f32[2,16,256]{2,1,0:T(8,128)S(1)} %get-tuple-element.49), channel_id=1, source_target_pairs={{0,6},{1,7},{2,4},{3,5},{4,2},{5,3},{6,0},{7,1},{8,14},{9,15},{10,... | collective-permute-start | bytes 98312 | tf_op jit(solution)/shard_map/ppermute | solution.py:278
  15.4 1.7 %collective-permute-done.5.refs_9_ = f32[2,16,256]{2,1,0:T(8,128)S(1)} collective-permute-done((f32[2,16,256]{2,1,0:T(8,128)S(1)}, f32[2,16,256]{2,1,0:T(8,128)S(1)}, u32[]{:S(2)}, u32[]{:S(2)}) %collective-permute-start.5) | collective-permute-done | bytes 32800 | tf_op jit(solution)/shard_map/ppermute | solution.py:278
  17.2 0.6 %collective-permute-done.3.refs_7_ = f32[2,16,256]{2,1,0:T(8,128)S(1)} collective-permute-done((f32[2,16,256]{2,1,0:T(8,128)S(1)}, f32[2,16,256]{2,1,0:T(8,128)S(1)}, u32[]{:S(2)}, u32[]{:S(2)}) %collective-permute-start.3) | collective-permute-done | bytes 32800 | tf_op jit(solution)/shard_map/ppermute | solution.py:278
  18.0 1.0 %layer.1 = (f32[128,256]{1,0:T(8,128)S(1)}, bf16[2,128,256]{2,1,0:T(8,128)(2,1)S(1)}, f32[256,256]{1,0:T(8,128)S(1)}, f32[256,256]{1,0:T(8,128)S(1)}) custom-call(f32[128,256]{1,0:T(8,128)S(1)} %get-tuple-element.24.refs_0_, bf16[2,128,256]{2,1,0:T(8,128)(2,1)S(1)} %get-tuple-element.25.refs_1_, bf16[2,256,256]{2,1,0:T(8,128)(2,1)S(1)} %get-tuple-element.26.refs_2_, ...), custom_call_target="tpu_custom_call" | custom-call | flops 251658240 | bytes 1048576 | tf_op jit(solution)/shard_map/layer/pallas_call | solution.py:216
  19.4 0.8 %inner.1 = (f32[128,256]{1,0:T(8,128)S(1)}, f32[1,128,256]{2,1,0:T(8,128)S(1)}, f32[128,256]{1,0:T(8,128)}) custom-call(bf16[2,2,128,128]{3,2,1,0:T(8,128)(2,1)S(1)} %get-tuple-element.23.refs_0_, bf16[2,128,256]{2,1,0:T(8,128)(2,1)S(1)} %get-tuple-element.29.refs_1_, f32[128,256]{1,0:T(8,128)S(1)} %get-tuple-element.30.refs_2_), custom_call_target="tpu_custom_call" | custom-call | flops 50331648 | bytes 786432 | tf_op jit(solution)/shard_map/inner/pallas_call | solution.py:216
  21.2 1.3 %collective-permute-start.11 = (f32[160,256]{1,0:T(8,128)S(1)}, f32[160,256]{1,0:T(8,128)S(1)}, u32[]{:S(2)}, u32[]{:S(2)}) collective-permute-start(f32[160,256]{1,0:T(8,128)S(1)} %get-tuple-element.38), channel_id=1, source_target_pairs={{0,1},{1,0},{2,3},{3,2},{4,5},{5,4},{6,7},{7,6},{8,9},{9,8},{10,11... | collective-permute-start | bytes 491528 | tf_op jit(solution)/shard_map/ppermute | solution.py:278
  22.5 1.1 %collective-permute-start.12 = (f32[32,256]{1,0:T(8,128)S(1)}, f32[32,256]{1,0:T(8,128)S(1)}, u32[]{:S(2)}, u32[]{:S(2)}) collective-permute-start(f32[32,256]{1,0:T(8,128)S(1)} %get-tuple-element.39), channel_id=1, source_target_pairs={{0,7},{1,6},{2,5},{3,4},{4,3},{5,2},{6,1},{7,0},{8,15},{9,14},{10,... | collective-permute-start | bytes 98312 | tf_op jit(solution)/shard_map/ppermute | solution.py:278
  23.6 4.6 %collective-permute-done.12.refs_2_ = f32[32,256]{1,0:T(8,128)S(1)} collective-permute-done((f32[32,256]{1,0:T(8,128)S(1)}, f32[32,256]{1,0:T(8,128)S(1)}, u32[]{:S(2)}, u32[]{:S(2)}) %collective-permute-start.12) | collective-permute-done | bytes 32800 | tf_op jit(solution)/shard_map/ppermute | solution.py:278
  28.2 2.8 %collective-permute-start.13 = (f32[96,256]{1,0:T(8,128)S(1)}, f32[96,256]{1,0:T(8,128)S(1)}, u32[]{:S(2)}, u32[]{:S(2)}) collective-permute-start(f32[96,256]{1,0:T(8,128)S(1)} %get-tuple-element.40), channel_id=1, source_target_pairs={{0,18},{1,19},{2,16},{3,17},{4,22},{5,23},{6,20},{7,21},{8,26},{9,... | collective-permute-start | bytes 294920 | tf_op jit(solution)/shard_map/ppermute | solution.py:278
  31.0 1.3 %collective-permute-start.14 = (f32[96,256]{1,0:T(8,128)S(1)}, f32[96,256]{1,0:T(8,128)S(1)}, u32[]{:S(2)}, u32[]{:S(2)}) collective-permute-start(f32[96,256]{1,0:T(8,128)S(1)} %get-tuple-element.41), channel_id=1, source_target_pairs={{0,24},{1,25},{2,26},{3,27},{4,28},{5,29},{6,30},{7,31},{8,16},{9,... | collective-permute-start | bytes 294920 | tf_op jit(solution)/shard_map/ppermute | solution.py:278
  32.3 5.6 %collective-permute-done.13.refs_6_.refs_5_ = f32[96,256]{1,0:T(8,128)S(1)} collective-permute-done((f32[96,256]{1,0:T(8,128)S(1)}, f32[96,256]{1,0:T(8,128)S(1)}, u32[]{:S(2)}, u32[]{:S(2)}) %collective-permute-start.13) | collective-permute-done | bytes 98336 | tf_op jit(solution)/shard_map/ppermute | solution.py:278
  38.4 1.6 %collective-permute-done.15.refs_8_.refs_7_ = f32[96,256]{1,0:T(8,128)S(1)} collective-permute-done((f32[96,256]{1,0:T(8,128)S(1)}, f32[96,256]{1,0:T(8,128)S(1)}, u32[]{:S(2)}, u32[]{:S(2)}) %collective-permute-start.15) | collective-permute-done | bytes 98336 | tf_op jit(solution)/shard_map/ppermute | solution.py:278
  40.0 1.5 %collective-permute-start.18 = (f32[1,32,256]{2,1,0:T(8,128)S(1)}, f32[1,32,256]{2,1,0:T(8,128)S(1)}, u32[]{:S(2)}, u32[]{:S(2)}) collective-permute-start(f32[1,32,256]{2,1,0:T(8,128)S(1)} %bitcast.23), channel_id=1, source_target_pairs={{0,7},{1,6},{2,5},{3,4},{4,3},{5,2},{6,1},{7,0},{8,15},{9,14},{10,... | collective-permute-start | bytes 98312 | tf_op jit(solution)/shard_map/ppermute | solution.py:278
  41.5 1.5 %collective-permute-start.16 = (f32[1,32,256]{2,1,0:T(8,128)S(1)}, f32[1,32,256]{2,1,0:T(8,128)S(1)}, u32[]{:S(2)}, u32[]{:S(2)}) collective-permute-start(f32[1,32,256]{2,1,0:T(8,128)S(1)} %bitcast.25), channel_id=1, source_target_pairs={{0,3},{1,2},{2,1},{3,0},{4,7},{5,6},{6,5},{7,4},{8,11},{9,10},{10,... | collective-permute-start | bytes 98312 | tf_op jit(solution)/shard_map/ppermute | solution.py:278
  43.0 1.4 %collective-permute-done.18 = f32[1,32,256]{2,1,0:T(8,128)S(1)} collective-permute-done((f32[1,32,256]{2,1,0:T(8,128)S(1)}, f32[1,32,256]{2,1,0:T(8,128)S(1)}, u32[]{:S(2)}, u32[]{:S(2)}) %collective-permute-start.18) | collective-permute-done | bytes 32800 | tf_op jit(solution)/shard_map/ppermute | solution.py:278
  44.4 0.8 %collective-permute-done.17 = f32[1,32,256]{2,1,0:T(8,128)S(1)} collective-permute-done((f32[1,32,256]{2,1,0:T(8,128)S(1)}, f32[1,32,256]{2,1,0:T(8,128)S(1)}, u32[]{:S(2)}, u32[]{:S(2)}) %collective-permute-start.17) | collective-permute-done | bytes 32800 | tf_op jit(solution)/shard_map/ppermute | solution.py:278
  45.4 0.9 %finish.1 = f32[128,256]{1,0:T(8,128)} custom-call(bf16[128,256]{1,0:T(8,128)(2,1)S(1)} %get-tuple-element.32.refs_0_, f32[128,256]{1,0:T(8,128)S(1)} %get-tuple-element.33.refs_1_, f32[256,256]{1,0:T(8,128)S(1)} %get-tuple-element.34.refs_0_.refs_2_, f32[256,256]{1,0:T(8,128)S(1)} %collective-permute-done.9.refs_1_.refs_3_, ...), custom_call_target="tpu_custom_call" | custom-call | flops 33554432 | bytes 655360 | tf_op jit(solution)/shard_map/finish/pallas_call | solution.py:216
  46.6 0.7 %place.1 = f32[256,256]{1,0:T(8,128)} custom-call(f32[4,32,256]{2,1,0:T(8,128)S(1)} %pad_maximum_fusion.refs_0_, f32[4,32,256]{2,1,0:T(8,128)S(1)} %collective-permute-done.19.refs_1_), custom_call_target="tpu_custom_call" | custom-call | bytes 524288 | tf_op jit(solution)/shard_map/place/pallas_call | solution.py:216
  (39 shorter events, 3.5 us)
Async XLA Ops:
  0.6 1.8 %copy-start = (f32[128,256]{1,0:T(8,128)S(1)}, f32[128,256]{1,0:T(8,128)}, u32[]{:S(2)}) copy-start(f32[128,256]{1,0:T(8,128)} %refs_2_.3) | copy-start | bytes 393220
  1.9 13.3 %copy-start.1 = (f32[256,256]{1,0:T(8,128)S(1)}, f32[256,256]{1,0:T(8,128)}, u32[]{:S(2)}) copy-start(f32[256,256]{1,0:T(8,128)} %refs_3_.2) | copy-start | bytes 786436
  1.9 3.1 %collective-permute-start.1 = (f32[8,16,256]{2,1,0:T(8,128)S(1)}, f32[8,16,256]{2,1,0:T(8,128)S(1)}, u32[]{:S(2)}, u32[]{:S(2)}) collective-permute-start(f32[8,16,256]{2,1,0:T(8,128)S(1)} %get-tuple-element.28), channel_id=1, source_target_pairs={{0,2},{1,3},{2,0},{3,1},{4,6},{5,7},{6,4},{7,5},{8,10},{9,11},{10,... | collective-permute-start | bytes 393224 | tf_op jit(solution)/shard_map/ppermute | solution.py:278
  2.4 9.5 %collective-permute-start = (f32[128,256]{1,0:T(8,128)S(1)}, f32[128,256]{1,0:T(8,128)S(1)}, u32[]{:S(2)}, u32[]{:S(2)}) collective-permute-start(f32[128,256]{1,0:T(8,128)S(1)} %copy-done), channel_id=1, source_target_pairs={{0,1},{1,0},{2,3},{3,2},{4,5},{5,4},{6,7},{7,6},{8,9},{9,8},{10,11... | collective-permute-start | bytes 393224 | tf_op jit(solution)/shard_map/ppermute | solution.py:240
  5.0 10.1 %copy-start.2 = (f32[128,256]{1,0:T(8,128)S(1)}, f32[128,256]{1,0:T(8,128)}, u32[]{:S(2)}) copy-start(f32[128,256]{1,0:T(8,128)} %refs_2_.2) | copy-start | bytes 393220
  5.0 9.4 %collective-permute-start.8 = (f32[2,16,256]{2,1,0:T(8,128)S(1)}, f32[2,16,256]{2,1,0:T(8,128)S(1)}, u32[]{:S(2)}, u32[]{:S(2)}) collective-permute-start(f32[2,16,256]{2,1,0:T(8,128)S(1)} %get-tuple-element.43), channel_id=1, source_target_pairs={{0,18},{1,19},{2,16},{3,17},{4,22},{5,23},{6,20},{7,21},{8,26},{9,... | collective-permute-start | bytes 98312 | tf_op jit(solution)/shard_map/ppermute | solution.py:278
  7.5 7.0 %collective-permute-start.7 = (f32[2,16,256]{2,1,0:T(8,128)S(1)}, f32[2,16,256]{2,1,0:T(8,128)S(1)}, u32[]{:S(2)}, u32[]{:S(2)}) collective-permute-start(f32[2,16,256]{2,1,0:T(8,128)S(1)} %get-tuple-element.44), channel_id=1, source_target_pairs={{0,26},{1,27},{2,24},{3,25},{4,30},{5,31},{6,28},{7,29},{8,18},{9,... | collective-permute-start | bytes 98312 | tf_op jit(solution)/shard_map/ppermute | solution.py:278
  8.8 6.7 %collective-permute-start.6 = (f32[2,16,256]{2,1,0:T(8,128)S(1)}, f32[2,16,256]{2,1,0:T(8,128)S(1)}, u32[]{:S(2)}, u32[]{:S(2)}) collective-permute-start(f32[2,16,256]{2,1,0:T(8,128)S(1)} %get-tuple-element.45), channel_id=1, source_target_pairs={{0,30},{1,31},{2,28},{3,29},{4,26},{5,27},{6,24},{7,25},{8,22},{9,... | collective-permute-start | bytes 98312 | tf_op jit(solution)/shard_map/ppermute | solution.py:278
  11.9 5.2 %collective-permute-start.5 = (f32[2,16,256]{2,1,0:T(8,128)S(1)}, f32[2,16,256]{2,1,0:T(8,128)S(1)}, u32[]{:S(2)}, u32[]{:S(2)}) collective-permute-start(f32[2,16,256]{2,1,0:T(8,128)S(1)} %get-tuple-element.46), channel_id=1, source_target_pairs={{0,22},{1,23},{2,20},{3,21},{4,18},{5,19},{6,16},{7,17},{8,30},{9,... | collective-permute-start | bytes 98312 | tf_op jit(solution)/shard_map/ppermute | solution.py:278
  11.9 5.2 %collective-permute-start.4 = (f32[2,16,256]{2,1,0:T(8,128)S(1)}, f32[2,16,256]{2,1,0:T(8,128)S(1)}, u32[]{:S(2)}, u32[]{:S(2)}) collective-permute-start(f32[2,16,256]{2,1,0:T(8,128)S(1)} %get-tuple-element.47), channel_id=1, source_target_pairs={{0,14},{1,15},{2,12},{3,13},{4,10},{5,11},{6,8},{7,9},{8,6},{9,7},... | collective-permute-start | bytes 98312 | tf_op jit(solution)/shard_map/ppermute | solution.py:278
  14.5 3.3 %collective-permute-start.3 = (f32[2,16,256]{2,1,0:T(8,128)S(1)}, f32[2,16,256]{2,1,0:T(8,128)S(1)}, u32[]{:S(2)}, u32[]{:S(2)}) collective-permute-start(f32[2,16,256]{2,1,0:T(8,128)S(1)} %get-tuple-element.48), channel_id=1, source_target_pairs={{0,10},{1,11},{2,8},{3,9},{4,14},{5,15},{6,12},{7,13},{8,2},{9,3},... | collective-permute-start | bytes 98312 | tf_op jit(solution)/shard_map/ppermute | solution.py:278
  14.5 3.5 %collective-permute-start.2 = (f32[2,16,256]{2,1,0:T(8,128)S(1)}, f32[2,16,256]{2,1,0:T(8,128)S(1)}, u32[]{:S(2)}, u32[]{:S(2)}) collective-permute-start(f32[2,16,256]{2,1,0:T(8,128)S(1)} %get-tuple-element.49), channel_id=1, source_target_pairs={{0,6},{1,7},{2,4},{3,5},{4,2},{5,3},{6,0},{7,1},{8,14},{9,15},{10,... | collective-permute-start | bytes 98312 | tf_op jit(solution)/shard_map/ppermute | solution.py:278
  15.2 2.8 %copy-start.3 = (f32[128,256]{1,0:T(8,128)S(1)}, f32[128,256]{1,0:T(8,128)}, u32[]{:S(2)}) copy-start(f32[128,256]{1,0:T(8,128)} %refs_3_.3) | copy-start | bytes 393220
  19.0 1.6 %collective-permute-start.9 = (f32[256,256]{1,0:T(8,128)S(1)}, f32[256,256]{1,0:T(8,128)S(1)}, u32[]{:S(2)}, u32[]{:S(2)}) collective-permute-start(f32[256,256]{1,0:T(8,128)S(1)} %get-tuple-element.35), channel_id=1, source_target_pairs={{0,2},{1,3},{2,0},{3,1},{4,6},{5,7},{6,4},{7,5},{8,10},{9,11},{10,... | collective-permute-start | bytes 786440 | tf_op jit(solution)/shard_map/ppermute | solution.py:278
  20.7 7.6 %collective-permute-start.10 = (f32[160,256]{1,0:T(8,128)S(1)}, f32[160,256]{1,0:T(8,128)S(1)}, u32[]{:S(2)}, u32[]{:S(2)}) collective-permute-start(f32[160,256]{1,0:T(8,128)S(1)} %get-tuple-element.37), channel_id=1, source_target_pairs={{0,6},{1,7},{2,4},{3,5},{4,2},{5,3},{6,0},{7,1},{8,14},{9,15},{10,... | collective-permute-start | bytes 491528 | tf_op jit(solution)/shard_map/ppermute | solution.py:278
  21.2 7.0 %collective-permute-start.11 = (f32[160,256]{1,0:T(8,128)S(1)}, f32[160,256]{1,0:T(8,128)S(1)}, u32[]{:S(2)}, u32[]{:S(2)}) collective-permute-start(f32[160,256]{1,0:T(8,128)S(1)} %get-tuple-element.38), channel_id=1, source_target_pairs={{0,1},{1,0},{2,3},{3,2},{4,5},{5,4},{6,7},{7,6},{8,9},{9,8},{10,11... | collective-permute-start | bytes 491528 | tf_op jit(solution)/shard_map/ppermute | solution.py:278
  22.5 5.7 %collective-permute-start.12 = (f32[32,256]{1,0:T(8,128)S(1)}, f32[32,256]{1,0:T(8,128)S(1)}, u32[]{:S(2)}, u32[]{:S(2)}) collective-permute-start(f32[32,256]{1,0:T(8,128)S(1)} %get-tuple-element.39), channel_id=1, source_target_pairs={{0,7},{1,6},{2,5},{3,4},{4,3},{5,2},{6,1},{7,0},{8,15},{9,14},{10,... | collective-permute-start | bytes 98312 | tf_op jit(solution)/shard_map/ppermute | solution.py:278
  28.2 9.7 %collective-permute-start.13 = (f32[96,256]{1,0:T(8,128)S(1)}, f32[96,256]{1,0:T(8,128)S(1)}, u32[]{:S(2)}, u32[]{:S(2)}) collective-permute-start(f32[96,256]{1,0:T(8,128)S(1)} %get-tuple-element.40), channel_id=1, source_target_pairs={{0,18},{1,19},{2,16},{3,17},{4,22},{5,23},{6,20},{7,21},{8,26},{9,... | collective-permute-start | bytes 294920 | tf_op jit(solution)/shard_map/ppermute | solution.py:278
  31.0 7.4 %collective-permute-start.14 = (f32[96,256]{1,0:T(8,128)S(1)}, f32[96,256]{1,0:T(8,128)S(1)}, u32[]{:S(2)}, u32[]{:S(2)}) collective-permute-start(f32[96,256]{1,0:T(8,128)S(1)} %get-tuple-element.41), channel_id=1, source_target_pairs={{0,24},{1,25},{2,26},{3,27},{4,28},{5,29},{6,30},{7,31},{8,16},{9,... | collective-permute-start | bytes 294920 | tf_op jit(solution)/shard_map/ppermute | solution.py:278
  32.3 7.7 %collective-permute-start.15 = (f32[96,256]{1,0:T(8,128)S(1)}, f32[96,256]{1,0:T(8,128)S(1)}, u32[]{:S(2)}, u32[]{:S(2)}) collective-permute-start(f32[96,256]{1,0:T(8,128)S(1)} %get-tuple-element.42), channel_id=1, source_target_pairs={{0,10},{1,11},{2,8},{3,9},{4,14},{5,15},{6,12},{7,13},{8,2},{9,3},... | collective-permute-start | bytes 294920 | tf_op jit(solution)/shard_map/ppermute | solution.py:278
  40.0 4.4 %collective-permute-start.18 = (f32[1,32,256]{2,1,0:T(8,128)S(1)}, f32[1,32,256]{2,1,0:T(8,128)S(1)}, u32[]{:S(2)}, u32[]{:S(2)}) collective-permute-start(f32[1,32,256]{2,1,0:T(8,128)S(1)} %bitcast.23), channel_id=1, source_target_pairs={{0,7},{1,6},{2,5},{3,4},{4,3},{5,2},{6,1},{7,0},{8,15},{9,14},{10,... | collective-permute-start | bytes 98312 | tf_op jit(solution)/shard_map/ppermute | solution.py:278
  41.5 3.7 %collective-permute-start.17 = (f32[1,32,256]{2,1,0:T(8,128)S(1)}, f32[1,32,256]{2,1,0:T(8,128)S(1)}, u32[]{:S(2)}, u32[]{:S(2)}) collective-permute-start(f32[1,32,256]{2,1,0:T(8,128)S(1)} %bitcast.24), channel_id=1, source_target_pairs={{0,6},{1,7},{2,4},{3,5},{4,2},{5,3},{6,0},{7,1},{8,14},{9,15},{10,... | collective-permute-start | bytes 98312 | tf_op jit(solution)/shard_map/ppermute | solution.py:278
  41.5 3.7 %collective-permute-start.16 = (f32[1,32,256]{2,1,0:T(8,128)S(1)}, f32[1,32,256]{2,1,0:T(8,128)S(1)}, u32[]{:S(2)}, u32[]{:S(2)}) collective-permute-start(f32[1,32,256]{2,1,0:T(8,128)S(1)} %bitcast.25), channel_id=1, source_target_pairs={{0,3},{1,2},{2,1},{3,0},{4,7},{5,6},{6,5},{7,4},{8,11},{9,10},{10,... | collective-permute-start | bytes 98312 | tf_op jit(solution)/shard_map/ppermute | solution.py:278
  45.2 1.4 %collective-permute-start.19 = (f32[4,32,256]{2,1,0:T(8,128)S(1)}, f32[4,32,256]{2,1,0:T(8,128)S(1)}, u32[]{:S(2)}, u32[]{:S(2)}) collective-permute-start(f32[4,32,256]{2,1,0:T(8,128)S(1)} %pad_maximum_fusion.refs_0_), channel_id=1, source_target_pairs={{0,2},{1,3},{2,0},{3,1},{4,6},{5,7},{6,4},{7,5},{8,10},{9,11},{10,... | collective-permute-start | bytes 393224 | tf_op jit(solution)/shard_map/ppermute | solution.py:278
  (2 other events, 1.4 us)
